TPU v7x, 32 devices: a whole 2x2x4 slice. The times are simulated.
32 devices in a mesh: section: 4 (over y, x), ctx: 4 (over z), tp: 2 (over core).
Axes of the slice: x: 2, y: 2, z: 4, core: 2. Of those that a mesh axis runs over, the one named last changes fastest.
Arguments:
- section_input: float32 [4, 512, 4096], P('section', 'ctx', 'tp'), may hold values from -60 to 60
- long_filter: bfloat16 [4, 512, 256], P('section', 'ctx', 'tp'), may hold values from -2 to 2
- short_filter: bfloat16 [4, 3, 3, 4096], P('section', None, None, 'tp'), may hold values from -12 to 12
- skip_gain: float32 [4, 4096], P('section', 'tp'), may hold values from -1 to 1
Outputs:
- received: float32 [4, 512, 4096], P('section', 'ctx', 'tp')
All inputs are finite; a program needn't handle non-finite values.
Results may differ from a plain program's by a relative error of at most 0.009.
Values may be sent and summed in bfloat16 or wider, within the bound.
No kernel may reach another device: no remote copies, remote signals or barrier semaphores. Data moves between devices by JAX's collectives and lax.ppermute only.
A program may use at most 64 MiB of HBM per device.

v0:
```python
import jax
import jax.numpy as jnp
from jax import lax
from jax.sharding import PartitionSpec as P

CHAN = 4096
TAPS = 3
BLOCK = 128


TWO_PI = 6.283185307179586


def from_behind(block, axis, distance):
    devices = range(lax.axis_size(axis))
    route = [(i - distance, i) for i in devices if i - distance in devices]
    return lax.ppermute(block, axis, route)


def passed_along(x, axis, by):
    peers = lax.axis_size(axis)
    return lax.ppermute(x, axis, [(i, (i + by) % peers) for i in range(peers)])


def unit_pair(position, period):
    mirror = period - position
    folded = jnp.minimum(position, mirror)
    angle_value = folded.astype(jnp.float32) * (TWO_PI / period)
    cosine = jnp.where(4 * folded == period, 0.0, jnp.cos(angle_value))
    sine_part = jnp.where((folded == 0) | (2 * folded == period), 0.0, jnp.sin(angle_value))
    sine_part = jnp.where(position > mirror, -sine_part, sine_part)
    return (cosine, -sine_part)


def first_section(table_re, table_im, data):
    real_out = jnp.einsum("ka,abc->kbc", table_re, data, preferred_element_type=jnp.float32)
    imag_out = jnp.einsum("ka,abc->kbc", table_im, data, preferred_element_type=jnp.float32)
    return (real_out.astype(jnp.bfloat16), imag_out.astype(jnp.bfloat16))


def rotate(turn_re, turn_im, data_re, data_im):
    plain_re = data_re.astype(jnp.float32)
    plain_im = data_im.astype(jnp.float32)
    real_out = turn_re[:, :, None] * plain_re - turn_im[:, :, None] * plain_im
    imag_out = turn_re[:, :, None] * plain_im + turn_im[:, :, None] * plain_re
    return (real_out.astype(jnp.bfloat16), imag_out.astype(jnp.bfloat16))


def mix_rows(form, table_re, table_im, data_re, data_im):

    def product_of(left, right):
        return jnp.einsum(form, left, right, preferred_element_type=jnp.float32)

    real_out = product_of(table_re, data_re) - product_of(table_im, data_im)
    imag_out = product_of(table_re, data_im) + product_of(table_im, data_re)
    return (real_out, imag_out)


def apply_filter(spec_re, spec_im, filt_re, filt_im):
    rows_count, inner_width, channels = spec_re.shape
    filters = filt_re.shape[2]
    grouped_shape = (rows_count, inner_width, filters, channels // filters)
    grouped_re = spec_re.reshape(grouped_shape)
    grouped_im = spec_im.reshape(grouped_shape)
    gain_re = filt_re[..., None]
    gain_im = filt_im[..., None]
    out_re = (grouped_re * gain_re - grouped_im * gain_im).reshape(spec_re.shape)
    out_im = (grouped_re * gain_im + grouped_im * gain_re).reshape(spec_re.shape)
    return (out_re.astype(jnp.bfloat16), out_im.astype(jnp.bfloat16))


def spectral_middle(parts, local_freq, inner_re, inner_im, freq_total):
    sig_re, sig_im, kern_re, kern_im = parts
    inner_ids = jnp.arange(BLOCK, dtype=jnp.int32)
    turn_re, turn_im = unit_pair(local_freq[:, None] * inner_ids[None, :] % freq_total, freq_total)
    turned_re, turned_im = rotate(turn_re, turn_im, sig_re, sig_im)
    kturn_re, kturn_im = rotate(turn_re, turn_im, kern_re, kern_im)
    spec_re, spec_im = mix_rows("qb,rbc->rqc", inner_re, inner_im, turned_re, turned_im)
    filt_re, filt_im = mix_rows("qb,rbc->rqc", inner_re, inner_im, kturn_re, kturn_im)
    weight_re, weight_im = apply_filter(spec_re, spec_im, filt_re, filt_im)
    back_re, back_im = mix_rows("bq,rqc->rbc", inner_re, -inner_im, weight_re, weight_im)
    return rotate(turn_re, -turn_im, back_re, back_im)


def block_columns(signal, kernel):
    return (
        lax.all_to_all(signal, "ctx", split_axis=1, concat_axis=0, tiled=True),
        lax.all_to_all(kernel, "ctx", split_axis=1, concat_axis=0, tiled=True),
    )


def token_rows(conv_vals):
    return lax.all_to_all(conv_vals, "ctx", split_axis=0, concat_axis=1, tiled=True)


def local(section_input, long_filter, short_filter, skip_gain):
    acts_local = section_input[0]
    tok_rows, chan_local = acts_local.shape
    filt_local = long_filter.shape[2]
    n_ctx = lax.axis_size("ctx")
    ctx_rank = lax.axis_index("ctx")
    blocks_local = tok_rows // BLOCK
    half_span = blocks_local * n_ctx
    full_span = 2 * half_span
    freq_total = full_span * BLOCK
    rows_local = full_span // n_ctx
    partial_squares = jnp.sum(acts_local * acts_local, axis=1)
    total_squares = lax.psum(partial_squares, "tp")
    normed = (acts_local * lax.rsqrt(total_squares / CHAN + 1e-06)[:, None]).astype(jnp.bfloat16)
    earlier = from_behind(normed[tok_rows - (TAPS - 1) :], "ctx", 1)
    extended = jnp.concatenate([earlier, normed], axis=0)
    taps_all = short_filter[0].astype(jnp.float32)
    featured = []
    for feature_id in range(3):
        running = jnp.zeros((tok_rows, chan_local), jnp.float32)
        for offset in range(TAPS):
            begin_row = TAPS - 1 - offset
            running = (
                running
                + taps_all[feature_id, offset][None, :] * extended[begin_row : begin_row + tok_rows]
            )
        featured.append(running)
    query = featured[0].astype(jnp.bfloat16)
    product = (featured[1] * featured[2]).astype(jnp.bfloat16)
    block_ids = jnp.arange(half_span, dtype=jnp.int32)
    inner_ids = jnp.arange(BLOCK, dtype=jnp.int32)
    inner_re, inner_im = unit_pair(inner_ids[:, None] * inner_ids[None, :] % BLOCK, BLOCK)
    inner_re = inner_re.astype(jnp.bfloat16)
    inner_im = inner_im.astype(jnp.bfloat16)
    signal = product.reshape(blocks_local, BLOCK, chan_local)
    kernel = long_filter[0].reshape(blocks_local, BLOCK, filt_local)
    signal_cols, kernel_cols = block_columns(signal, kernel)
    freq_rows = jnp.arange(full_span, dtype=jnp.int32)
    outer_re, outer_im = unit_pair(freq_rows[:, None] * block_ids[None, :] % full_span, full_span)
    table_re = outer_re.astype(jnp.bfloat16)
    table_im = outer_im.astype(jnp.bfloat16)
    sig_re, sig_im = first_section(table_re, table_im, signal_cols)
    kern_re, kern_im = first_section(table_re, table_im, kernel_cols)
    got = (
        lax.all_to_all(sig_re, "ctx", split_axis=0, concat_axis=1, tiled=True),
        lax.all_to_all(sig_im, "ctx", split_axis=0, concat_axis=1, tiled=True),
        lax.all_to_all(kern_re, "ctx", split_axis=0, concat_axis=1, tiled=True),
        lax.all_to_all(kern_im, "ctx", split_axis=0, concat_axis=1, tiled=True),
    )
    local_freq = ctx_rank * rows_local + jnp.arange(rows_local, dtype=jnp.int32)
    back_re, back_im = spectral_middle(got, local_freq, inner_re, inner_im, freq_total)
    gathered_re, gathered_im = (
        lax.all_to_all(back_re, "ctx", split_axis=1, concat_axis=0, tiled=True),
        lax.all_to_all(back_im, "ctx", split_axis=1, concat_axis=0, tiled=True),
    )
    conv_vals = jnp.einsum("ka,kbc->abc", table_re, gathered_re, preferred_element_type=jnp.float32)
    conv_vals = conv_vals + jnp.einsum(
        "ka,kbc->abc", table_im, gathered_im, preferred_element_type=jnp.float32
    )
    conv_vals = (conv_vals * (1.0 / freq_total)).astype(jnp.bfloat16)
    conv_tokens = token_rows(conv_vals).reshape(tok_rows, chan_local)
    finished = acts_local + query.astype(jnp.float32) * (
        conv_tokens.astype(jnp.float32) + skip_gain[0][None, :] * product.astype(jnp.float32)
    )
    received = passed_along(finished.astype(jnp.bfloat16), "section", 1).astype(finished.dtype)
    return received[None]


def solution(mesh):
    in_specs = (
        P("section", "ctx", "tp"),
        P("section", "ctx", "tp"),
        P("section", None, None, "tp"),
        P("section", "tp"),
    )
    out_specs = P("section", "ctx", "tp")
    return jax.shard_map(local, mesh=mesh, in_specs=in_specs, out_specs=out_specs, check_vma=False)
```

profile of v0, /device:TPU:0, one launch (start us, length us, event | category | flops | bytes accessed | tf_op | source)
XLA Modules:
  0.0 223.0 jit_solution(12301455431627811711)
XLA Ops:
  0.0 0.9 copy.107
  0.9 0.5 broadcast.264
  1.4 0.8 reduce.1
  2.2 0.6 reshape.162
  2.9 6.3 %all-to-all-start.3 = ((bf16[4,2,2048]{2,1,0:T(2,128)(2,1)}), bf16[4,2,2048]{2,1,0:T(2,128)(2,1)S(1)}, u32[]{:S(2)}, u32[]{:S(2)}) async-start(bf16[4,2,2048]{2,1,0:T(2,128)(2,1)} %reshape.162), calls=%async_computation.3 | async-start | bytes 65536 | tf_op jit(solution)/shard_map/all_to_all | solution.py:88
  9.2 1.4 fusion.28
  10.6 2.5 %psum.7 = f32[128]{0:T(128)S(1)} all-reduce(f32[128]{0:T(128)S(1)} %fusion.28), channel_id=1, replica_groups=mesh['section'=4,'ctx'=4,'tp'=2] {'tp'}, use_global_device_ids=true, to_apply=%region_1.0 | all-reduce | flops 128 | bytes 1024 | tf_op jit(solution)/shard_map/psum | solution.py:108
  13.2 3.9 %collective-permute-start = (bf16[2,2048]{1,0:T(2,128)(2,1)S(1)}, bf16[2,2048]{1,0:T(2,128)(2,1)S(1)}, u32[]{:S(2)}, u32[]{:S(2)}) collective-permute-start(bf16[2,2048]{1,0:T(2,128)(2,1)S(1)} %slice.54), channel_id=1, source_target_pairs={{0,2},{2,4},{4,6},{1,3},{3,5},{5,7},{8,10},{10,12},{12,14},{9,11},... | collective-permute-start | bytes 24584 | tf_op jit(solution)/shard_map/ppermute | solution.py:17
  17.2 1.3 collective-permute-done
  18.5 0.6 fusion.195
  19.1 0.8 copy.106
  19.9 3.7 %reduce = bf16[128,2048]{1,0:T(8,128)(2,1)S(1)} reduce(bf16[128,1,2048]{2,1,0:T(2,128)(2,1)S(1)} %bitcast.194, bf16[]{:T(256)} %broadcast.264), dimensions={1}, to_apply=%bitcast.188.reduce_sub_computation | reduce | bytes 1048578
  23.6 1.2 reshape.160
  24.8 5.4 %all-to-all-start = ((bf16[4,2,32768]{2,1,0:T(2,128)(2,1)}), bf16[4,2,32768]{2,1,0:T(2,128)(2,1)S(1)}, u32[]{:S(2)}, u32[]{:S(2)}) async-start(bf16[4,2,32768]{2,1,0:T(2,128)(2,1)} %reshape.160), calls=%async_computation | async-start | bytes 1048576 | tf_op jit(solution)/shard_map/all_to_all | solution.py:87
  30.4 0.6 copy.71
  31.1 12.7 %all-to-all-done = bf16[4,2,32768]{2,1,0:T(2,128)(2,1)S(1)} async-done(((bf16[4,2,32768]{2,1,0:T(2,128)(2,1)}), bf16[4,2,32768]{2,1,0:T(2,128)(2,1)S(1)}, u32[]{:S(2)}, u32[]{:S(2)}) %all-to-all-start) | async-done | bytes 524320 | tf_op jit(solution)/shard_map/all_to_all | solution.py:87
  43.8 3.3 %all-to-all-start.5 = ((bf16[8,32,128]{2,1,0:T(8,128)(2,1)}), bf16[8,32,128]{2,1,0:T(8,128)(2,1)S(1)}, u32[]{:S(2)}, u32[]{:S(2)}) async-start(bf16[8,32,128]{2,1,0:T(8,128)(2,1)} %copy.71), calls=%async_computation.5 | async-start | bytes 131072 | tf_op jit(solution)/shard_map/all_to_all | solution.py:143
  47.3 0.6 copy.68
  48.0 0.5 reshape.161
  48.5 0.3 copy.94
  48.8 4.0 %all-to-all-done.5 = bf16[8,32,128]{2,1,0:T(8,128)(2,1)S(1)} async-done(((bf16[8,32,128]{2,1,0:T(8,128)(2,1)}), bf16[8,32,128]{2,1,0:T(8,128)(2,1)S(1)}, u32[]{:S(2)}, u32[]{:S(2)}) %all-to-all-start.5) | async-done | bytes 65568 | tf_op jit(solution)/shard_map/all_to_all | solution.py:143
  52.8 3.3 %all-to-all-start.4 = ((bf16[8,32,128]{2,1,0:T(8,128)(2,1)}), bf16[8,32,128]{2,1,0:T(8,128)(2,1)S(1)}, u32[]{:S(2)}, u32[]{:S(2)}) async-start(bf16[8,32,128]{2,1,0:T(8,128)(2,1)} %copy.68), calls=%async_computation.4 | async-start | bytes 131072 | tf_op jit(solution)/shard_map/all_to_all | solution.py:142
  56.1 0.6 convolution_convert_fusion.1
  56.7 1.6 copy.59
  58.3 3.5 %all-to-all-done.4 = bf16[8,32,128]{2,1,0:T(8,128)(2,1)S(1)} async-done(((bf16[8,32,128]{2,1,0:T(8,128)(2,1)}), bf16[8,32,128]{2,1,0:T(8,128)(2,1)S(1)}, u32[]{:S(2)}, u32[]{:S(2)}) %all-to-all-start.4) | async-done | bytes 65568 | tf_op jit(solution)/shard_map/all_to_all | solution.py:142
  61.8 3.5 %all-to-all-start.1 = ((bf16[8,32,2048]{2,1,0:T(8,128)(2,1)}), bf16[8,32,2048]{2,1,0:T(8,128)(2,1)S(1)}, u32[]{:S(2)}, u32[]{:S(2)}) async-start(bf16[8,32,2048]{2,1,0:T(8,128)(2,1)} %copy.59), calls=%async_computation.1 | async-start | bytes 2097152 | tf_op jit(solution)/shard_map/all_to_all | solution.py:140
  65.5 0.6 convolution_convert_fusion
  66.2 1.5 copy.62
  67.7 20.5 %all-to-all-done.1 = bf16[8,32,2048]{2,1,0:T(8,128)(2,1)S(1)} async-done(((bf16[8,32,2048]{2,1,0:T(8,128)(2,1)}), bf16[8,32,2048]{2,1,0:T(8,128)(2,1)S(1)}, u32[]{:S(2)}, u32[]{:S(2)}) %all-to-all-start.1) | async-done | bytes 1048608 | tf_op jit(solution)/shard_map/all_to_all | solution.py:140
  88.2 4.4 %all-to-all-start.2 = ((bf16[8,32,2048]{2,1,0:T(8,128)(2,1)}), bf16[8,32,2048]{2,1,0:T(8,128)(2,1)}, u32[]{:S(2)}, u32[]{:S(2)}) async-start(bf16[8,32,2048]{2,1,0:T(8,128)(2,1)} %copy.62), calls=%async_computation.2 | async-start | bytes 2097152 | tf_op jit(solution)/shard_map/all_to_all | solution.py:141
  92.8 0.4 fusion.58
  93.2 0.4 fusion.54
  93.6 0.4 fusion.13
  94.0 0.4 fusion.12
  95.0 22.4 %all-to-all-done.2 = bf16[8,32,2048]{2,1,0:T(8,128)(2,1)} async-done(((bf16[8,32,2048]{2,1,0:T(8,128)(2,1)}), bf16[8,32,2048]{2,1,0:T(8,128)(2,1)}, u32[]{:S(2)}, u32[]{:S(2)}) %all-to-all-start.2) | async-done | bytes 1048608 | tf_op jit(solution)/shard_map/all_to_all | solution.py:141
  117.3 1.5 convert_bitcast_fusion
  118.9 0.9 fusion.9
  119.9 0.7 fusion.60
  120.6 0.7 fusion.56
  121.3 0.7 fusion
  122.0 1.3 fusion.5
  123.3 0.7 fusion.52
  124.0 0.7 fusion.50
  124.7 0.7 convolution_add_fusion
  125.4 1.2 fusion.24
  126.5 2.1 copy.82
  128.6 3.5 %all-to-all-start.7 = ((bf16[2,128,2048]{2,0,1:T(2,128)(2,1)}), bf16[2,128,2048]{2,0,1:T(2,128)(2,1)S(1)}, u32[]{:S(2)}, u32[]{:S(2)}) async-start(bf16[2,128,2048]{2,0,1:T(2,128)(2,1)} %copy.82), calls=%async_computation.7 | async-start | bytes 2097152 | tf_op jit(solution)/shard_map/all_to_all | solution.py:149
  132.1 2.0 copy.79
  134.1 23.2 %all-to-all-done.7 = bf16[2,128,2048]{2,0,1:T(2,128)(2,1)S(1)} async-done(((bf16[2,128,2048]{2,0,1:T(2,128)(2,1)}), bf16[2,128,2048]{2,0,1:T(2,128)(2,1)S(1)}, u32[]{:S(2)}, u32[]{:S(2)}) %all-to-all-start.7) | async-done | bytes 1048608 | tf_op jit(solution)/shard_map/all_to_all | solution.py:149
  157.3 3.7 %all-to-all-start.6 = ((bf16[2,128,2048]{2,0,1:T(2,128)(2,1)}), bf16[2,128,2048]{2,0,1:T(2,128)(2,1)S(1)}, u32[]{:S(2)}, u32[]{:S(2)}) async-start(bf16[2,128,2048]{2,0,1:T(2,128)(2,1)} %copy.79), calls=%async_computation.6 | async-start | bytes 2097152 | tf_op jit(solution)/shard_map/all_to_all | solution.py:148
  161.1 0.4 copy.83
  161.4 2.1 copy.84
  163.5 1.5 all_to_all.94
  165.0 21.1 %all-to-all-done.6 = bf16[2,128,2048]{2,0,1:T(2,128)(2,1)S(1)} async-done(((bf16[2,128,2048]{2,0,1:T(2,128)(2,1)}), bf16[2,128,2048]{2,0,1:T(2,128)(2,1)S(1)}, u32[]{:S(2)}, u32[]{:S(2)}) %all-to-all-start.6) | async-done | bytes 1048608 | tf_op jit(solution)/shard_map/all_to_all | solution.py:148
  186.0 0.3 copy.80
  186.4 1.1 copy.81
  187.5 1.2 all_to_all.90
  188.7 1.7 fusion.79
  190.4 0.5 fusion.3
  191.2 16.4 %all_to_all.105 = bf16[4,32,2048]{2,1,0:T(8,128)(2,1)S(1)} all-to-all(bf16[4,32,2048]{2,1,0:T(8,128)(2,1)S(1)} %copy.85), channel_id=1, replica_groups=mesh['section'=4,'ctx'=4,'tp'=2] {'ctx'}, dimensions={0} | all-to-all | bytes 1048576 | tf_op jit(solution)/shard_map/all_to_all | solution.py:93
  207.6 1.0 fusion.27
  208.6 1.5 collective-permute-start.1
  210.1 11.9 %collective-permute-done.1 = bf16[128,2048]{1,0:T(8,128)(2,1)S(1)} collective-permute-done((bf16[128,2048]{1,0:T(8,128)(2,1)S(1)}, bf16[128,2048]{1,0:T(8,128)(2,1)S(1)}, u32[]{:S(2)}, u32[]{:S(2)}) %collective-permute-start.1) | collective-permute-done | bytes 524320 | tf_op jit(solution)/shard_map/ppermute | solution.py:22
  222.0 1.1 bitcast_convert_fusion
  (31 shorter events, 2.0 us)
Async XLA Ops:
  0.0 13.0 %copy-start = (f32[1,128,2048]{2,1,0:T(8,128)S(1)}, f32[1,128,2048]{2,1,0:T(8,128)}, u32[]{:S(2)}) copy-start(f32[1,128,2048]{2,1,0:T(8,128)} %param.4) | copy-start | bytes 3145732
  0.0 17.1 %copy-start.3 = (bf16[1,3,3,2048]{3,2,1,0:T(4,128)(2,1)S(1)}, bf16[1,3,3,2048]{3,2,1,0:T(4,128)(2,1)}, u32[]{:S(2)}) copy-start(bf16[1,3,3,2048]{3,2,1,0:T(4,128)(2,1)} %param.6) | copy-start | bytes 110596
  2.9 21.9 %all-to-all-start.3 = ((bf16[4,2,2048]{2,1,0:T(2,128)(2,1)}), bf16[4,2,2048]{2,1,0:T(2,128)(2,1)S(1)}, u32[]{:S(2)}, u32[]{:S(2)}) async-start(bf16[4,2,2048]{2,1,0:T(2,128)(2,1)} %reshape.162), calls=%async_computation.3 | async-start | bytes 65536 | tf_op jit(solution)/shard_map/all_to_all | solution.py:88
  13.2 5.3 %copy-start.1 = (bf16[128,2048]{1,0:T(8,128)(2,1)}, bf16[128,2048]{1,0:T(8,128)(2,1)S(1)}, u32[]{:S(2)}) copy-start(bf16[128,2048]{1,0:T(8,128)(2,1)S(1)} %fusion.29) | copy-start | bytes 1572868
  13.2 5.3 %collective-permute-start = (bf16[2,2048]{1,0:T(2,128)(2,1)S(1)}, bf16[2,2048]{1,0:T(2,128)(2,1)S(1)}, u32[]{:S(2)}, u32[]{:S(2)}) collective-permute-start(bf16[2,2048]{1,0:T(2,128)(2,1)S(1)} %slice.54), channel_id=1, source_target_pairs={{0,2},{2,4},{4,6},{1,3},{3,5},{5,7},{8,10},{10,12},{12,14},{9,11},... | collective-permute-start | bytes 24584 | tf_op jit(solution)/shard_map/ppermute | solution.py:17
  24.8 19.0 %all-to-all-start = ((bf16[4,2,32768]{2,1,0:T(2,128)(2,1)}), bf16[4,2,32768]{2,1,0:T(2,128)(2,1)S(1)}, u32[]{:S(2)}, u32[]{:S(2)}) async-start(bf16[4,2,32768]{2,1,0:T(2,128)(2,1)} %reshape.160), calls=%async_computation | async-start | bytes 1048576 | tf_op jit(solution)/shard_map/all_to_all | solution.py:87
  43.8 9.0 %all-to-all-start.5 = ((bf16[8,32,128]{2,1,0:T(8,128)(2,1)}), bf16[8,32,128]{2,1,0:T(8,128)(2,1)S(1)}, u32[]{:S(2)}, u32[]{:S(2)}) async-start(bf16[8,32,128]{2,1,0:T(8,128)(2,1)} %copy.71), calls=%async_computation.5 | async-start | bytes 131072 | tf_op jit(solution)/shard_map/all_to_all | solution.py:143
  52.8 9.0 %all-to-all-start.4 = ((bf16[8,32,128]{2,1,0:T(8,128)(2,1)}), bf16[8,32,128]{2,1,0:T(8,128)(2,1)S(1)}, u32[]{:S(2)}, u32[]{:S(2)}) async-start(bf16[8,32,128]{2,1,0:T(8,128)(2,1)} %copy.68), calls=%async_computation.4 | async-start | bytes 131072 | tf_op jit(solution)/shard_map/all_to_all | solution.py:142
  61.8 26.4 %all-to-all-start.1 = ((bf16[8,32,2048]{2,1,0:T(8,128)(2,1)}), bf16[8,32,2048]{2,1,0:T(8,128)(2,1)S(1)}, u32[]{:S(2)}, u32[]{:S(2)}) async-start(bf16[8,32,2048]{2,1,0:T(8,128)(2,1)} %copy.59), calls=%async_computation.1 | async-start | bytes 2097152 | tf_op jit(solution)/shard_map/all_to_all | solution.py:140
  88.2 29.1 %all-to-all-start.2 = ((bf16[8,32,2048]{2,1,0:T(8,128)(2,1)}), bf16[8,32,2048]{2,1,0:T(8,128)(2,1)}, u32[]{:S(2)}, u32[]{:S(2)}) async-start(bf16[8,32,2048]{2,1,0:T(8,128)(2,1)} %copy.62), calls=%async_computation.2 | async-start | bytes 2097152 | tf_op jit(solution)/shard_map/all_to_all | solution.py:141
  128.6 28.7 %all-to-all-start.7 = ((bf16[2,128,2048]{2,0,1:T(2,128)(2,1)}), bf16[2,128,2048]{2,0,1:T(2,128)(2,1)S(1)}, u32[]{:S(2)}, u32[]{:S(2)}) async-start(bf16[2,128,2048]{2,0,1:T(2,128)(2,1)} %copy.82), calls=%async_computation.7 | async-start | bytes 2097152 | tf_op jit(solution)/shard_map/all_to_all | solution.py:149
  157.3 28.7 %all-to-all-start.6 = ((bf16[2,128,2048]{2,0,1:T(2,128)(2,1)}), bf16[2,128,2048]{2,0,1:T(2,128)(2,1)S(1)}, u32[]{:S(2)}, u32[]{:S(2)}) async-start(bf16[2,128,2048]{2,0,1:T(2,128)(2,1)} %copy.79), calls=%async_computation.6 | async-start | bytes 2097152 | tf_op jit(solution)/shard_map/all_to_all | solution.py:148
  190.4 17.2 %copy-start.2 = (bf16[128,2048]{1,0:T(8,128)(2,1)S(1)}, bf16[128,2048]{1,0:T(8,128)(2,1)}, u32[]{:S(2)}) copy-start(bf16[128,2048]{1,0:T(8,128)(2,1)} %copy-done.1) | copy-start | bytes 1572868
  190.4 17.2 %copy-start.4 = (f32[1,2048]{1,0:T(1,128)S(1)}, f32[1,2048]{1,0:T(1,128)}, u32[]{:S(2)}) copy-start(f32[1,2048]{1,0:T(1,128)} %param.7) | copy-start | bytes 24580
  208.6 13.4 %collective-permute-start.1 = (bf16[128,2048]{1,0:T(8,128)(2,1)S(1)}, bf16[128,2048]{1,0:T(8,128)(2,1)S(1)}, u32[]{:S(2)}, u32[]{:S(2)}) collective-permute-start(bf16[128,2048]{1,0:T(8,128)(2,1)S(1)} %fusion.27), channel_id=1, source_target_pairs={{0,8},{8,16},{16,24},{24,0},{1,9},{9,17},{17,25},{25,1},{2,10},{10... | collective-permute-start | bytes 1572872 | tf_op jit(solution)/shard_map/ppermute | solution.py:22
where the time goes:
time: 224 us; the launch traced here: 223 us
  waiting for transfers between devices  120 us (54%)
  starting transfers between devices  38.9 us (17%)
  local copies, waits for them, and re-layouts  20.7 us (9%)
  blocking collectives  18.8 us (8%)
  matrix products  12.2 us (5%)
  other arithmetic  11.6 us (5%)
    all_to_all x1, waiting for transfers between devices, local(): lax.all_to_all(back_im, 'ctx', split_axis=1, concat_axis=0, tiled=True)  23.2 us
    all_to_all x1, waiting for transfers between devices, local(): lax.all_to_all(sig_im, 'ctx', split_axis=0, concat_axis=1, tiled=True)  22.4 us
    all_to_all x1, waiting for transfers between devices, local(): lax.all_to_all(back_re, 'ctx', split_axis=1, concat_axis=0, tiled=True)  21.1 us
    all_to_all x1, waiting for transfers between devices, local(): lax.all_to_all(sig_re, 'ctx', split_axis=0, concat_axis=1, tiled=True)  20.5 us
    all_to_all x1, blocking collectives, token_rows(): lax.all_to_all(conv_vals, 'ctx', split_axis=0, concat_axis=1, tiled=True)  16.4 us
    all_to_all x1, waiting for transfers between devices, block_columns(): lax.all_to_all(signal, 'ctx', split_axis=1, concat_axis=0, tiled=True)  12.7 us
    ppermute x1, waiting for transfers between devices, passed_along(): return lax.ppermute(x, axis, [(i, (i + by) % peers) for i in range(peers)])  11.9 us
    dot_general x12, matrix products, product_of(): return jnp.einsum(form, left, right, preferred_element_type=jnp.float32)  8.31 us
  transfers between devices with their start and end apart: 10, of which 9 were waited for; matrix products, arithmetic and copies ran while one was open for 10% of the time, Pallas kernels for 0%

commit v1 on v0

--- a/solution.py
+++ b/solution.py
@@ -1,6 +1,12 @@
+import functools
+
 import jax
 import jax.numpy as jnp
+import ml_dtypes
+import numpy as np
 from jax import lax
+from jax.experimental import pallas as pl
+from jax.experimental.pallas import tpu as pltpu
 from jax.sharding import PartitionSpec as P
 
 CHAN = 4096
@@ -93,7 +99,7 @@
     return lax.all_to_all(conv_vals, "ctx", split_axis=0, concat_axis=1, tiled=True)
 
 
-def local(section_input, long_filter, short_filter, skip_gain):
+def general_local(section_input, long_filter, short_filter, skip_gain):
     acts_local = section_input[0]
     tok_rows, chan_local = acts_local.shape
     filt_local = long_filter.shape[2]
@@ -161,6 +167,202 @@
     return received[None]
 
 
+EXTRA = 16
+LANES = 128
+
+
+def odd_tables(length):
+    phase = (2 * np.arange(length)[:, None] + 1) * np.arange(length)[None, :] % (4 * length)
+    turn = phase * (2.0 * np.pi / (4 * length))
+    ahead = np.concatenate([np.cos(turn), -np.sin(turn)], axis=0)
+    return ahead.astype(ml_dtypes.bfloat16), (ahead.T / length).astype(ml_dtypes.bfloat16)
+
+
+def spread_table(filters, channels):
+    owner = np.arange(channels) // (channels // filters)
+    return (np.arange(filters)[:, None] == owner[None, :]).astype(ml_dtypes.bfloat16)
+
+
+def column_of(row):
+    return jnp.transpose(jnp.broadcast_to(row[:1], (LANES, row.shape[1])))
+
+
+def cut_kernel(peers, place, x_ref, filt_ref, *refs):
+    outs, sums_ref, turned = refs[:peers], refs[peers], refs[peers + 1]
+    rank = place[0]
+    rows, chans = x_ref.shape
+    width = chans // peers
+    filters = filt_ref.shape[1] // peers
+    turned[...] = jnp.transpose(filt_ref[...].astype(jnp.float32)).astype(jnp.bfloat16)
+    total = jnp.zeros((rows, LANES), jnp.float32)
+    for step in range(peers):
+        target = lax.rem(rank + step, peers)
+        part = x_ref[:, pl.ds(pl.multiple_of(target * width, width), width)]
+        square = part * part
+        for first in range(0, width, LANES):
+            total = total + square[:, first : first + LANES]
+        outs[step][:rows, :] = part.astype(jnp.bfloat16)
+        own = turned[pl.ds(pl.multiple_of(target * filters, filters), filters), :]
+        extra = [own[first : first + EXTRA] for first in range(0, filters, EXTRA)]
+        extra.append(jnp.zeros((EXTRA, width - rows * len(extra)), jnp.bfloat16))
+        outs[step][rows:, :] = jnp.concatenate(extra, axis=1)
+    column = jnp.sum(total, axis=1, keepdims=True)
+    sums_ref[...] = jnp.transpose(jnp.broadcast_to(column, (rows, LANES)))[:8, :]
+
+
+def layer_kernel(peers, place, *refs):
+    blocks = refs[:peers]
+    sums = refs[peers : 2 * peers]
+    taps_ref, skip_ref, ahead_ref, return_ref, spread_ref = refs[2 * peers : 2 * peers + 5]
+    outs = refs[2 * peers + 5 : 3 * peers + 5]
+    held, query, product, spread_filter, spec, filt_spec, weighted, conv = refs[3 * peers + 5 :]
+    rank = place[0]
+    rows = blocks[0].shape[0] - EXTRA
+    width = blocks[0].shape[1]
+    filters = spread_ref.shape[0]
+    half = rows * peers
+    chans = pl.ds(pl.multiple_of(rank * width, width), width)
+    held[:8, :] = jnp.zeros((8, width), jnp.float32)
+    for step in range(peers):
+        begin = pl.multiple_of(lax.rem(rank - step + peers, peers) * rows, rows)
+        scale = column_of(lax.rsqrt(sums[step][...] * (1.0 / CHAN) + 1e-06))
+        for first in range(0, width, LANES):
+            lanes = slice(first, first + LANES)
+            held[pl.ds(begin + 8, rows), lanes] = blocks[step][:rows, lanes].astype(jnp.float32) * scale
+        parts = [blocks[step][rows:, i * rows : (i + 1) * rows] for i in range(filters // EXTRA)]
+        spread_filter[pl.ds(begin, rows), :] = lax.dot_general(
+            jnp.concatenate(parts, axis=0),
+            spread_ref[...],
+            (((0,), (0,)), ((), ())),
+            preferred_element_type=jnp.float32,
+        ).astype(jnp.bfloat16)
+    taps = [[taps_ref[f, i : i + 1, chans].astype(jnp.float32) for i in range(TAPS)] for f in range(3)]
+    for block in range(peers):
+        begin = block * rows
+        moved = [held[pl.ds(begin + 8 - i, rows), :] for i in range(TAPS)]
+        features = []
+        for feature in range(3):
+            running = taps[feature][0] * moved[0]
+            for i in range(1, TAPS):
+                running = running + taps[feature][i] * moved[i]
+            features.append(running)
+        query[pl.ds(begin, rows), :] = features[0].astype(jnp.bfloat16)
+        product[pl.ds(begin, rows), :] = (features[1] * features[2]).astype(jnp.bfloat16)
+    spec[...] = jnp.dot(ahead_ref[...], product[...], preferred_element_type=jnp.float32)
+    filt_spec[...] = jnp.dot(ahead_ref[...], spread_filter[...], preferred_element_type=jnp.float32)
+    sig_re, sig_im = spec[:half, :], spec[half:, :]
+    gain_re, gain_im = filt_spec[:half, :], filt_spec[half:, :]
+    weighted[:half, :] = (sig_re * gain_re - sig_im * gain_im).astype(jnp.bfloat16)
+    weighted[half:, :] = (sig_re * gain_im + sig_im * gain_re).astype(jnp.bfloat16)
+    conv[...] = jnp.dot(return_ref[...], weighted[...], preferred_element_type=jnp.float32)
+    skip = skip_ref[:, chans]
+    for step in range(peers):
+        begin = pl.multiple_of(lax.rem(rank + step, peers) * rows, rows)
+        tokens = pl.ds(begin, rows)
+        acts = blocks[(peers - step) % peers][:rows, :].astype(jnp.float32)
+        gated = conv[tokens, :] + skip * product[tokens, :].astype(jnp.float32)
+        outs[step][...] = (acts + query[tokens, :].astype(jnp.float32) * gated).astype(jnp.bfloat16)
+
+
+def join_kernel(peers, place, *refs):
+    out_ref = refs[peers]
+    width = refs[0].shape[1]
+    for step in range(peers):
+        source = lax.rem(place[0] - step + peers, peers)
+        chans = pl.ds(pl.multiple_of(source * width, width), width)
+        out_ref[:, chans] = refs[step][...].astype(jnp.float32)
+
+
+def on_device(kernel, place, args, outs, scratch=(), flops=0, limit=32):
+    whole = pl.BlockSpec(memory_space=pltpu.VMEM)
+    touched = sum(a.size * a.dtype.itemsize for a in (*args, *outs))
+    return pl.pallas_call(
+        kernel,
+        out_shape=outs,
+        in_specs=[pl.BlockSpec(memory_space=pltpu.SMEM)] + [whole] * len(args),
+        out_specs=[whole] * len(outs),
+        scratch_shapes=list(scratch),
+        compiler_params=pltpu.CompilerParams(vmem_limit_bytes=limit * 2**20),
+        cost_estimate=pl.CostEstimate(flops=flops, bytes_accessed=touched, transcendentals=0),
+    )(place, *args)
+
+
+def hop(x, sections, peers, by_section, by_ctx):
+    route = [
+        (s * peers + c, (s + by_section) % sections * peers + (c + by_ctx) % peers)
+        for s in range(sections)
+        for c in range(peers)
+    ]
+    return lax.ppermute(x, ("section", "ctx"), route)
+
+
+def channel_local(section_input, long_filter, short_filter, skip_gain):
+    acts = section_input[0]
+    rows, chans = acts.shape
+    sections, peers = lax.axis_size("section"), lax.axis_size("ctx")
+    width, filters = chans // peers, long_filter.shape[2] // peers
+    half = rows * peers
+    place = lax.axis_index("ctx").astype(jnp.int32).reshape(1)
+    bf16, f32 = jnp.bfloat16, jnp.float32
+    message = jax.ShapeDtypeStruct((rows + EXTRA, width), bf16)
+    *sent, sums = on_device(
+        functools.partial(cut_kernel, peers),
+        place,
+        [acts, long_filter[0]],
+        [message] * peers + [jax.ShapeDtypeStruct((8, rows), f32)],
+        [pltpu.VMEM((long_filter.shape[2], rows), bf16)],
+    )
+    sums = sums + lax.ppermute(sums, "tp", [(0, 1), (1, 0)])
+    got = [sent[0]] + [hop(sent[k], sections, peers, 0, k) for k in range(1, peers)]
+    got_sums = [sums] + [hop(sums, sections, peers, 0, k) for k in range(1, peers)]
+    ahead, back = odd_tables(half)
+    scratch = [
+        pltpu.VMEM((half + 8, width), f32),
+        pltpu.VMEM((half, width), bf16),
+        pltpu.VMEM((half, width), bf16),
+        pltpu.VMEM((half, width), bf16),
+        pltpu.VMEM((2 * half, width), f32),
+        pltpu.VMEM((2 * half, width), f32),
+        pltpu.VMEM((2 * half, width), bf16),
+        pltpu.VMEM((half, width), f32),
+    ]
+    done = on_device(
+        functools.partial(layer_kernel, peers),
+        place,
+        [
+            *got,
+            *got_sums,
+            short_filter[0],
+            skip_gain,
+            jnp.asarray(ahead),
+            jnp.asarray(back),
+            jnp.asarray(spread_table(filters, width)),
+        ],
+        [jax.ShapeDtypeStruct((rows, width), bf16)] * peers,
+        scratch,
+        flops=12 * half * half * width,
+    )
+    arrived = [hop(done[k], sections, peers, 1, k) for k in range(peers)]
+    (received,) = on_device(
+        functools.partial(join_kernel, peers), place, arrived, [jax.ShapeDtypeStruct((rows, chans), f32)]
+    )
+    return received[None]
+
+
+def fits_channel_plan(mesh, section_input, long_filter):
+    peers, cores = mesh.shape["ctx"], mesh.shape["tp"]
+    tokens = section_input.shape[1]
+    width = section_input.shape[2] // (peers * cores)
+    filters = long_filter.shape[2] // (peers * cores)
+    return (
+        tokens == peers * LANES
+        and tokens <= 1024
+        and width % LANES == 0
+        and filters % EXTRA == 0
+        and filters // EXTRA * LANES <= width
+    )
+
+
 def solution(mesh):
     in_specs = (
         P("section", "ctx", "tp"),
@@ -169,4 +371,10 @@
         P("section", "tp"),
     )
     out_specs = P("section", "ctx", "tp")
-    return jax.shard_map(local, mesh=mesh, in_specs=in_specs, out_specs=out_specs, check_vma=False)
+
+    def layer(section_input, long_filter, short_filter, skip_gain):
+        local = channel_local if fits_channel_plan(mesh, section_input, long_filter) else general_local
+        mapped = jax.shard_map(local, mesh=mesh, in_specs=in_specs, out_specs=out_specs, check_vma=False)
+        return mapped(section_input, long_filter, short_filter, skip_gain)
+
+    return layer

time: 224 us -> 45.8 us (0.20)
  waiting for transfers between devices: 120 us -> 12.6 us
  blocking collectives: 18.8 us -> 0 us
  local copies, waits for them, and re-layouts: 20.7 us -> 4.44 us
  starting transfers between devices: 38.9 us -> 23.4 us
  matrix products: 12.2 us -> 0 us
  other arithmetic: 11.6 us -> 0.01 us
  Pallas kernels: 0 us -> 4.86 us
    all_to_all x8 -> x0, waiting for transfers between devices: 107 us -> none  [the longest x1 23.2 us: local(): lax.all_to_all(back_im, 'ctx', split_axis=1, concat_axis=0, tiled=True)]
    all_to_all x8 -> x0, starting transfers between devices: 33.4 us -> none  [the longest x1 6.32 us: block_columns(): lax.all_to_all(kernel, 'ctx', split_axis=1, concat_axis=0, tiled=True)]
    ppermute x2 -> x11, starting transfers between devices: 5.47 us -> 23.4 us  [the longest x10 23.4 us: hop(): return lax.ppermute(x, ('section', 'ctx'), route)]
    all_to_all x1 -> x0, blocking collectives: 16.4 us -> none  [token_rows(): lax.all_to_all(conv_vals, 'ctx', split_axis=0, concat_axis=1, tiled=True)]
    dot_general x18 -> x0, matrix products: 12.2 us -> none  [the longest x12 8.31 us: product_of(): return jnp.einsum(form, left, right, preferred_element_type=jnp.float32)]
    convert_element_type x11 -> x0, local copies, waits for them, and re-layouts: 9.16 us -> none  [the longest x4 4.41 us: first_section(): return (real_out.astype(jnp.bfloat16), imag_out.astype(jnp.bfloat16))]
    all_to_all x6 -> x0, local copies, waits for them, and re-layouts: 6.54 us -> none  [the longest x3 3.89 us: local(): lax.all_to_all(back_im, 'ctx', split_axis=1, concat_axis=0, tiled=True)]
    pallas_call x0 -> x3, Pallas kernels: none -> 4.86 us  [on_device(): pl.pallas_call(kernel, out_shape=outs, in_specs=[pl.BlockSpec(memory_spac...]
  transfers between devices with their start and end apart: 10 -> 11, of which waited for: 9 -> 5; matrix products, arithmetic and copies ran while one was open for 10% -> 0% of each run, Pallas kernels for 0% -> 0%
where the time goes in v1:
time: 45.8 us; the launch traced here: 45.3 us
  starting transfers between devices  23.4 us (51%)
  waiting for transfers between devices  12.6 us (28%)
  Pallas kernels  4.86 us (11%)
  local copies, waits for them, and re-layouts  4.44 us (10%)
    ppermute x10, starting transfers between devices, hop(): return lax.ppermute(x, ('section', 'ctx'), route)  23.4 us
    ppermute x10, waiting for transfers between devices, hop(): return lax.ppermute(x, ('section', 'ctx'), route)  11.4 us
    pallas_call x3, Pallas kernels, on_device(): pl.pallas_call(kernel, out_shape=outs, in_specs=[pl.BlockSpec(memory_spac...  4.86 us
    unnamed x14, local copies, waits for them, and re-layouts  4.44 us
    ppermute x1, waiting for transfers between devices, channel_local(): sums = sums + lax.ppermute(sums, 'tp', [(0, 1), (1, 0)])  1.16 us
  transfers between devices with their start and end apart: 11, of which 5 were waited for; matrix products, arithmetic and copies ran while one was open for 0% of the time, Pallas kernels for 0%

profile of v1, /device:TPU:0, one launch (start us, length us, event | category | flops | bytes accessed | tf_op | source)
XLA Modules:
  0.0 45.3 jit_solution(17475454815200055108)
XLA Ops:
  0.0 0.0 copy-start
  0.0 1.2 %copy-done = f32[1,128,2048]{2,1,0:T(8,128)S(1)} copy-done((f32[1,128,2048]{2,1,0:T(8,128)S(1)}, f32[1,128,2048]{2,1,0:T(8,128)}, u32[]{:S(2)}) %copy-start) | copy-done | bytes 1048600
  1.2 0.0 copy-start.1
  1.2 0.8 %copy-done.1 = bf16[1,128,128]{2,1,0:T(8,128)(2,1)S(1)} copy-done((bf16[1,128,128]{2,1,0:T(8,128)(2,1)S(1)}, bf16[1,128,128]{2,1,0:T(8,128)(2,1)}, u32[]{:S(2)}) %copy-start.1) | copy-done | bytes 32792
  2.0 0.0 copy-start.2
  2.0 0.0 copy-start.6
  2.0 0.2 shard_map.73
  2.2 3.1 %collective-permute-start = (bf16[144,512]{1,0:T(8,128)(2,1)S(1)}, bf16[144,512]{1,0:T(8,128)(2,1)S(1)}, u32[]{:S(2)}, u32[]{:S(2)}) collective-permute-start(bf16[144,512]{1,0:T(8,128)(2,1)S(1)} %get-tuple-element.15), channel_id=1, source_target_pairs={{0,2},{2,4},{4,6},{6,0},{8,10},{10,12},{12,14},{14,8},{16,18},{18,... | collective-permute-start | bytes 442376 | tf_op jit(solution)/shard_map/ppermute | solution.py:296
  5.2 2.6 %collective-permute-start.1 = (bf16[144,512]{1,0:T(8,128)(2,1)S(1)}, bf16[144,512]{1,0:T(8,128)(2,1)S(1)}, u32[]{:S(2)}, u32[]{:S(2)}) collective-permute-start(bf16[144,512]{1,0:T(8,128)(2,1)S(1)} %get-tuple-element.16), channel_id=1, source_target_pairs={{0,4},{2,6},{4,0},{6,2},{8,12},{10,14},{12,8},{14,10},{16,20},{18,... | collective-permute-start | bytes 442376 | tf_op jit(solution)/shard_map/ppermute | solution.py:296
  7.8 1.3 %collective-permute-start.2 = (bf16[144,512]{1,0:T(8,128)(2,1)S(1)}, bf16[144,512]{1,0:T(8,128)(2,1)S(1)}, u32[]{:S(2)}, u32[]{:S(2)}) collective-permute-start(bf16[144,512]{1,0:T(8,128)(2,1)S(1)} %get-tuple-element.17), channel_id=1, source_target_pairs={{0,6},{2,0},{4,2},{6,4},{8,14},{10,8},{12,10},{14,12},{16,22},{18,... | collective-permute-start | bytes 442376 | tf_op jit(solution)/shard_map/ppermute | solution.py:296
  9.2 0.0 copy-start.3
  9.2 0.0 collective-permute-start.3
  9.2 1.2 %collective-permute-done.3 = f32[8,128]{1,0:T(8,128)S(1)} collective-permute-done((f32[8,128]{1,0:T(8,128)S(1)}, f32[8,128]{1,0:T(8,128)S(1)}, u32[]{:S(2)}, u32[]{:S(2)}) %collective-permute-start.3) | collective-permute-done | bytes 4128 | tf_op jit(solution)/shard_map/ppermute | solution.py:315
  10.4 0.4 collective-permute-start.6
  10.8 1.7 %collective-permute-start.5 = (f32[8,128]{1,0:T(8,128)S(1)}, f32[8,128]{1,0:T(8,128)S(1)}, u32[]{:S(2)}, u32[]{:S(2)}) collective-permute-start(f32[8,128]{1,0:T(8,128)S(1)} %add.3.refs_4_), channel_id=1, source_target_pairs={{0,4},{2,6},{4,0},{6,2},{8,12},{10,14},{12,8},{14,10},{16,20},{18,... | collective-permute-start | bytes 12296 | tf_op jit(solution)/shard_map/ppermute | solution.py:296
  12.5 2.8 %collective-permute-done.6.refs_7_ = f32[8,128]{1,0:T(8,128)S(1)} collective-permute-done((f32[8,128]{1,0:T(8,128)S(1)}, f32[8,128]{1,0:T(8,128)S(1)}, u32[]{:S(2)}, u32[]{:S(2)}) %collective-permute-start.6) | collective-permute-done | bytes 4128 | tf_op jit(solution)/shard_map/ppermute | solution.py:296
  15.2 6.3 %collective-permute-start.4 = (f32[8,128]{1,0:T(8,128)S(1)}, f32[8,128]{1,0:T(8,128)S(1)}, u32[]{:S(2)}, u32[]{:S(2)}) collective-permute-start(f32[8,128]{1,0:T(8,128)S(1)} %add.3.refs_4_), channel_id=1, source_target_pairs={{0,2},{2,4},{4,6},{6,0},{8,10},{10,12},{12,14},{14,8},{16,18},{18,... | collective-permute-start | bytes 12296 | tf_op jit(solution)/shard_map/ppermute | solution.py:296
  21.5 0.0 collective-permute-done.5.refs_6_
  21.5 1.3 %collective-permute-done.4.refs_5_ = f32[8,128]{1,0:T(8,128)S(1)} collective-permute-done((f32[8,128]{1,0:T(8,128)S(1)}, f32[8,128]{1,0:T(8,128)S(1)}, u32[]{:S(2)}, u32[]{:S(2)}) %collective-permute-start.4) | collective-permute-done | bytes 4128 | tf_op jit(solution)/shard_map/ppermute | solution.py:296
  22.8 0.0 collective-permute-done.refs_1_
  22.8 0.0 collective-permute-done.1.refs_2_
  22.8 0.0 collective-permute-done.2.refs_3_
  22.8 0.0 copy-done.2
  22.9 0.0 copy-done.6
  22.9 0.0 copy-done.3
  22.9 0.0 copy-start.4
  22.9 1.2 %copy-done.4 = bf16[512,1024]{1,0:T(8,128)(2,1)S(1)} copy-done((bf16[512,1024]{1,0:T(8,128)(2,1)S(1)}, bf16[512,1024]{1,0:T(8,128)(2,1)}, u32[]{:S(2)}) %copy-start.4) | copy-done | bytes 1048600
  24.1 0.0 copy-start.5
  24.1 1.2 %copy-done.5 = bf16[1024,512]{1,0:T(8,128)(2,1)S(1)} copy-done((bf16[1024,512]{1,0:T(8,128)(2,1)S(1)}, bf16[1024,512]{1,0:T(8,128)(2,1)}, u32[]{:S(2)}) %copy-start.5) | copy-done | bytes 1048600
  25.3 3.6 %shard_map.74 = (bf16[128,512]{1,0:T(8,128)(2,1)S(1)}, bf16[128,512]{1,0:T(8,128)(2,1)S(1)}, bf16[128,512]{1,0:T(8,128)(2,1)S(1)}, bf16[128,512]{1,0:T(8,128)(2,1)S(1)}) custom-call(s32[1]{0:T(128)} %bitcast.place, bf16[144,512]{1,0:T(8,128)(2,1)S(1)} %get-tuple-element.14.refs_0_, bf16[144,512]{1,0:T(8,128)(2,1)S(1)} %collective-permute-done.refs_1_, ...), custom_call_target="tpu_custom_call" | custom-call | flops 1610612736 | bytes 3305472 | tf_op jit(solution)/shard_map/pallas_call | solution.py:279
  29.0 1.5 %collective-permute-start.7 = (bf16[128,512]{1,0:T(8,128)(2,1)S(1)}, bf16[128,512]{1,0:T(8,128)(2,1)S(1)}, u32[]{:S(2)}, u32[]{:S(2)}) collective-permute-start(bf16[128,512]{1,0:T(8,128)(2,1)S(1)} %get-tuple-element.19), channel_id=1, source_target_pairs={{0,8},{2,10},{4,12},{6,14},{8,16},{10,18},{12,20},{14,22},{16,24},... | collective-permute-start | bytes 393224 | tf_op jit(solution)/shard_map/ppermute | solution.py:296
  30.5 3.2 %collective-permute-start.8 = (bf16[128,512]{1,0:T(8,128)(2,1)S(1)}, bf16[128,512]{1,0:T(8,128)(2,1)S(1)}, u32[]{:S(2)}, u32[]{:S(2)}) collective-permute-start(bf16[128,512]{1,0:T(8,128)(2,1)S(1)} %get-tuple-element.20), channel_id=1, source_target_pairs={{0,10},{2,12},{4,14},{6,8},{8,18},{10,20},{12,22},{14,16},{16,26},... | collective-permute-start | bytes 393224 | tf_op jit(solution)/shard_map/ppermute | solution.py:296
  33.7 0.0 collective-permute-start.9
  33.7 3.3 %collective-permute-start.10 = (bf16[128,512]{1,0:T(8,128)(2,1)S(1)}, bf16[128,512]{1,0:T(8,128)(2,1)S(1)}, u32[]{:S(2)}, u32[]{:S(2)}) collective-permute-start(bf16[128,512]{1,0:T(8,128)(2,1)S(1)} %get-tuple-element.22), channel_id=1, source_target_pairs={{0,14},{2,8},{4,10},{6,12},{8,22},{10,16},{12,18},{14,20},{16,30},... | collective-permute-start | bytes 393224 | tf_op jit(solution)/shard_map/ppermute | solution.py:296
  37.0 0.0 collective-permute-done.7.refs_0_
  37.0 3.2 %collective-permute-done.8.refs_1_ = bf16[128,512]{1,0:T(8,128)(2,1)S(1)} collective-permute-done((bf16[128,512]{1,0:T(8,128)(2,1)S(1)}, bf16[128,512]{1,0:T(8,128)(2,1)S(1)}, u32[]{:S(2)}, u32[]{:S(2)}) %collective-permute-start.8) | collective-permute-done | bytes 131104 | tf_op jit(solution)/shard_map/ppermute | solution.py:296
  40.2 4.1 %collective-permute-done.9.refs_2_ = bf16[128,512]{1,0:T(8,128)(2,1)S(1)} collective-permute-done((bf16[128,512]{1,0:T(8,128)(2,1)S(1)}, bf16[128,512]{1,0:T(8,128)(2,1)S(1)}, u32[]{:S(2)}, u32[]{:S(2)}) %collective-permute-start.9) | collective-permute-done | bytes 131104 | tf_op jit(solution)/shard_map/ppermute | solution.py:296
  44.3 0.0 collective-permute-done.10.refs_3_
  44.3 1.0 %shard_map.75 = f32[128,2048]{1,0:T(8,128)} custom-call(s32[1]{0:T(128)} %bitcast.place, bf16[128,512]{1,0:T(8,128)(2,1)S(1)} %collective-permute-done.7.refs_0_, bf16[128,512]{1,0:T(8,128)(2,1)S(1)} %collective-permute-done.8.refs_1_, bf16[128,512]{1,0:T(8,128)(2,1)S(1)} %collective-permute-done.9.refs_2_, bf16[128,512]{1,0:T(8,128)(2,1)S(1)} %collective-permute-done.10.refs_3_), custom_call_target="tpu_custom_call" | custom-call | bytes 1572864 | tf_op jit(solution)/shard_map/pallas_call | solution.py:279
  (1 shorter events, 0.0 us)
Async XLA Ops:
  0.0 1.2 %copy-start = (f32[1,128,2048]{2,1,0:T(8,128)S(1)}, f32[1,128,2048]{2,1,0:T(8,128)}, u32[]{:S(2)}) copy-start(f32[1,128,2048]{2,1,0:T(8,128)} %param.7) | copy-start | bytes 3145732
  1.2 0.8 %copy-start.1 = (bf16[1,128,128]{2,1,0:T(8,128)(2,1)S(1)}, bf16[1,128,128]{2,1,0:T(8,128)(2,1)}, u32[]{:S(2)}) copy-start(bf16[1,128,128]{2,1,0:T(8,128)(2,1)} %param.8) | copy-start | bytes 98308
  2.0 20.9 %copy-start.2 = (bf16[1,3,3,2048]{3,2,1,0:T(4,128)(2,1)S(1)}, bf16[1,3,3,2048]{3,2,1,0:T(4,128)(2,1)}, u32[]{:S(2)}) copy-start(bf16[1,3,3,2048]{3,2,1,0:T(4,128)(2,1)} %param.9) | copy-start | bytes 110596
  2.0 20.9 %copy-start.6 = (bf16[32,512]{1,0:T(8,128)(2,1)S(1)}, bf16[32,512]{1,0:T(8,128)(2,1)}, u32[]{:S(2)}) copy-start(bf16[32,512]{1,0:T(8,128)(2,1)} %constant.14.clone.refs_12_) | copy-start | bytes 98308
  2.2 20.6 %collective-permute-start = (bf16[144,512]{1,0:T(8,128)(2,1)S(1)}, bf16[144,512]{1,0:T(8,128)(2,1)S(1)}, u32[]{:S(2)}, u32[]{:S(2)}) collective-permute-start(bf16[144,512]{1,0:T(8,128)(2,1)S(1)} %get-tuple-element.15), channel_id=1, source_target_pairs={{0,2},{2,4},{4,6},{6,0},{8,10},{10,12},{12,14},{14,8},{16,18},{18,... | collective-permute-start | bytes 442376 | tf_op jit(solution)/shard_map/ppermute | solution.py:296
  5.2 17.6 %collective-permute-start.1 = (bf16[144,512]{1,0:T(8,128)(2,1)S(1)}, bf16[144,512]{1,0:T(8,128)(2,1)S(1)}, u32[]{:S(2)}, u32[]{:S(2)}) collective-permute-start(bf16[144,512]{1,0:T(8,128)(2,1)S(1)} %get-tuple-element.16), channel_id=1, source_target_pairs={{0,4},{2,6},{4,0},{6,2},{8,12},{10,14},{12,8},{14,10},{16,20},{18,... | collective-permute-start | bytes 442376 | tf_op jit(solution)/shard_map/ppermute | solution.py:296
  7.8 15.0 %collective-permute-start.2 = (bf16[144,512]{1,0:T(8,128)(2,1)S(1)}, bf16[144,512]{1,0:T(8,128)(2,1)S(1)}, u32[]{:S(2)}, u32[]{:S(2)}) collective-permute-start(bf16[144,512]{1,0:T(8,128)(2,1)S(1)} %get-tuple-element.17), channel_id=1, source_target_pairs={{0,6},{2,0},{4,2},{6,4},{8,14},{10,8},{12,10},{14,12},{16,22},{18,... | collective-permute-start | bytes 442376 | tf_op jit(solution)/shard_map/ppermute | solution.py:296
  9.2 13.7 %copy-start.3 = (f32[1,2048]{1,0:T(1,128)S(1)}, f32[1,2048]{1,0:T(1,128)}, u32[]{:S(2)}) copy-start(f32[1,2048]{1,0:T(1,128)} %refs_9_.1) | copy-start | bytes 24580
  9.2 1.2 %collective-permute-start.3 = (f32[8,128]{1,0:T(8,128)S(1)}, f32[8,128]{1,0:T(8,128)S(1)}, u32[]{:S(2)}, u32[]{:S(2)}) collective-permute-start(f32[8,128]{1,0:T(8,128)S(1)} %get-tuple-element.18), channel_id=1, source_target_pairs={{0,1},{1,0},{2,3},{3,2},{4,5},{5,4},{6,7},{7,6},{8,9},{9,8},{10,11... | collective-permute-start | bytes 12296 | tf_op jit(solution)/shard_map/ppermute | solution.py:315
  10.4 4.9 %collective-permute-start.6 = (f32[8,128]{1,0:T(8,128)S(1)}, f32[8,128]{1,0:T(8,128)S(1)}, u32[]{:S(2)}, u32[]{:S(2)}) collective-permute-start(f32[8,128]{1,0:T(8,128)S(1)} %add.3.refs_4_), channel_id=1, source_target_pairs={{0,6},{2,0},{4,2},{6,4},{8,14},{10,8},{12,10},{14,12},{16,22},{18,... | collective-permute-start | bytes 12296 | tf_op jit(solution)/shard_map/ppermute | solution.py:296
  10.8 10.7 %collective-permute-start.5 = (f32[8,128]{1,0:T(8,128)S(1)}, f32[8,128]{1,0:T(8,128)S(1)}, u32[]{:S(2)}, u32[]{:S(2)}) collective-permute-start(f32[8,128]{1,0:T(8,128)S(1)} %add.3.refs_4_), channel_id=1, source_target_pairs={{0,4},{2,6},{4,0},{6,2},{8,12},{10,14},{12,8},{14,10},{16,20},{18,... | collective-permute-start | bytes 12296 | tf_op jit(solution)/shard_map/ppermute | solution.py:296
  15.2 7.6 %collective-permute-start.4 = (f32[8,128]{1,0:T(8,128)S(1)}, f32[8,128]{1,0:T(8,128)S(1)}, u32[]{:S(2)}, u32[]{:S(2)}) collective-permute-start(f32[8,128]{1,0:T(8,128)S(1)} %add.3.refs_4_), channel_id=1, source_target_pairs={{0,2},{2,4},{4,6},{6,0},{8,10},{10,12},{12,14},{14,8},{16,18},{18,... | collective-permute-start | bytes 12296 | tf_op jit(solution)/shard_map/ppermute | solution.py:296
  22.9 1.2 %copy-start.4 = (bf16[512,1024]{1,0:T(8,128)(2,1)S(1)}, bf16[512,1024]{1,0:T(8,128)(2,1)}, u32[]{:S(2)}) copy-start(bf16[512,1024]{1,0:T(8,128)(2,1)} %constant.13.clone.refs_11_) | copy-start | bytes 3145732
  24.1 1.2 %copy-start.5 = (bf16[1024,512]{1,0:T(8,128)(2,1)S(1)}, bf16[1024,512]{1,0:T(8,128)(2,1)}, u32[]{:S(2)}) copy-start(bf16[1024,512]{1,0:T(8,128)(2,1)} %constant.12.clone.refs_10_) | copy-start | bytes 3145732
  29.0 8.0 %collective-permute-start.7 = (bf16[128,512]{1,0:T(8,128)(2,1)S(1)}, bf16[128,512]{1,0:T(8,128)(2,1)S(1)}, u32[]{:S(2)}, u32[]{:S(2)}) collective-permute-start(bf16[128,512]{1,0:T(8,128)(2,1)S(1)} %get-tuple-element.19), channel_id=1, source_target_pairs={{0,8},{2,10},{4,12},{6,14},{8,16},{10,18},{12,20},{14,22},{16,24},... | collective-permute-start | bytes 393224 | tf_op jit(solution)/shard_map/ppermute | solution.py:296
  30.5 9.7 %collective-permute-start.8 = (bf16[128,512]{1,0:T(8,128)(2,1)S(1)}, bf16[128,512]{1,0:T(8,128)(2,1)S(1)}, u32[]{:S(2)}, u32[]{:S(2)}) collective-permute-start(bf16[128,512]{1,0:T(8,128)(2,1)S(1)} %get-tuple-element.20), channel_id=1, source_target_pairs={{0,10},{2,12},{4,14},{6,8},{8,18},{10,20},{12,22},{14,16},{16,26},... | collective-permute-start | bytes 393224 | tf_op jit(solution)/shard_map/ppermute | solution.py:296
  33.7 10.6 %collective-permute-start.9 = (bf16[128,512]{1,0:T(8,128)(2,1)S(1)}, bf16[128,512]{1,0:T(8,128)(2,1)S(1)}, u32[]{:S(2)}, u32[]{:S(2)}) collective-permute-start(bf16[128,512]{1,0:T(8,128)(2,1)S(1)} %get-tuple-element.21), channel_id=1, source_target_pairs={{0,12},{2,14},{4,8},{6,10},{8,20},{10,22},{12,16},{14,18},{16,28},... | collective-permute-start | bytes 393224 | tf_op jit(solution)/shard_map/ppermute | solution.py:296
  33.7 10.6 %collective-permute-start.10 = (bf16[128,512]{1,0:T(8,128)(2,1)S(1)}, bf16[128,512]{1,0:T(8,128)(2,1)S(1)}, u32[]{:S(2)}, u32[]{:S(2)}) collective-permute-start(bf16[128,512]{1,0:T(8,128)(2,1)S(1)} %get-tuple-element.22), channel_id=1, source_target_pairs={{0,14},{2,8},{4,10},{6,12},{8,22},{10,16},{12,18},{14,20},{16,30},... | collective-permute-start | bytes 393224 | tf_op jit(solution)/shard_map/ppermute | solution.py:296

commit v2 on v1

--- a/solution.py
+++ b/solution.py
@@ -184,58 +184,120 @@
 
 
 def column_of(row):
-    return jnp.transpose(jnp.broadcast_to(row[:1], (LANES, row.shape[1])))
-
-
-def cut_kernel(peers, place, x_ref, filt_ref, *refs):
-    outs, sums_ref, turned = refs[:peers], refs[peers], refs[peers + 1]
-    rank = place[0]
-    rows, chans = x_ref.shape
+    return jnp.transpose(jnp.broadcast_to(row, (LANES, row.shape[1])))
+
+
+def three_terms(x):
+    terms = []
+    for _ in range(3):
+        terms.append(x.astype(jnp.bfloat16).astype(jnp.float32))
+        x = x - terms[-1]
+    return terms
+
+
+def next_place(rank, step, peers):
+    return lax.rem(rank + step + peers, peers)
+
+
+def cut_kernel(peers, x_hbm, filt_hbm, *refs):
+    outs, (x_ref, filt_ref, turned, sems) = refs[:peers], refs[peers:]
+    rank = lax.axis_index("ctx")
+    rows, chans = x_hbm.shape
     width = chans // peers
-    filters = filt_ref.shape[1] // peers
+    filters = filt_hbm.shape[1] // peers
+    pieces = sems.shape[0] - 1
+    depth = rows // pieces
+    copies = [
+        pltpu.make_async_copy(
+            x_hbm.at[pl.ds(i * depth, depth)], x_ref.at[pl.ds(i * depth, depth)], sems.at[i]
+        )
+        for i in range(pieces)
+    ]
+    copies.append(pltpu.make_async_copy(filt_hbm, filt_ref, sems.at[pieces]))
+    for copy in copies:
+        copy.start()
+    columns = []
+    for i in range(pieces):
+        copies[i].wait()
+        here = pl.ds(i * depth, depth)
+        total = jnp.zeros((depth, LANES), jnp.float32)
+        for step in range(peers):
+            target = next_place(rank, step, peers)
+            part = x_ref[here, pl.ds(pl.multiple_of(target * width, width), width)]
+            outs[step][here, :] = part.astype(jnp.bfloat16)
+            for first in range(0, width, LANES):
+                total = total + part[:, first : first + LANES] * part[:, first : first + LANES]
+        columns.append(jnp.sum(total, axis=1, keepdims=True))
+    column = jnp.concatenate(columns, axis=0)
+    row = jnp.transpose(jnp.broadcast_to(column, (rows, LANES)))[:EXTRA, :]
+    nth = lax.broadcasted_iota(jnp.int32, (EXTRA, rows), 0)
+    terms = three_terms(row)
+    sums = jnp.where(nth == 0, terms[0], jnp.where(nth == 1, terms[1], jnp.where(nth == 2, terms[2], 0.0)))
+    sums = sums.astype(jnp.bfloat16)
+    copies[pieces].wait()
     turned[...] = jnp.transpose(filt_ref[...].astype(jnp.float32)).astype(jnp.bfloat16)
-    total = jnp.zeros((rows, LANES), jnp.float32)
     for step in range(peers):
-        target = lax.rem(rank + step, peers)
-        part = x_ref[:, pl.ds(pl.multiple_of(target * width, width), width)]
-        square = part * part
-        for first in range(0, width, LANES):
-            total = total + square[:, first : first + LANES]
-        outs[step][:rows, :] = part.astype(jnp.bfloat16)
+        target = next_place(rank, step, peers)
         own = turned[pl.ds(pl.multiple_of(target * filters, filters), filters), :]
-        extra = [own[first : first + EXTRA] for first in range(0, filters, EXTRA)]
-        extra.append(jnp.zeros((EXTRA, width - rows * len(extra)), jnp.bfloat16))
+        extra = [sums] + [own[first : first + EXTRA] for first in range(0, filters, EXTRA)]
+        if width > rows * len(extra):
+            extra.append(jnp.zeros((EXTRA, width - rows * len(extra)), jnp.bfloat16))
         outs[step][rows:, :] = jnp.concatenate(extra, axis=1)
-    column = jnp.sum(total, axis=1, keepdims=True)
-    sums_ref[...] = jnp.transpose(jnp.broadcast_to(column, (rows, LANES)))[:8, :]
-
-
-def layer_kernel(peers, place, *refs):
+
+
+def table_kernel(pieces, after, *refs):
+    count = (len(refs) - 1) // 2
+    tables, outs, sems = refs[:count], refs[count : 2 * count], refs[2 * count]
+    copies = []
+    for t in range(count):
+        depth = tables[t].shape[0] // pieces
+        for i in range(pieces):
+            here = pl.ds(i * depth, depth)
+            copies.append(pltpu.make_async_copy(tables[t].at[here], outs[t].at[here], sems.at[len(copies)]))
+    for copy in copies:
+        copy.start()
+    for copy in copies:
+        copy.wait()
+
+
+def filter_kernel(peers, *refs):
     blocks = refs[:peers]
-    sums = refs[peers : 2 * peers]
-    taps_ref, skip_ref, ahead_ref, return_ref, spread_ref = refs[2 * peers : 2 * peers + 5]
-    outs = refs[2 * peers + 5 : 3 * peers + 5]
-    held, query, product, spread_filter, spec, filt_spec, weighted, conv = refs[3 * peers + 5 :]
-    rank = place[0]
+    ahead_ref, spread_ref, filt_spec, spread_filter = refs[peers:]
+    rank = lax.axis_index("ctx")
     rows = blocks[0].shape[0] - EXTRA
-    width = blocks[0].shape[1]
     filters = spread_ref.shape[0]
-    half = rows * peers
-    chans = pl.ds(pl.multiple_of(rank * width, width), width)
-    held[:8, :] = jnp.zeros((8, width), jnp.float32)
     for step in range(peers):
-        begin = pl.multiple_of(lax.rem(rank - step + peers, peers) * rows, rows)
-        scale = column_of(lax.rsqrt(sums[step][...] * (1.0 / CHAN) + 1e-06))
-        for first in range(0, width, LANES):
-            lanes = slice(first, first + LANES)
-            held[pl.ds(begin + 8, rows), lanes] = blocks[step][:rows, lanes].astype(jnp.float32) * scale
-        parts = [blocks[step][rows:, i * rows : (i + 1) * rows] for i in range(filters // EXTRA)]
+        begin = pl.multiple_of(next_place(rank, -step, peers) * rows, rows)
+        parts = [blocks[step][rows:, i * rows : (i + 1) * rows] for i in range(1, 1 + filters // EXTRA)]
         spread_filter[pl.ds(begin, rows), :] = lax.dot_general(
             jnp.concatenate(parts, axis=0),
             spread_ref[...],
             (((0,), (0,)), ((), ())),
             preferred_element_type=jnp.float32,
         ).astype(jnp.bfloat16)
+    filt_spec[...] = jnp.dot(ahead_ref[...], spread_filter[...], preferred_element_type=jnp.float32)
+
+
+def layer_kernel(peers, *refs):
+    blocks = refs[:peers]
+    other_sums, taps_ref, skip_ref, ahead_ref, return_ref, filt_spec = refs[peers : peers + 6]
+    outs = refs[peers + 6 : 2 * peers + 6]
+    held, query, product, spec, weighted, conv = refs[2 * peers + 6 :]
+    rank = lax.axis_index("ctx")
+    rows = blocks[0].shape[0] - EXTRA
+    width = blocks[0].shape[1]
+    half = rows * peers
+    chans = pl.ds(pl.multiple_of(rank * width, width), width)
+    held[:8, :] = jnp.zeros((8, width), jnp.float32)
+    for step in range(peers):
+        begin = pl.multiple_of(next_place(rank, -step, peers) * rows, rows)
+        here = blocks[step][rows:, :rows].astype(jnp.float32)
+        there = other_sums[step * EXTRA : (step + 1) * EXTRA, :].astype(jnp.float32)
+        square = jnp.sum(here, axis=0, keepdims=True) + jnp.sum(there, axis=0, keepdims=True)
+        scale = column_of(lax.rsqrt(square * (1.0 / CHAN) + 1e-06))
+        for first in range(0, width, LANES):
+            lanes = slice(first, first + LANES)
+            held[pl.ds(begin + 8, rows), lanes] = blocks[step][:rows, lanes].astype(jnp.float32) * scale
     taps = [[taps_ref[f, i : i + 1, chans].astype(jnp.float32) for i in range(TAPS)] for f in range(3)]
     for block in range(peers):
         begin = block * rows
@@ -249,7 +311,6 @@
         query[pl.ds(begin, rows), :] = features[0].astype(jnp.bfloat16)
         product[pl.ds(begin, rows), :] = (features[1] * features[2]).astype(jnp.bfloat16)
     spec[...] = jnp.dot(ahead_ref[...], product[...], preferred_element_type=jnp.float32)
-    filt_spec[...] = jnp.dot(ahead_ref[...], spread_filter[...], preferred_element_type=jnp.float32)
     sig_re, sig_im = spec[:half, :], spec[half:, :]
     gain_re, gain_im = filt_spec[:half, :], filt_spec[half:, :]
     weighted[:half, :] = (sig_re * gain_re - sig_im * gain_im).astype(jnp.bfloat16)
@@ -257,34 +318,40 @@
     conv[...] = jnp.dot(return_ref[...], weighted[...], preferred_element_type=jnp.float32)
     skip = skip_ref[:, chans]
     for step in range(peers):
-        begin = pl.multiple_of(lax.rem(rank + step, peers) * rows, rows)
-        tokens = pl.ds(begin, rows)
+        tokens = pl.ds(pl.multiple_of(next_place(rank, step, peers) * rows, rows), rows)
         acts = blocks[(peers - step) % peers][:rows, :].astype(jnp.float32)
         gated = conv[tokens, :] + skip * product[tokens, :].astype(jnp.float32)
         outs[step][...] = (acts + query[tokens, :].astype(jnp.float32) * gated).astype(jnp.bfloat16)
 
 
-def join_kernel(peers, place, *refs):
-    out_ref = refs[peers]
-    width = refs[0].shape[1]
+def join_kernel(peers, *refs):
+    parts, out_hbm, wide, sems = refs[:peers], refs[peers], refs[peers + 1], refs[peers + 2]
+    width = parts[0].shape[1]
+    rank = lax.axis_index("ctx")
+    copies = []
     for step in range(peers):
-        source = lax.rem(place[0] - step + peers, peers)
-        chans = pl.ds(pl.multiple_of(source * width, width), width)
-        out_ref[:, chans] = refs[step][...].astype(jnp.float32)
-
-
-def on_device(kernel, place, args, outs, scratch=(), flops=0, limit=32):
+        wide[step, :, :] = parts[step][...].astype(jnp.float32)
+        chans = pl.ds(pl.multiple_of(next_place(rank, -step, peers) * width, width), width)
+        copies.append(pltpu.make_async_copy(wide.at[step], out_hbm.at[:, chans], sems.at[step]))
+        copies[-1].start()
+    for copy in copies:
+        copy.wait()
+
+
+def on_device(kernel, args, outs, scratch=(), in_hbm=(), out_hbm=False, flops=0, limit=32):
     whole = pl.BlockSpec(memory_space=pltpu.VMEM)
+    far = pl.BlockSpec(memory_space=pltpu.HBM)
     touched = sum(a.size * a.dtype.itemsize for a in (*args, *outs))
+    args = [pltpu.with_memory_space_constraint(a, pltpu.HBM) if i in in_hbm else a for i, a in enumerate(args)]
     return pl.pallas_call(
         kernel,
         out_shape=outs,
-        in_specs=[pl.BlockSpec(memory_space=pltpu.SMEM)] + [whole] * len(args),
-        out_specs=[whole] * len(outs),
+        in_specs=[far if i in in_hbm else whole for i in range(len(args))],
+        out_specs=[far if out_hbm else whole] * len(outs),
         scratch_shapes=list(scratch),
         compiler_params=pltpu.CompilerParams(vmem_limit_bytes=limit * 2**20),
         cost_estimate=pl.CostEstimate(flops=flops, bytes_accessed=touched, transcendentals=0),
-    )(place, *args)
+    )(*args)
 
 
 def hop(x, sections, peers, by_section, by_ctx):
@@ -302,49 +369,64 @@
     sections, peers = lax.axis_size("section"), lax.axis_size("ctx")
     width, filters = chans // peers, long_filter.shape[2] // peers
     half = rows * peers
-    place = lax.axis_index("ctx").astype(jnp.int32).reshape(1)
     bf16, f32 = jnp.bfloat16, jnp.float32
-    message = jax.ShapeDtypeStruct((rows + EXTRA, width), bf16)
-    *sent, sums = on_device(
+    pieces = 4
+    sent = on_device(
         functools.partial(cut_kernel, peers),
-        place,
         [acts, long_filter[0]],
-        [message] * peers + [jax.ShapeDtypeStruct((8, rows), f32)],
-        [pltpu.VMEM((long_filter.shape[2], rows), bf16)],
-    )
-    sums = sums + lax.ppermute(sums, "tp", [(0, 1), (1, 0)])
-    got = [sent[0]] + [hop(sent[k], sections, peers, 0, k) for k in range(1, peers)]
-    got_sums = [sums] + [hop(sums, sections, peers, 0, k) for k in range(1, peers)]
-    ahead, back = odd_tables(half)
-    scratch = [
-        pltpu.VMEM((half + 8, width), f32),
-        pltpu.VMEM((half, width), bf16),
-        pltpu.VMEM((half, width), bf16),
-        pltpu.VMEM((half, width), bf16),
-        pltpu.VMEM((2 * half, width), f32),
-        pltpu.VMEM((2 * half, width), f32),
-        pltpu.VMEM((2 * half, width), bf16),
-        pltpu.VMEM((half, width), f32),
-    ]
+        [jax.ShapeDtypeStruct((rows + EXTRA, width), bf16)] * peers,
+        [
+            pltpu.VMEM((rows, chans), f32),
+            pltpu.VMEM(long_filter.shape[1:], bf16),
+            pltpu.VMEM((long_filter.shape[2], rows), bf16),
+            pltpu.SemaphoreType.DMA((pieces + 1,)),
+        ],
+        in_hbm=(0, 1),
+    )
+    got = [sent[0]] + [None] * (peers - 1)
+    far_first = sorted(range(1, peers), key=lambda k: abs(2 * k - peers))
+    for k in far_first:
+        got[k] = hop(sent[k], sections, peers, 0, k)
+    tables = [jnp.asarray(t) for t in odd_tables(half)]
+    ahead, back = on_device(
+        functools.partial(table_kernel, pieces),
+        [sent[0], *tables],
+        [jax.ShapeDtypeStruct(t.shape, bf16) for t in tables],
+        [pltpu.SemaphoreType.DMA((2 * pieces,))],
+        in_hbm=(1, 2),
+    )
+    own_sums = jnp.concatenate([g[rows:, :rows] for g in got], axis=0)
+    other_sums = lax.ppermute(own_sums, "tp", [(0, 1), (1, 0)])
+    (filt_spec,) = on_device(
+        functools.partial(filter_kernel, peers),
+        [*got, ahead, jnp.asarray(spread_table(filters, width))],
+        [jax.ShapeDtypeStruct((2 * half, width), f32)],
+        [pltpu.VMEM((half, width), bf16)],
+        flops=4 * half * half * width,
+    )
     done = on_device(
         functools.partial(layer_kernel, peers),
-        place,
+        [*got, other_sums, short_filter[0], skip_gain, ahead, back, filt_spec],
+        [jax.ShapeDtypeStruct((rows, width), bf16)] * peers,
         [
-            *got,
-            *got_sums,
-            short_filter[0],
-            skip_gain,
-            jnp.asarray(ahead),
-            jnp.asarray(back),
-            jnp.asarray(spread_table(filters, width)),
+            pltpu.VMEM((half + 8, width), f32),
+            pltpu.VMEM((half, width), bf16),
+            pltpu.VMEM((half, width), bf16),
+            pltpu.VMEM((2 * half, width), f32),
+            pltpu.VMEM((2 * half, width), bf16),
+            pltpu.VMEM((half, width), f32),
         ],
-        [jax.ShapeDtypeStruct((rows, width), bf16)] * peers,
-        scratch,
-        flops=12 * half * half * width,
-    )
-    arrived = [hop(done[k], sections, peers, 1, k) for k in range(peers)]
+        flops=8 * half * half * width,
+    )
+    arrived = [None] * peers
+    for k in [*far_first, 0]:
+        arrived[k] = hop(done[k], sections, peers, 1, k)
     (received,) = on_device(
-        functools.partial(join_kernel, peers), place, arrived, [jax.ShapeDtypeStruct((rows, chans), f32)]
+        functools.partial(join_kernel, peers),
+        arrived,
+        [jax.ShapeDtypeStruct((rows, chans), f32)],
+        [pltpu.VMEM((peers, rows, width), f32), pltpu.SemaphoreType.DMA((peers,))],
+        out_hbm=True,
     )
     return received[None]
 
@@ -359,7 +441,7 @@
         and tokens <= 1024
         and width % LANES == 0
         and filters % EXTRA == 0
-        and filters // EXTRA * LANES <= width
+        and (1 + filters // EXTRA) * LANES <= width
     )
 
 

time: 45.8 us -> 40.4 us (0.88)
  starting transfers between devices: 23.4 us -> 16.4 us
  local copies, waits for them, and re-layouts: 4.44 us -> 0.02 us
  Pallas kernels: 4.86 us -> 8.24 us
  waiting for transfers between devices: 12.6 us -> 15.5 us
    ppermute x10 -> x7, starting transfers between devices: 23.4 us -> 16.4 us  [hop(): return lax.ppermute(x, ('section', 'ctx'), route)]
    unnamed x14 -> x6, local copies, waits for them, and re-layouts: 4.44 us -> 0.02 us
    ppermute x10 -> x7, waiting for transfers between devices: 11.4 us -> 15.3 us  [hop(): return lax.ppermute(x, ('section', 'ctx'), route)]
    pallas_call x3 -> x5, Pallas kernels: 4.86 us -> 8.24 us  [on_device(): pl.pallas_call(kernel, out_shape=outs, in_specs=[far if i in in_hbm else...]
    ppermute x1, waiting for transfers between devices: 1.16 us -> 0.13 us  [channel_local(): other_sums = lax.ppermute(own_sums, 'tp', [(0, 1), (1, 0)])]
  transfers between devices with their start and end apart: 11 -> 8, of which waited for: 5 -> 6; matrix products, arithmetic and copies ran while one was open for 0% -> 0% of each run, Pallas kernels for 0% -> 6%
where the time goes in v2:
time: 40.4 us; the launch traced here: 40.2 us
  starting transfers between devices  16.4 us (41%)
  waiting for transfers between devices  15.5 us (38%)
  Pallas kernels  8.24 us (20%)
    ppermute x7, starting transfers between devices, hop(): return lax.ppermute(x, ('section', 'ctx'), route)  16.4 us
    ppermute x7, waiting for transfers between devices, hop(): return lax.ppermute(x, ('section', 'ctx'), route)  15.3 us
    pallas_call x5, Pallas kernels, on_device(): pl.pallas_call(kernel, out_shape=outs, in_specs=[far if i in in_hbm else...  8.24 us
  transfers between devices with their start and end apart: 8, of which 6 were waited for; matrix products, arithmetic and copies ran while one was open for 0% of the time, Pallas kernels for 6%

profile of v2, /device:TPU:0, one launch (start us, length us, event | category | flops | bytes accessed | tf_op | source)
XLA Modules:
  0.0 40.2 jit_solution(10290582875674154964)
XLA Ops:
  0.0 0.0 copy-start.1
  0.0 1.6 %shard_map.73 = (bf16[144,512]{1,0:T(8,128)(2,1)S(1)}, bf16[144,512]{1,0:T(8,128)(2,1)S(1)}, bf16[144,512]{1,0:T(8,128)(2,1)S(1)}, bf16[144,512]{1,0:T(8,128)(2,1)S(1)}) custom-call(f32[128,2048]{1,0:T(8,128)} %bitcast.5, bf16[128,128]{1,0:T(8,128)(2,1)} %bitcast.6), custom_call_target="tpu_custom_call" | custom-call | bytes 1671168 | tf_op jit(solution)/shard_map/pallas_call | solution.py:346
  1.7 3.1 %collective-permute-start = (bf16[144,512]{1,0:T(8,128)(2,1)S(1)}, bf16[144,512]{1,0:T(8,128)(2,1)S(1)}, u32[]{:S(2)}, u32[]{:S(2)}) collective-permute-start(bf16[144,512]{1,0:T(8,128)(2,1)S(1)} %get-tuple-element.16), channel_id=1, source_target_pairs={{0,2},{2,4},{4,6},{6,0},{8,10},{10,12},{12,14},{14,8},{16,18},{18,... | collective-permute-start | bytes 442376 | tf_op jit(solution)/shard_map/ppermute | solution.py:363
  4.7 2.6 %collective-permute-start.1 = (bf16[144,512]{1,0:T(8,128)(2,1)S(1)}, bf16[144,512]{1,0:T(8,128)(2,1)S(1)}, u32[]{:S(2)}, u32[]{:S(2)}) collective-permute-start(bf16[144,512]{1,0:T(8,128)(2,1)S(1)} %get-tuple-element.17), channel_id=1, source_target_pairs={{0,4},{2,6},{4,0},{6,2},{8,12},{10,14},{12,8},{14,10},{16,20},{18,... | collective-permute-start | bytes 442376 | tf_op jit(solution)/shard_map/ppermute | solution.py:363
  7.3 1.3 %collective-permute-start.2 = (bf16[144,512]{1,0:T(8,128)(2,1)S(1)}, bf16[144,512]{1,0:T(8,128)(2,1)S(1)}, u32[]{:S(2)}, u32[]{:S(2)}) collective-permute-start(bf16[144,512]{1,0:T(8,128)(2,1)S(1)} %get-tuple-element.18), channel_id=1, source_target_pairs={{0,6},{2,0},{4,2},{6,4},{8,14},{10,8},{12,10},{14,12},{16,22},{18,... | collective-permute-start | bytes 442376 | tf_op jit(solution)/shard_map/ppermute | solution.py:363
  8.7 1.6 %shard_map.74 = (bf16[1024,512]{1,0:T(8,128)(2,1)S(1)}, bf16[512,1024]{1,0:T(8,128)(2,1)S(1)}) custom-call(bf16[144,512]{1,0:T(8,128)(2,1)S(1)} %get-tuple-element.15.after.refs_0_, bf16[1024,512]{1,0:T(8,128)(2,1)} %constant.6.clone.refs_0_, bf16[512,1024]{1,0:T(8,128)(2,1)} %constant.7.clone.refs_1_), custom_call_target="tpu_custom_call" | custom-call | bytes 4341760 | tf_op jit(solution)/shard_map/pallas_call | solution.py:346
  10.3 0.0 copy-start
  10.3 0.0 copy-start.2
  10.3 1.3 %collective-permute-done.refs_1_ = bf16[144,512]{1,0:T(8,128)(2,1)S(1)} collective-permute-done((bf16[144,512]{1,0:T(8,128)(2,1)S(1)}, bf16[144,512]{1,0:T(8,128)(2,1)S(1)}, u32[]{:S(2)}, u32[]{:S(2)}) %collective-permute-start) | collective-permute-done | bytes 147488 | tf_op jit(solution)/shard_map/ppermute | solution.py:363
  11.5 5.5 %collective-permute-done.1.refs_2_ = bf16[144,512]{1,0:T(8,128)(2,1)S(1)} collective-permute-done((bf16[144,512]{1,0:T(8,128)(2,1)S(1)}, bf16[144,512]{1,0:T(8,128)(2,1)S(1)}, u32[]{:S(2)}, u32[]{:S(2)}) %collective-permute-start.1) | collective-permute-done | bytes 147488 | tf_op jit(solution)/shard_map/ppermute | solution.py:363
  17.0 0.0 collective-permute-done.2.refs_3_
  17.0 0.1 collective-permute-start.3
  17.1 0.0 copy-done.1
  17.1 1.0 %shard_map.75.refs_9_ = f32[1024,512]{1,0:T(8,128)S(1)} custom-call(bf16[144,512]{1,0:T(8,128)(2,1)S(1)} %get-tuple-element.15.after.refs_0_, bf16[144,512]{1,0:T(8,128)(2,1)S(1)} %collective-permute-done.refs_1_, bf16[144,512]{1,0:T(8,128)(2,1)S(1)} %collective-permute-done.1.refs_2_, bf16[144,512]{1,0:T(8,128)(2,1)S(1)} %collective-permute-done.2.refs_3_, ...), custom_call_target="tpu_custom_call" | custom-call | flops 536870912 | bytes 3768320 | tf_op jit(solution)/shard_map/pallas_call | solution.py:346
  18.2 0.1 collective-permute-done.3.refs_4_
  18.3 0.0 copy-done
  18.3 0.0 copy-done.2
  18.3 3.0 %shard_map.76 = (bf16[128,512]{1,0:T(8,128)(2,1)S(1)}, bf16[128,512]{1,0:T(8,128)(2,1)S(1)}, bf16[128,512]{1,0:T(8,128)(2,1)S(1)}, bf16[128,512]{1,0:T(8,128)(2,1)S(1)}) custom-call(bf16[144,512]{1,0:T(8,128)(2,1)S(1)} %get-tuple-element.15.after.refs_0_, bf16[144,512]{1,0:T(8,128)(2,1)S(1)} %collective-permute-done.refs_1_, ...), custom_call_target="tpu_custom_call" | custom-call | flops 1073741824 | bytes 5369856 | tf_op jit(solution)/shard_map/pallas_call | solution.py:346
  21.3 1.6 %collective-permute-start.4 = (bf16[128,512]{1,0:T(8,128)(2,1)S(1)}, bf16[128,512]{1,0:T(8,128)(2,1)S(1)}, u32[]{:S(2)}, u32[]{:S(2)}) collective-permute-start(bf16[128,512]{1,0:T(8,128)(2,1)S(1)} %get-tuple-element.21), channel_id=1, source_target_pairs={{0,8},{2,10},{4,12},{6,14},{8,16},{10,18},{12,20},{14,22},{16,24},... | collective-permute-start | bytes 393224 | tf_op jit(solution)/shard_map/ppermute | solution.py:363
  22.9 4.5 %collective-permute-start.5 = (bf16[128,512]{1,0:T(8,128)(2,1)S(1)}, bf16[128,512]{1,0:T(8,128)(2,1)S(1)}, u32[]{:S(2)}, u32[]{:S(2)}) collective-permute-start(bf16[128,512]{1,0:T(8,128)(2,1)S(1)} %get-tuple-element.22), channel_id=1, source_target_pairs={{0,10},{2,12},{4,14},{6,8},{8,18},{10,20},{12,22},{14,16},{16,26},... | collective-permute-start | bytes 393224 | tf_op jit(solution)/shard_map/ppermute | solution.py:363
  27.3 2.6 %collective-permute-start.6 = (bf16[128,512]{1,0:T(8,128)(2,1)S(1)}, bf16[128,512]{1,0:T(8,128)(2,1)S(1)}, u32[]{:S(2)}, u32[]{:S(2)}) collective-permute-start(bf16[128,512]{1,0:T(8,128)(2,1)S(1)} %get-tuple-element.23), channel_id=1, source_target_pairs={{0,12},{2,14},{4,8},{6,10},{8,20},{10,22},{12,16},{14,18},{16,28},... | collective-permute-start | bytes 393224 | tf_op jit(solution)/shard_map/ppermute | solution.py:363
  30.0 0.7 %collective-permute-start.7 = (bf16[128,512]{1,0:T(8,128)(2,1)S(1)}, bf16[128,512]{1,0:T(8,128)(2,1)S(1)}, u32[]{:S(2)}, u32[]{:S(2)}) collective-permute-start(bf16[128,512]{1,0:T(8,128)(2,1)S(1)} %get-tuple-element.24), channel_id=1, source_target_pairs={{0,14},{2,8},{4,10},{6,12},{8,22},{10,16},{12,18},{14,20},{16,30},... | collective-permute-start | bytes 393224 | tf_op jit(solution)/shard_map/ppermute | solution.py:363
  30.6 0.0 collective-permute-done.4.refs_0_
  30.6 2.2 %collective-permute-done.5.refs_1_ = bf16[128,512]{1,0:T(8,128)(2,1)S(1)} collective-permute-done((bf16[128,512]{1,0:T(8,128)(2,1)S(1)}, bf16[128,512]{1,0:T(8,128)(2,1)S(1)}, u32[]{:S(2)}, u32[]{:S(2)}) %collective-permute-start.5) | collective-permute-done | bytes 131104 | tf_op jit(solution)/shard_map/ppermute | solution.py:363
  32.8 5.1 %collective-permute-done.6.refs_2_ = bf16[128,512]{1,0:T(8,128)(2,1)S(1)} collective-permute-done((bf16[128,512]{1,0:T(8,128)(2,1)S(1)}, bf16[128,512]{1,0:T(8,128)(2,1)S(1)}, u32[]{:S(2)}, u32[]{:S(2)}) %collective-permute-start.6) | collective-permute-done | bytes 131104 | tf_op jit(solution)/shard_map/ppermute | solution.py:363
  38.0 1.3 %collective-permute-done.7.refs_3_ = bf16[128,512]{1,0:T(8,128)(2,1)S(1)} collective-permute-done((bf16[128,512]{1,0:T(8,128)(2,1)S(1)}, bf16[128,512]{1,0:T(8,128)(2,1)S(1)}, u32[]{:S(2)}, u32[]{:S(2)}) %collective-permute-start.7) | collective-permute-done | bytes 131104 | tf_op jit(solution)/shard_map/ppermute | solution.py:363
  39.2 1.0 %shard_map.77 = f32[128,2048]{1,0:T(8,128)} custom-call(bf16[128,512]{1,0:T(8,128)(2,1)S(1)} %collective-permute-done.4.refs_0_, bf16[128,512]{1,0:T(8,128)(2,1)S(1)} %collective-permute-done.5.refs_1_, bf16[128,512]{1,0:T(8,128)(2,1)S(1)} %collective-permute-done.6.refs_2_, bf16[128,512]{1,0:T(8,128)(2,1)S(1)} %collective-permute-done.7.refs_3_), custom_call_target="tpu_custom_call" | custom-call | bytes 1572864 | tf_op jit(solution)/shard_map/pallas_call | solution.py:346
  (5 shorter events, 0.0 us)
Async XLA Ops:
  0.0 17.1 %copy-start.1 = (bf16[32,512]{1,0:T(8,128)(2,1)S(1)}, bf16[32,512]{1,0:T(8,128)(2,1)}, u32[]{:S(2)}) copy-start(bf16[32,512]{1,0:T(8,128)(2,1)} %constant.8.clone.refs_5_) | copy-start | bytes 98308
  1.7 9.9 %collective-permute-start = (bf16[144,512]{1,0:T(8,128)(2,1)S(1)}, bf16[144,512]{1,0:T(8,128)(2,1)S(1)}, u32[]{:S(2)}, u32[]{:S(2)}) collective-permute-start(bf16[144,512]{1,0:T(8,128)(2,1)S(1)} %get-tuple-element.16), channel_id=1, source_target_pairs={{0,2},{2,4},{4,6},{6,0},{8,10},{10,12},{12,14},{14,8},{16,18},{18,... | collective-permute-start | bytes 442376 | tf_op jit(solution)/shard_map/ppermute | solution.py:363
  4.7 12.3 %collective-permute-start.1 = (bf16[144,512]{1,0:T(8,128)(2,1)S(1)}, bf16[144,512]{1,0:T(8,128)(2,1)S(1)}, u32[]{:S(2)}, u32[]{:S(2)}) collective-permute-start(bf16[144,512]{1,0:T(8,128)(2,1)S(1)} %get-tuple-element.17), channel_id=1, source_target_pairs={{0,4},{2,6},{4,0},{6,2},{8,12},{10,14},{12,8},{14,10},{16,20},{18,... | collective-permute-start | bytes 442376 | tf_op jit(solution)/shard_map/ppermute | solution.py:363
  7.3 9.7 %collective-permute-start.2 = (bf16[144,512]{1,0:T(8,128)(2,1)S(1)}, bf16[144,512]{1,0:T(8,128)(2,1)S(1)}, u32[]{:S(2)}, u32[]{:S(2)}) collective-permute-start(bf16[144,512]{1,0:T(8,128)(2,1)S(1)} %get-tuple-element.18), channel_id=1, source_target_pairs={{0,6},{2,0},{4,2},{6,4},{8,14},{10,8},{12,10},{14,12},{16,22},{18,... | collective-permute-start | bytes 442376 | tf_op jit(solution)/shard_map/ppermute | solution.py:363
  10.3 8.0 %copy-start = (bf16[1,3,3,2048]{3,2,1,0:T(4,128)(2,1)S(1)}, bf16[1,3,3,2048]{3,2,1,0:T(4,128)(2,1)}, u32[]{:S(2)}) copy-start(bf16[1,3,3,2048]{3,2,1,0:T(4,128)(2,1)} %param.9) | copy-start | bytes 110596
  10.3 8.0 %copy-start.2 = (f32[1,2048]{1,0:T(1,128)S(1)}, f32[1,2048]{1,0:T(1,128)}, u32[]{:S(2)}) copy-start(f32[1,2048]{1,0:T(1,128)} %refs_6_.1) | copy-start | bytes 24580
  17.0 1.2 %collective-permute-start.3 = (bf16[64,128]{1,0:T(8,128)(2,1)S(1)}, bf16[64,128]{1,0:T(8,128)(2,1)S(1)}, u32[]{:S(2)}, u32[]{:S(2)}) collective-permute-start(bf16[64,128]{1,0:T(8,128)(2,1)S(1)} %pad_maximum_fusion), channel_id=1, source_target_pairs={{0,1},{1,0},{2,3},{3,2},{4,5},{5,4},{6,7},{7,6},{8,9},{9,8},{10,11... | collective-permute-start | bytes 49160 | tf_op jit(solution)/shard_map/ppermute | solution.py:399
  21.3 9.3 %collective-permute-start.4 = (bf16[128,512]{1,0:T(8,128)(2,1)S(1)}, bf16[128,512]{1,0:T(8,128)(2,1)S(1)}, u32[]{:S(2)}, u32[]{:S(2)}) collective-permute-start(bf16[128,512]{1,0:T(8,128)(2,1)S(1)} %get-tuple-element.21), channel_id=1, source_target_pairs={{0,8},{2,10},{4,12},{6,14},{8,16},{10,18},{12,20},{14,22},{16,24},... | collective-permute-start | bytes 393224 | tf_op jit(solution)/shard_map/ppermute | solution.py:363
  22.9 9.9 %collective-permute-start.5 = (bf16[128,512]{1,0:T(8,128)(2,1)S(1)}, bf16[128,512]{1,0:T(8,128)(2,1)S(1)}, u32[]{:S(2)}, u32[]{:S(2)}) collective-permute-start(bf16[128,512]{1,0:T(8,128)(2,1)S(1)} %get-tuple-element.22), channel_id=1, source_target_pairs={{0,10},{2,12},{4,14},{6,8},{8,18},{10,20},{12,22},{14,16},{16,26},... | collective-permute-start | bytes 393224 | tf_op jit(solution)/shard_map/ppermute | solution.py:363
  27.3 10.6 %collective-permute-start.6 = (bf16[128,512]{1,0:T(8,128)(2,1)S(1)}, bf16[128,512]{1,0:T(8,128)(2,1)S(1)}, u32[]{:S(2)}, u32[]{:S(2)}) collective-permute-start(bf16[128,512]{1,0:T(8,128)(2,1)S(1)} %get-tuple-element.23), channel_id=1, source_target_pairs={{0,12},{2,14},{4,8},{6,10},{8,20},{10,22},{12,16},{14,18},{16,28},... | collective-permute-start | bytes 393224 | tf_op jit(solution)/shard_map/ppermute | solution.py:363
  30.0 9.3 %collective-permute-start.7 = (bf16[128,512]{1,0:T(8,128)(2,1)S(1)}, bf16[128,512]{1,0:T(8,128)(2,1)S(1)}, u32[]{:S(2)}, u32[]{:S(2)}) collective-permute-start(bf16[128,512]{1,0:T(8,128)(2,1)S(1)} %get-tuple-element.24), channel_id=1, source_target_pairs={{0,14},{2,8},{4,10},{6,12},{8,22},{10,16},{12,18},{14,20},{16,30},... | collective-permute-start | bytes 393224 | tf_op jit(solution)/shard_map/ppermute | solution.py:363

commit v3 on v2

--- a/solution.py
+++ b/solution.py
@@ -169,13 +169,17 @@
 
 EXTRA = 16
 LANES = 128
+DEPTH = 64
 
 
 def odd_tables(length):
-    phase = (2 * np.arange(length)[:, None] + 1) * np.arange(length)[None, :] % (4 * length)
-    turn = phase * (2.0 * np.pi / (4 * length))
-    ahead = np.concatenate([np.cos(turn), -np.sin(turn)], axis=0)
-    return ahead.astype(ml_dtypes.bfloat16), (ahead.T / length).astype(ml_dtypes.bfloat16)
+    ahead, back = [], []
+    for first in range(2):
+        phase = (2 * np.arange(length // 2)[:, None] + 1) * np.arange(first, length, 2)[None, :] % (4 * length)
+        turn = phase * (2.0 * np.pi / (4 * length))
+        ahead.append(np.concatenate([np.cos(turn), -np.sin(turn)], axis=0))
+        back.append(ahead[-1].T / length)
+    return [np.concatenate(parts, axis=0).astype(ml_dtypes.bfloat16) for parts in (ahead, back)]
 
 
 def spread_table(filters, channels):
@@ -200,49 +204,48 @@
 
 
 def cut_kernel(peers, x_hbm, filt_hbm, *refs):
-    outs, (x_ref, filt_ref, turned, sems) = refs[:peers], refs[peers:]
+    outs, (x_ref, filt_ref, plain, turned, sems) = refs[:peers], refs[peers:]
     rank = lax.axis_index("ctx")
     rows, chans = x_hbm.shape
-    width = chans // peers
+    part, width = rows // 2, chans // peers
     filters = filt_hbm.shape[1] // peers
-    pieces = sems.shape[0] - 1
-    depth = rows // pieces
-    copies = [
-        pltpu.make_async_copy(
-            x_hbm.at[pl.ds(i * depth, depth)], x_ref.at[pl.ds(i * depth, depth)], sems.at[i]
-        )
-        for i in range(pieces)
-    ]
-    copies.append(pltpu.make_async_copy(filt_hbm, filt_ref, sems.at[pieces]))
+    tiles = width // LANES
+    copies = [pltpu.make_async_copy(filt_hbm, filt_ref, sems.at[peers * tiles])]
+    for step in range(peers):
+        begin = next_place(rank, step, peers) * width
+        for tile in range(tiles):
+            lanes = pl.ds(pl.multiple_of(begin + tile * LANES, LANES), LANES)
+            at = step * tiles + tile
+            copies.append(pltpu.make_async_copy(x_hbm.at[:, lanes], x_ref.at[at], sems.at[at]))
     for copy in copies:
         copy.start()
-    columns = []
-    for i in range(pieces):
-        copies[i].wait()
-        here = pl.ds(i * depth, depth)
-        total = jnp.zeros((depth, LANES), jnp.float32)
-        for step in range(peers):
-            target = next_place(rank, step, peers)
-            part = x_ref[here, pl.ds(pl.multiple_of(target * width, width), width)]
-            outs[step][here, :] = part.astype(jnp.bfloat16)
-            for first in range(0, width, LANES):
-                total = total + part[:, first : first + LANES] * part[:, first : first + LANES]
-        columns.append(jnp.sum(total, axis=1, keepdims=True))
-    column = jnp.concatenate(columns, axis=0)
+    copies[0].wait()
+    for at in range(plain.shape[0]):
+        lanes = slice(at * LANES, (at + 1) * LANES)
+        plain[at] = filt_ref[:, lanes].astype(jnp.float32)
+        halves = [plain[at, pl.ds(odd, part, stride=2), :] for odd in range(2)]
+        turned[lanes, :] = jnp.transpose(jnp.concatenate(halves, axis=0)).astype(jnp.bfloat16)
+    base = tiles * rows
+    for step in range(peers):
+        own = pl.ds(pl.multiple_of(next_place(rank, step, peers) * filters, filters), filters)
+        outs[step][base : base + filters, :] = turned[own, :]
+    totals = [jnp.zeros((part, LANES), jnp.float32)] * 2
+    for step in range(peers):
+        for tile in range(tiles):
+            at = step * tiles + tile
+            copies[1 + at].wait()
+            for odd in range(2):
+                acts = x_ref[at, pl.ds(odd, part, stride=2), :]
+                top = tile * rows + odd * part
+                outs[step][top : top + part, :] = acts.astype(jnp.bfloat16)
+                totals[odd] = totals[odd] + acts * acts
+    column = jnp.sum(jnp.concatenate(totals, axis=0), axis=1, keepdims=True)
     row = jnp.transpose(jnp.broadcast_to(column, (rows, LANES)))[:EXTRA, :]
     nth = lax.broadcasted_iota(jnp.int32, (EXTRA, rows), 0)
     terms = three_terms(row)
     sums = jnp.where(nth == 0, terms[0], jnp.where(nth == 1, terms[1], jnp.where(nth == 2, terms[2], 0.0)))
-    sums = sums.astype(jnp.bfloat16)
-    copies[pieces].wait()
-    turned[...] = jnp.transpose(filt_ref[...].astype(jnp.float32)).astype(jnp.bfloat16)
-    for step in range(peers):
-        target = next_place(rank, step, peers)
-        own = turned[pl.ds(pl.multiple_of(target * filters, filters), filters), :]
-        extra = [sums] + [own[first : first + EXTRA] for first in range(0, filters, EXTRA)]
-        if width > rows * len(extra):
-            extra.append(jnp.zeros((EXTRA, width - rows * len(extra)), jnp.bfloat16))
-        outs[step][rows:, :] = jnp.concatenate(extra, axis=1)
+    for step in range(peers):
+        outs[step][base + filters :, :] = sums.astype(jnp.bfloat16)
 
 
 def table_kernel(pieces, after, *refs):
@@ -262,20 +265,30 @@
 
 def filter_kernel(peers, *refs):
     blocks = refs[:peers]
-    ahead_ref, spread_ref, filt_spec, spread_filter = refs[peers:]
+    ahead_ref, spread_ref, filt_spec, even, odd = refs[peers:]
     rank = lax.axis_index("ctx")
-    rows = blocks[0].shape[0] - EXTRA
-    filters = spread_ref.shape[0]
-    for step in range(peers):
-        begin = pl.multiple_of(next_place(rank, -step, peers) * rows, rows)
-        parts = [blocks[step][rows:, i * rows : (i + 1) * rows] for i in range(1, 1 + filters // EXTRA)]
-        spread_filter[pl.ds(begin, rows), :] = lax.dot_general(
-            jnp.concatenate(parts, axis=0),
+    filters, width = spread_ref.shape
+    rows = blocks[0].shape[1]
+    part = rows // 2
+    half = part * peers
+    base = width // LANES * rows
+    for step in range(peers):
+        here = pl.ds(pl.multiple_of(next_place(rank, -step, peers) * part, part), part)
+        spread = lax.dot_general(
+            blocks[step][base : base + filters, :],
             spread_ref[...],
             (((0,), (0,)), ((), ())),
             preferred_element_type=jnp.float32,
         ).astype(jnp.bfloat16)
-    filt_spec[...] = jnp.dot(ahead_ref[...], spread_filter[...], preferred_element_type=jnp.float32)
+        even[here, :] = spread[:part]
+        odd[here, :] = spread[part:]
+    for im in range(2):
+        here = slice(im * half, (im + 1) * half)
+        there = slice((im + 2) * half, (im + 3) * half)
+        of_even = jnp.dot(ahead_ref[here, :], even[...], preferred_element_type=jnp.float32)
+        of_odd = jnp.dot(ahead_ref[there, :], odd[...], preferred_element_type=jnp.float32)
+        filt_spec[here, :] = of_even + of_odd
+        filt_spec[there, :] = of_odd - of_even if im else of_even - of_odd
 
 
 def layer_kernel(peers, *refs):
@@ -284,61 +297,98 @@
     outs = refs[peers + 6 : 2 * peers + 6]
     held, query, product, spec, weighted, conv = refs[2 * peers + 6 :]
     rank = lax.axis_index("ctx")
-    rows = blocks[0].shape[0] - EXTRA
-    width = blocks[0].shape[1]
-    half = rows * peers
+    rows, width = outs[0].shape
+    part, half = rows // 2, rows * peers // 2
+    base = blocks[0].shape[0] - EXTRA
     chans = pl.ds(pl.multiple_of(rank * width, width), width)
-    held[:8, :] = jnp.zeros((8, width), jnp.float32)
-    for step in range(peers):
-        begin = pl.multiple_of(next_place(rank, -step, peers) * rows, rows)
-        here = blocks[step][rows:, :rows].astype(jnp.float32)
+    taps = [[taps_ref[f, i : i + 1, chans].astype(jnp.float32) for i in range(TAPS)] for f in range(3)]
+    skip = skip_ref[:, chans]
+    held[:, :8, :] = jnp.zeros((2, 8, width), jnp.float32)
+    for step in range(peers):
+        here = blocks[step][base:, :].astype(jnp.float32)
         there = other_sums[step * EXTRA : (step + 1) * EXTRA, :].astype(jnp.float32)
         square = jnp.sum(here, axis=0, keepdims=True) + jnp.sum(there, axis=0, keepdims=True)
         scale = column_of(lax.rsqrt(square * (1.0 / CHAN) + 1e-06))
-        for first in range(0, width, LANES):
-            lanes = slice(first, first + LANES)
-            held[pl.ds(begin + 8, rows), lanes] = blocks[step][:rows, lanes].astype(jnp.float32) * scale
-    taps = [[taps_ref[f, i : i + 1, chans].astype(jnp.float32) for i in range(TAPS)] for f in range(3)]
-    for block in range(peers):
-        begin = block * rows
-        moved = [held[pl.ds(begin + 8 - i, rows), :] for i in range(TAPS)]
-        features = []
-        for feature in range(3):
-            running = taps[feature][0] * moved[0]
-            for i in range(1, TAPS):
-                running = running + taps[feature][i] * moved[i]
-            features.append(running)
-        query[pl.ds(begin, rows), :] = features[0].astype(jnp.bfloat16)
-        product[pl.ds(begin, rows), :] = (features[1] * features[2]).astype(jnp.bfloat16)
-    spec[...] = jnp.dot(ahead_ref[...], product[...], preferred_element_type=jnp.float32)
-    sig_re, sig_im = spec[:half, :], spec[half:, :]
-    gain_re, gain_im = filt_spec[:half, :], filt_spec[half:, :]
-    weighted[:half, :] = (sig_re * gain_re - sig_im * gain_im).astype(jnp.bfloat16)
-    weighted[half:, :] = (sig_re * gain_im + sig_im * gain_re).astype(jnp.bfloat16)
-    conv[...] = jnp.dot(return_ref[...], weighted[...], preferred_element_type=jnp.float32)
-    skip = skip_ref[:, chans]
-    for step in range(peers):
-        tokens = pl.ds(pl.multiple_of(next_place(rank, step, peers) * rows, rows), rows)
-        acts = blocks[(peers - step) % peers][:rows, :].astype(jnp.float32)
-        gated = conv[tokens, :] + skip * product[tokens, :].astype(jnp.float32)
-        outs[step][...] = (acts + query[tokens, :].astype(jnp.float32) * gated).astype(jnp.bfloat16)
-
-
-def join_kernel(peers, *refs):
-    parts, out_hbm, wide, sems = refs[:peers], refs[peers], refs[peers + 1], refs[peers + 2]
-    width = parts[0].shape[1]
+        begin = pl.multiple_of(next_place(rank, -step, peers) * part, part) + 8
+        for tile in range(width // LANES):
+            lanes = slice(tile * LANES, (tile + 1) * LANES)
+            for odd in range(2):
+                acts = blocks[step][tile * rows + odd * part : tile * rows + (odd + 1) * part, :]
+                scaled = acts.astype(jnp.float32) * scale[odd * part : (odd + 1) * part]
+                held[odd, pl.ds(pl.multiple_of(begin, 8), part), lanes] = scaled
+    for first in range(0, width, LANES):
+        lanes = slice(first, first + LANES)
+        near = [[jnp.broadcast_to(tap[:, lanes], (DEPTH, LANES)) for tap in feature] for feature in taps]
+        for top in range(0, half, DEPTH):
+            now = [held[odd, 8 + top : 8 + top + DEPTH, lanes] for odd in range(2)]
+            last = [held[odd, 7 + top : 7 + top + DEPTH, lanes] for odd in range(2)]
+            for odd, moved in ((0, (now[0], last[1], last[0])), (1, (now[1], now[0], last[1]))):
+                features = []
+                for feature in near:
+                    running = feature[0] * moved[0]
+                    for i in range(1, TAPS):
+                        running = running + feature[i] * moved[i]
+                    features.append(running)
+                query[odd, top : top + DEPTH, lanes] = features[0].astype(jnp.bfloat16)
+                product[odd, top : top + DEPTH, lanes] = (features[1] * features[2]).astype(jnp.bfloat16)
+    for odd in range(2):
+        table = ahead_ref[2 * odd * half : 2 * (odd + 1) * half, :]
+        spec[odd] = jnp.dot(table, product[odd], preferred_element_type=jnp.float32)
+    for first in range(0, width, LANES):
+        lanes = slice(first, first + LANES)
+        for top in range(0, half, DEPTH):
+            re, im = slice(top, top + DEPTH), slice(half + top, half + top + DEPTH)
+            far_re, far_im = (slice(2 * half + at.start, 2 * half + at.stop) for at in (re, im))
+            even_re, even_im = spec[0, re, lanes], spec[0, im, lanes]
+            odd_re, odd_im = spec[1, re, lanes], spec[1, im, lanes]
+            near_out = product_of(even_re + odd_re, even_im + odd_im, filt_spec[re, lanes], filt_spec[im, lanes])
+            far_out = product_of(
+                even_re - odd_re, odd_im - even_im, filt_spec[far_re, lanes], filt_spec[far_im, lanes]
+            )
+            weighted[0, re, lanes] = (near_out[0] + far_out[0]).astype(jnp.bfloat16)
+            weighted[0, im, lanes] = (near_out[1] - far_out[1]).astype(jnp.bfloat16)
+            weighted[1, re, lanes] = (near_out[0] - far_out[0]).astype(jnp.bfloat16)
+            weighted[1, im, lanes] = (near_out[1] + far_out[1]).astype(jnp.bfloat16)
+    for odd in range(2):
+        table = return_ref[odd * half : (odd + 1) * half, :]
+        conv[odd] = jnp.dot(table, weighted[odd], preferred_element_type=jnp.float32)
+    for step in range(peers):
+        tokens = pl.ds(pl.multiple_of(next_place(rank, step, peers) * part, part), part)
+        for tile in range(width // LANES):
+            lanes = slice(tile * LANES, (tile + 1) * LANES)
+            for odd in range(2):
+                own = tile * rows + odd * part
+                acts = blocks[(peers - step) % peers][own : own + part, :].astype(jnp.float32)
+                gated = conv[odd, tokens, lanes] + skip[:, lanes] * product[odd, tokens, lanes].astype(jnp.float32)
+                finished = acts + query[odd, tokens, lanes].astype(jnp.float32) * gated
+                outs[step][odd * part : (odd + 1) * part, lanes] = finished.astype(jnp.bfloat16)
+
+
+def product_of(left_re, left_im, right_re, right_im):
+    return left_re * right_re - left_im * right_im, left_re * right_im + left_im * right_re
+
+
+def join_kernel(peers, steps, *refs):
+    parts, (out_hbm, wide, sems) = refs[: len(steps)], refs[-3:]
+    rows, width = parts[0].shape
     rank = lax.axis_index("ctx")
+    tiles = width // LANES
     copies = []
-    for step in range(peers):
-        wide[step, :, :] = parts[step][...].astype(jnp.float32)
-        chans = pl.ds(pl.multiple_of(next_place(rank, -step, peers) * width, width), width)
-        copies.append(pltpu.make_async_copy(wide.at[step], out_hbm.at[:, chans], sems.at[step]))
-        copies[-1].start()
+    for i, step in enumerate(steps):
+        begin = next_place(rank, -step, peers) * width
+        for tile in range(tiles):
+            at = i * tiles + tile
+            for odd in range(2):
+                part = parts[i][odd * (rows // 2) : (odd + 1) * (rows // 2), tile * LANES : (tile + 1) * LANES]
+                wide[at, pl.ds(odd, rows // 2, stride=2), :] = part.astype(jnp.float32)
+            lanes = pl.ds(pl.multiple_of(begin + tile * LANES, LANES), LANES)
+            copies.append(pltpu.make_async_copy(wide.at[at], out_hbm.at[:, lanes], sems.at[at]))
+            copies[-1].start()
     for copy in copies:
         copy.wait()
 
 
-def on_device(kernel, args, outs, scratch=(), in_hbm=(), out_hbm=False, flops=0, limit=32):
+def on_device(kernel, args, outs, scratch=(), in_hbm=(), out_hbm=False, flops=0, limit=32, aliases=None):
     whole = pl.BlockSpec(memory_space=pltpu.VMEM)
     far = pl.BlockSpec(memory_space=pltpu.HBM)
     touched = sum(a.size * a.dtype.itemsize for a in (*args, *outs))
@@ -349,6 +399,7 @@
         in_specs=[far if i in in_hbm else whole for i in range(len(args))],
         out_specs=[far if out_hbm else whole] * len(outs),
         scratch_shapes=list(scratch),
+        input_output_aliases=aliases or {},
         compiler_params=pltpu.CompilerParams(vmem_limit_bytes=limit * 2**20),
         cost_estimate=pl.CostEstimate(flops=flops, bytes_accessed=touched, transcendentals=0),
     )(*args)
@@ -368,18 +419,21 @@
     rows, chans = acts.shape
     sections, peers = lax.axis_size("section"), lax.axis_size("ctx")
     width, filters = chans // peers, long_filter.shape[2] // peers
-    half = rows * peers
+    length = rows * peers
+    half = length // 2
     bf16, f32 = jnp.bfloat16, jnp.float32
     pieces = 4
+    base = width // LANES * rows + filters
     sent = on_device(
         functools.partial(cut_kernel, peers),
         [acts, long_filter[0]],
-        [jax.ShapeDtypeStruct((rows + EXTRA, width), bf16)] * peers,
+        [jax.ShapeDtypeStruct((base + EXTRA, rows), bf16)] * peers,
         [
-            pltpu.VMEM((rows, chans), f32),
+            pltpu.VMEM((chans // LANES, rows, LANES), f32),
             pltpu.VMEM(long_filter.shape[1:], bf16),
+            pltpu.VMEM((long_filter.shape[2] // LANES, rows, LANES), f32),
             pltpu.VMEM((long_filter.shape[2], rows), bf16),
-            pltpu.SemaphoreType.DMA((pieces + 1,)),
+            pltpu.SemaphoreType.DMA((chans // LANES + 1,)),
         ],
         in_hbm=(0, 1),
     )
@@ -387,7 +441,7 @@
     far_first = sorted(range(1, peers), key=lambda k: abs(2 * k - peers))
     for k in far_first:
         got[k] = hop(sent[k], sections, peers, 0, k)
-    tables = [jnp.asarray(t) for t in odd_tables(half)]
+    tables = [jnp.asarray(t) for t in odd_tables(length)]
     ahead, back = on_device(
         functools.partial(table_kernel, pieces),
         [sent[0], *tables],
@@ -395,38 +449,53 @@
         [pltpu.SemaphoreType.DMA((2 * pieces,))],
         in_hbm=(1, 2),
     )
-    own_sums = jnp.concatenate([g[rows:, :rows] for g in got], axis=0)
+    own_sums = jnp.concatenate([g[base:] for g in got], axis=0)
     other_sums = lax.ppermute(own_sums, "tp", [(0, 1), (1, 0)])
     (filt_spec,) = on_device(
         functools.partial(filter_kernel, peers),
         [*got, ahead, jnp.asarray(spread_table(filters, width))],
-        [jax.ShapeDtypeStruct((2 * half, width), f32)],
-        [pltpu.VMEM((half, width), bf16)],
-        flops=4 * half * half * width,
+        [jax.ShapeDtypeStruct((2 * length, width), f32)],
+        [pltpu.VMEM((half, width), bf16)] * 2,
+        flops=2 * length * length * width,
     )
     done = on_device(
         functools.partial(layer_kernel, peers),
         [*got, other_sums, short_filter[0], skip_gain, ahead, back, filt_spec],
         [jax.ShapeDtypeStruct((rows, width), bf16)] * peers,
         [
-            pltpu.VMEM((half + 8, width), f32),
-            pltpu.VMEM((half, width), bf16),
-            pltpu.VMEM((half, width), bf16),
-            pltpu.VMEM((2 * half, width), f32),
-            pltpu.VMEM((2 * half, width), bf16),
-            pltpu.VMEM((half, width), f32),
+            pltpu.VMEM((2, half + 8, width), f32),
+            pltpu.VMEM((2, half, width), bf16),
+            pltpu.VMEM((2, half, width), bf16),
+            pltpu.VMEM((2, length, width), f32),
+            pltpu.VMEM((2, length, width), bf16),
+            pltpu.VMEM((2, half, width), f32),
         ],
-        flops=8 * half * half * width,
+        flops=4 * length * length * width,
     )
     arrived = [None] * peers
     for k in [*far_first, 0]:
         arrived[k] = hop(done[k], sections, peers, 1, k)
+    out = jax.ShapeDtypeStruct((rows, chans), f32)
+    tiles = width // LANES
+
+    def staging(count):
+        return [pltpu.VMEM((count * tiles, rows, LANES), f32), pltpu.SemaphoreType.DMA((count * tiles,))]
+
     (received,) = on_device(
-        functools.partial(join_kernel, peers),
-        arrived,
-        [jax.ShapeDtypeStruct((rows, chans), f32)],
-        [pltpu.VMEM((peers, rows, width), f32), pltpu.SemaphoreType.DMA((peers,))],
+        functools.partial(join_kernel, peers, far_first),
+        [arrived[k] for k in far_first],
+        [out],
+        staging(len(far_first)),
         out_hbm=True,
+    )
+    (received,) = on_device(
+        functools.partial(join_kernel, peers, [0]),
+        [arrived[0], received],
+        [out],
+        staging(1),
+        in_hbm=(1,),
+        out_hbm=True,
+        aliases={1: 0},
     )
     return received[None]
 
@@ -441,7 +510,7 @@
         and tokens <= 1024
         and width % LANES == 0
         and filters % EXTRA == 0
-        and (1 + filters // EXTRA) * LANES <= width
+        and long_filter.shape[2] // cores % LANES == 0
     )
 
 

time: 40.4 us -> 40.8 us (level)
    pallas_call x5 -> x6, Pallas kernels: 8.24 us -> 8.03 us  [on_device(): pl.pallas_call(kernel, out_shape=outs, in_specs=[far if i in in_hbm else...]
  transfers between devices with their start and end apart: 8 -> 8, of which waited for: 6 -> 6; matrix products, arithmetic and copies ran while one was open for 0% -> 0% of each run, Pallas kernels for 6% -> 8%
where the time goes in v3:
time: 40.8 us; the launch traced here: 40.6 us
  starting transfers between devices  16.7 us (41%)
  waiting for transfers between devices  15.8 us (39%)
  Pallas kernels  8.03 us (20%)
    ppermute x7, starting transfers between devices, hop(): return lax.ppermute(x, ('section', 'ctx'), route)  16.6 us
    ppermute x7, waiting for transfers between devices, hop(): return lax.ppermute(x, ('section', 'ctx'), route)  15.4 us
    pallas_call x6, Pallas kernels, on_device(): pl.pallas_call(kernel, out_shape=outs, in_specs=[far if i in in_hbm else...  8.03 us
  transfers between devices with their start and end apart: 8, of which 6 were waited for; matrix products, arithmetic and copies ran while one was open for 0% of the time, Pallas kernels for 8%

profile of v3, /device:TPU:0, one launch (start us, length us, event | category | flops | bytes accessed | tf_op | source)
XLA Modules:
  0.0 40.6 jit_solution(10586043537768550571)
XLA Ops:
  0.0 0.0 copy-start.1
  0.0 1.6 %shard_map.73 = (bf16[560,128]{1,0:T(8,128)(2,1)S(1)}, bf16[560,128]{1,0:T(8,128)(2,1)S(1)}, bf16[560,128]{1,0:T(8,128)(2,1)S(1)}, bf16[560,128]{1,0:T(8,128)(2,1)S(1)}) custom-call(f32[128,2048]{1,0:T(8,128)} %bitcast.5, bf16[128,128]{1,0:T(8,128)(2,1)} %bitcast.6), custom_call_target="tpu_custom_call" | custom-call | bytes 1654784 | tf_op jit(solution)/shard_map/pallas_call | solution.py:396
  1.6 3.1 %collective-permute-start = (bf16[560,128]{1,0:T(8,128)(2,1)S(1)}, bf16[560,128]{1,0:T(8,128)(2,1)S(1)}, u32[]{:S(2)}, u32[]{:S(2)}) collective-permute-start(bf16[560,128]{1,0:T(8,128)(2,1)S(1)} %get-tuple-element.16), channel_id=1, source_target_pairs={{0,2},{2,4},{4,6},{6,0},{8,10},{10,12},{12,14},{14,8},{16,18},{18,... | collective-permute-start | bytes 430088 | tf_op jit(solution)/shard_map/ppermute | solution.py:414
  4.7 2.6 %collective-permute-start.1 = (bf16[560,128]{1,0:T(8,128)(2,1)S(1)}, bf16[560,128]{1,0:T(8,128)(2,1)S(1)}, u32[]{:S(2)}, u32[]{:S(2)}) collective-permute-start(bf16[560,128]{1,0:T(8,128)(2,1)S(1)} %get-tuple-element.17), channel_id=1, source_target_pairs={{0,4},{2,6},{4,0},{6,2},{8,12},{10,14},{12,8},{14,10},{16,20},{18,... | collective-permute-start | bytes 430088 | tf_op jit(solution)/shard_map/ppermute | solution.py:414
  7.2 1.3 %collective-permute-start.2 = (bf16[560,128]{1,0:T(8,128)(2,1)S(1)}, bf16[560,128]{1,0:T(8,128)(2,1)S(1)}, u32[]{:S(2)}, u32[]{:S(2)}) collective-permute-start(bf16[560,128]{1,0:T(8,128)(2,1)S(1)} %get-tuple-element.18), channel_id=1, source_target_pairs={{0,6},{2,0},{4,2},{6,4},{8,14},{10,8},{12,10},{14,12},{16,22},{18,... | collective-permute-start | bytes 430088 | tf_op jit(solution)/shard_map/ppermute | solution.py:414
  8.6 0.0 copy-start
  8.6 0.0 copy-start.2
  8.6 1.4 %shard_map.74 = (bf16[1024,256]{1,0:T(8,128)(2,1)S(1)}, bf16[512,512]{1,0:T(8,128)(2,1)S(1)}) custom-call(bf16[560,128]{1,0:T(8,128)(2,1)S(1)} %get-tuple-element.15.after.refs_0_, bf16[1024,256]{1,0:T(8,128)(2,1)} %constant.6.clone.refs_0_, bf16[512,512]{1,0:T(8,128)(2,1)} %constant.7.clone.refs_1_), custom_call_target="tpu_custom_call" | custom-call | bytes 2240512 | tf_op jit(solution)/shard_map/pallas_call | solution.py:396
  10.0 1.4 %collective-permute-done.refs_1_ = bf16[560,128]{1,0:T(8,128)(2,1)S(1)} collective-permute-done((bf16[560,128]{1,0:T(8,128)(2,1)S(1)}, bf16[560,128]{1,0:T(8,128)(2,1)S(1)}, u32[]{:S(2)}, u32[]{:S(2)}) %collective-permute-start) | collective-permute-done | bytes 143392 | tf_op jit(solution)/shard_map/ppermute | solution.py:414
  11.4 5.3 %collective-permute-done.1.refs_2_ = bf16[560,128]{1,0:T(8,128)(2,1)S(1)} collective-permute-done((bf16[560,128]{1,0:T(8,128)(2,1)S(1)}, bf16[560,128]{1,0:T(8,128)(2,1)S(1)}, u32[]{:S(2)}, u32[]{:S(2)}) %collective-permute-start.1) | collective-permute-done | bytes 143392 | tf_op jit(solution)/shard_map/ppermute | solution.py:414
  16.7 0.0 collective-permute-done.2.refs_3_
  16.7 0.1 collective-permute-start.3
  16.8 0.0 copy-done.1
  16.8 0.8 %shard_map.75.refs_9_ = f32[1024,512]{1,0:T(8,128)S(1)} custom-call(bf16[560,128]{1,0:T(8,128)(2,1)S(1)} %get-tuple-element.15.after.refs_0_, bf16[560,128]{1,0:T(8,128)(2,1)S(1)} %collective-permute-done.refs_1_, bf16[560,128]{1,0:T(8,128)(2,1)S(1)} %collective-permute-done.1.refs_2_, bf16[560,128]{1,0:T(8,128)(2,1)S(1)} %collective-permute-done.2.refs_3_, ...), custom_call_target="tpu_custom_call" | custom-call | flops 268435456 | bytes 3227648 | tf_op jit(solution)/shard_map/pallas_call | solution.py:396
  17.5 0.4 collective-permute-done.3.refs_4_
  17.9 0.0 copy-done
  18.0 0.0 copy-done.2
  18.0 2.6 %shard_map.76 = (bf16[128,512]{1,0:T(8,128)(2,1)S(1)}, bf16[128,512]{1,0:T(8,128)(2,1)S(1)}, bf16[128,512]{1,0:T(8,128)(2,1)S(1)}, bf16[128,512]{1,0:T(8,128)(2,1)S(1)}) custom-call(bf16[560,128]{1,0:T(8,128)(2,1)S(1)} %get-tuple-element.15.after.refs_0_, bf16[560,128]{1,0:T(8,128)(2,1)S(1)} %collective-permute-done.refs_1_, ...), custom_call_target="tpu_custom_call" | custom-call | flops 536870912 | bytes 4304896 | tf_op jit(solution)/shard_map/pallas_call | solution.py:396
  20.6 3.4 %collective-permute-start.5 = (bf16[128,512]{1,0:T(8,128)(2,1)S(1)}, bf16[128,512]{1,0:T(8,128)(2,1)S(1)}, u32[]{:S(2)}, u32[]{:S(2)}) collective-permute-start(bf16[128,512]{1,0:T(8,128)(2,1)S(1)} %get-tuple-element.22), channel_id=1, source_target_pairs={{0,12},{2,14},{4,8},{6,10},{8,20},{10,22},{12,16},{14,18},{16,28},... | collective-permute-start | bytes 393224 | tf_op jit(solution)/shard_map/ppermute | solution.py:414
  24.0 3.7 %collective-permute-start.6 = (bf16[128,512]{1,0:T(8,128)(2,1)S(1)}, bf16[128,512]{1,0:T(8,128)(2,1)S(1)}, u32[]{:S(2)}, u32[]{:S(2)}) collective-permute-start(bf16[128,512]{1,0:T(8,128)(2,1)S(1)} %get-tuple-element.23), channel_id=1, source_target_pairs={{0,10},{2,12},{4,14},{6,8},{8,18},{10,20},{12,22},{14,16},{16,26},... | collective-permute-start | bytes 393224 | tf_op jit(solution)/shard_map/ppermute | solution.py:414
  27.7 2.0 %collective-permute-start.7 = (bf16[128,512]{1,0:T(8,128)(2,1)S(1)}, bf16[128,512]{1,0:T(8,128)(2,1)S(1)}, u32[]{:S(2)}, u32[]{:S(2)}) collective-permute-start(bf16[128,512]{1,0:T(8,128)(2,1)S(1)} %get-tuple-element.24), channel_id=1, source_target_pairs={{0,14},{2,8},{4,10},{6,12},{8,22},{10,16},{12,18},{14,20},{16,30},... | collective-permute-start | bytes 393224 | tf_op jit(solution)/shard_map/ppermute | solution.py:414
  29.7 0.5 %collective-permute-start.4 = (bf16[128,512]{1,0:T(8,128)(2,1)S(1)}, bf16[128,512]{1,0:T(8,128)(2,1)S(1)}, u32[]{:S(2)}, u32[]{:S(2)}) collective-permute-start(bf16[128,512]{1,0:T(8,128)(2,1)S(1)} %get-tuple-element.21), channel_id=1, source_target_pairs={{0,8},{2,10},{4,12},{6,14},{8,16},{10,18},{12,20},{14,22},{16,24},... | collective-permute-start | bytes 393224 | tf_op jit(solution)/shard_map/ppermute | solution.py:414
  30.2 0.0 collective-permute-done.5.refs_0_
  30.2 5.3 %collective-permute-done.6.refs_1_ = bf16[128,512]{1,0:T(8,128)(2,1)S(1)} collective-permute-done((bf16[128,512]{1,0:T(8,128)(2,1)S(1)}, bf16[128,512]{1,0:T(8,128)(2,1)S(1)}, u32[]{:S(2)}, u32[]{:S(2)}) %collective-permute-start.6) | collective-permute-done | bytes 131104 | tf_op jit(solution)/shard_map/ppermute | solution.py:414
  35.5 1.6 %collective-permute-done.7.refs_2_ = bf16[128,512]{1,0:T(8,128)(2,1)S(1)} collective-permute-done((bf16[128,512]{1,0:T(8,128)(2,1)S(1)}, bf16[128,512]{1,0:T(8,128)(2,1)S(1)}, u32[]{:S(2)}, u32[]{:S(2)}) %collective-permute-start.7) | collective-permute-done | bytes 131104 | tf_op jit(solution)/shard_map/ppermute | solution.py:414
  37.1 1.0 %shard_map.77.refs_1_ = f32[128,2048]{1,0:T(8,128)} custom-call(bf16[128,512]{1,0:T(8,128)(2,1)S(1)} %collective-permute-done.5.refs_0_, bf16[128,512]{1,0:T(8,128)(2,1)S(1)} %collective-permute-done.6.refs_1_, bf16[128,512]{1,0:T(8,128)(2,1)S(1)} %collective-permute-done.7.refs_2_), custom_call_target="tpu_custom_call" | custom-call | bytes 1441792 | tf_op jit(solution)/shard_map/pallas_call | solution.py:396
  38.1 1.7 %collective-permute-done.4.refs_0_ = bf16[128,512]{1,0:T(8,128)(2,1)S(1)} collective-permute-done((bf16[128,512]{1,0:T(8,128)(2,1)S(1)}, bf16[128,512]{1,0:T(8,128)(2,1)S(1)}, u32[]{:S(2)}, u32[]{:S(2)}) %collective-permute-start.4) | collective-permute-done | bytes 131104 | tf_op jit(solution)/shard_map/ppermute | solution.py:414
  39.8 0.7 %shard_map.78 = f32[128,2048]{1,0:T(8,128)} custom-call(bf16[128,512]{1,0:T(8,128)(2,1)S(1)} %collective-permute-done.4.refs_0_, f32[128,2048]{1,0:T(8,128)} %shard_map.77.refs_1_), custom_call_target="tpu_custom_call", output_to_operand_aliasing={{}: (1, {})} | custom-call | bytes 2228224 | tf_op jit(solution)/shard_map/pallas_call | solution.py:396
  (5 shorter events, 0.0 us)
Async XLA Ops:
  0.0 16.8 %copy-start.1 = (bf16[32,512]{1,0:T(8,128)(2,1)S(1)}, bf16[32,512]{1,0:T(8,128)(2,1)}, u32[]{:S(2)}) copy-start(bf16[32,512]{1,0:T(8,128)(2,1)} %constant.8.clone.refs_5_) | copy-start | bytes 98308
  1.6 9.8 %collective-permute-start = (bf16[560,128]{1,0:T(8,128)(2,1)S(1)}, bf16[560,128]{1,0:T(8,128)(2,1)S(1)}, u32[]{:S(2)}, u32[]{:S(2)}) collective-permute-start(bf16[560,128]{1,0:T(8,128)(2,1)S(1)} %get-tuple-element.16), channel_id=1, source_target_pairs={{0,2},{2,4},{4,6},{6,0},{8,10},{10,12},{12,14},{14,8},{16,18},{18,... | collective-permute-start | bytes 430088 | tf_op jit(solution)/shard_map/ppermute | solution.py:414
  4.7 12.0 %collective-permute-start.1 = (bf16[560,128]{1,0:T(8,128)(2,1)S(1)}, bf16[560,128]{1,0:T(8,128)(2,1)S(1)}, u32[]{:S(2)}, u32[]{:S(2)}) collective-permute-start(bf16[560,128]{1,0:T(8,128)(2,1)S(1)} %get-tuple-element.17), channel_id=1, source_target_pairs={{0,4},{2,6},{4,0},{6,2},{8,12},{10,14},{12,8},{14,10},{16,20},{18,... | collective-permute-start | bytes 430088 | tf_op jit(solution)/shard_map/ppermute | solution.py:414
  7.2 9.4 %collective-permute-start.2 = (bf16[560,128]{1,0:T(8,128)(2,1)S(1)}, bf16[560,128]{1,0:T(8,128)(2,1)S(1)}, u32[]{:S(2)}, u32[]{:S(2)}) collective-permute-start(bf16[560,128]{1,0:T(8,128)(2,1)S(1)} %get-tuple-element.18), channel_id=1, source_target_pairs={{0,6},{2,0},{4,2},{6,4},{8,14},{10,8},{12,10},{14,12},{16,22},{18,... | collective-permute-start | bytes 430088 | tf_op jit(solution)/shard_map/ppermute | solution.py:414
  8.6 9.4 %copy-start = (bf16[1,3,3,2048]{3,2,1,0:T(4,128)(2,1)S(1)}, bf16[1,3,3,2048]{3,2,1,0:T(4,128)(2,1)}, u32[]{:S(2)}) copy-start(bf16[1,3,3,2048]{3,2,1,0:T(4,128)(2,1)} %param.9) | copy-start | bytes 110596
  8.6 9.4 %copy-start.2 = (f32[1,2048]{1,0:T(1,128)S(1)}, f32[1,2048]{1,0:T(1,128)}, u32[]{:S(2)}) copy-start(f32[1,2048]{1,0:T(1,128)} %refs_6_.1) | copy-start | bytes 24580
  16.7 1.2 %collective-permute-start.3 = (bf16[64,128]{1,0:T(8,128)(2,1)S(1)}, bf16[64,128]{1,0:T(8,128)(2,1)S(1)}, u32[]{:S(2)}, u32[]{:S(2)}) collective-permute-start(bf16[64,128]{1,0:T(8,128)(2,1)S(1)} %pad_maximum_fusion), channel_id=1, source_target_pairs={{0,1},{1,0},{2,3},{3,2},{4,5},{5,4},{6,7},{7,6},{8,9},{9,8},{10,11... | collective-permute-start | bytes 49160 | tf_op jit(solution)/shard_map/ppermute | solution.py:453
  20.6 9.6 %collective-permute-start.5 = (bf16[128,512]{1,0:T(8,128)(2,1)S(1)}, bf16[128,512]{1,0:T(8,128)(2,1)S(1)}, u32[]{:S(2)}, u32[]{:S(2)}) collective-permute-start(bf16[128,512]{1,0:T(8,128)(2,1)S(1)} %get-tuple-element.22), channel_id=1, source_target_pairs={{0,12},{2,14},{4,8},{6,10},{8,20},{10,22},{12,16},{14,18},{16,28},... | collective-permute-start | bytes 393224 | tf_op jit(solution)/shard_map/ppermute | solution.py:414
  24.0 11.5 %collective-permute-start.6 = (bf16[128,512]{1,0:T(8,128)(2,1)S(1)}, bf16[128,512]{1,0:T(8,128)(2,1)S(1)}, u32[]{:S(2)}, u32[]{:S(2)}) collective-permute-start(bf16[128,512]{1,0:T(8,128)(2,1)S(1)} %get-tuple-element.23), channel_id=1, source_target_pairs={{0,10},{2,12},{4,14},{6,8},{8,18},{10,20},{12,22},{14,16},{16,26},... | collective-permute-start | bytes 393224 | tf_op jit(solution)/shard_map/ppermute | solution.py:414
  27.7 9.4 %collective-permute-start.7 = (bf16[128,512]{1,0:T(8,128)(2,1)S(1)}, bf16[128,512]{1,0:T(8,128)(2,1)S(1)}, u32[]{:S(2)}, u32[]{:S(2)}) collective-permute-start(bf16[128,512]{1,0:T(8,128)(2,1)S(1)} %get-tuple-element.24), channel_id=1, source_target_pairs={{0,14},{2,8},{4,10},{6,12},{8,22},{10,16},{12,18},{14,20},{16,30},... | collective-permute-start | bytes 393224 | tf_op jit(solution)/shard_map/ppermute | solution.py:414
  29.7 10.1 %collective-permute-start.4 = (bf16[128,512]{1,0:T(8,128)(2,1)S(1)}, bf16[128,512]{1,0:T(8,128)(2,1)S(1)}, u32[]{:S(2)}, u32[]{:S(2)}) collective-permute-start(bf16[128,512]{1,0:T(8,128)(2,1)S(1)} %get-tuple-element.21), channel_id=1, source_target_pairs={{0,8},{2,10},{4,12},{6,14},{8,16},{10,18},{12,20},{14,22},{16,24},... | collective-permute-start | bytes 393224 | tf_op jit(solution)/shard_map/ppermute | solution.py:414

commit v4 on v3

--- a/solution.py
+++ b/solution.py
@@ -204,7 +204,7 @@
 
 
 def cut_kernel(peers, x_hbm, filt_hbm, *refs):
-    outs, (x_ref, filt_ref, plain, turned, sems) = refs[:peers], refs[peers:]
+    outs, (sums_ref, x_ref, filt_ref, plain, turned, sems) = refs[:peers], refs[peers:]
     rank = lax.axis_index("ctx")
     rows, chans = x_hbm.shape
     part, width = rows // 2, chans // peers
@@ -244,8 +244,17 @@
     nth = lax.broadcasted_iota(jnp.int32, (EXTRA, rows), 0)
     terms = three_terms(row)
     sums = jnp.where(nth == 0, terms[0], jnp.where(nth == 1, terms[1], jnp.where(nth == 2, terms[2], 0.0)))
+    sums_ref[...] = sums.astype(jnp.bfloat16)
     for step in range(peers):
         outs[step][base + filters :, :] = sums.astype(jnp.bfloat16)
+
+
+def attach_kernel(count, *refs):
+    messages, (own_ref, other_ref) = refs[:count], refs[count : count + 2]
+    outs = refs[count + 2 :]
+    both = own_ref[...].astype(jnp.float32) + pltpu.roll(other_ref[...].astype(jnp.float32), 3, 0)
+    for out in outs:
+        out[out.shape[0] - EXTRA :, :] = both.astype(jnp.bfloat16)
 
 
 def table_kernel(pieces, after, *refs):
@@ -253,8 +262,9 @@
     tables, outs, sems = refs[:count], refs[count : 2 * count], refs[2 * count]
     copies = []
     for t in range(count):
-        depth = tables[t].shape[0] // pieces
-        for i in range(pieces):
+        parts = pieces if tables[t].shape[0] % (pieces * LANES) == 0 else 1
+        depth = tables[t].shape[0] // parts
+        for i in range(parts):
             here = pl.ds(i * depth, depth)
             copies.append(pltpu.make_async_copy(tables[t].at[here], outs[t].at[here], sems.at[len(copies)]))
     for copy in copies:
@@ -263,104 +273,146 @@
         copy.wait()
 
 
-def filter_kernel(peers, *refs):
+def scale_of(*sums):
+    square = sum(jnp.sum(terms.astype(jnp.float32), axis=0, keepdims=True) for terms in sums)
+    return column_of(lax.rsqrt(square * (1.0 / CHAN) + 1e-06))
+
+
+def scale_block(block, scale, held):
+    rows = block.shape[1]
+    part = rows // 2
+    for tile in range(held.shape[2] // LANES):
+        for odd in range(2):
+            own = tile * rows + odd * part
+            acts = block[own : own + part, :].astype(jnp.float32) * scale[odd * part : (odd + 1) * part]
+            held[odd, 8:, tile * LANES : (tile + 1) * LANES] = acts
+
+
+def short_filters(held, depth, taps, lanes):
+    now = [held[odd, 8 : 8 + depth, lanes] for odd in range(2)]
+    last = [held[odd, 7 : 7 + depth, lanes] for odd in range(2)]
+    results = []
+    for moved in ((now[0], last[1], last[0]), (now[1], now[0], last[1])):
+        features = []
+        for feature in taps:
+            running = feature[0][:, lanes] * moved[0]
+            for i in range(1, TAPS):
+                running = running + feature[i][:, lanes] * moved[i]
+            features.append(running)
+        results.append((features[0].astype(jnp.bfloat16), (features[1] * features[2]).astype(jnp.bfloat16)))
+    return results
+
+
+def read_taps(taps_ref, chans):
+    return [[taps_ref[f, i : i + 1, chans].astype(jnp.float32) for i in range(TAPS)] for f in range(3)]
+
+
+def spread_out(block, spread_ref):
+    filters = spread_ref.shape[0]
+    base = block.shape[0] - EXTRA - filters
+    return lax.dot_general(
+        block[base : base + filters, :],
+        spread_ref[...],
+        (((0,), (0,)), ((), ())),
+        preferred_element_type=jnp.float32,
+    ).astype(jnp.bfloat16)
+
+
+def early_kernel(*refs):
+    blocks, sums = refs[:2], (refs[2:4], refs[4:6])
+    taps_ref, spread_ref, held, query, product, spread = refs[6:]
+    width = held.shape[3]
+    chans = pl.ds(pl.multiple_of(lax.axis_index("ctx") * width, width), width)
+    taps = read_taps(taps_ref, chans)
+    part = product.shape[2]
+    for i in range(2):
+        held[i, :, :8, :] = jnp.zeros((2, 8, width), jnp.float32)
+        scale_block(blocks[i], scale_of(sums[i][0][...], sums[i][1][...]), held.at[i])
+        for first in range(0, width, LANES):
+            lanes = slice(first, first + LANES)
+            for odd, results in enumerate(short_filters(held.at[i], part, taps, lanes)):
+                query[i, odd, :, lanes], product[i, odd, :, lanes] = results
+        spread[i] = spread_out(blocks[i], spread_ref)
+
+
+def layer_kernel(peers, early, late, *refs):
     blocks = refs[:peers]
-    ahead_ref, spread_ref, filt_spec, even, odd = refs[peers:]
-    rank = lax.axis_index("ctx")
-    filters, width = spread_ref.shape
-    rows = blocks[0].shape[1]
-    part = rows // 2
-    half = part * peers
-    base = width // LANES * rows
-    for step in range(peers):
-        here = pl.ds(pl.multiple_of(next_place(rank, -step, peers) * part, part), part)
-        spread = lax.dot_general(
-            blocks[step][base : base + filters, :],
-            spread_ref[...],
-            (((0,), (0,)), ((), ())),
-            preferred_element_type=jnp.float32,
-        ).astype(jnp.bfloat16)
-        even[here, :] = spread[:part]
-        odd[here, :] = spread[part:]
-    for im in range(2):
-        here = slice(im * half, (im + 1) * half)
-        there = slice((im + 2) * half, (im + 3) * half)
-        of_even = jnp.dot(ahead_ref[here, :], even[...], preferred_element_type=jnp.float32)
-        of_odd = jnp.dot(ahead_ref[there, :], odd[...], preferred_element_type=jnp.float32)
-        filt_spec[here, :] = of_even + of_odd
-        filt_spec[there, :] = of_odd - of_even if im else of_even - of_odd
-
-
-def layer_kernel(peers, *refs):
-    blocks = refs[:peers]
-    other_sums, taps_ref, skip_ref, ahead_ref, return_ref, filt_spec = refs[peers : peers + 6]
-    outs = refs[peers + 6 : 2 * peers + 6]
-    held, query, product, spec, weighted, conv = refs[2 * peers + 6 :]
+    taps_ref, skip_ref, ahead_ref, return_ref, spread_ref = refs[peers : peers + 5]
+    early_held, early_query, early_product, early_spread = refs[peers + 5 : peers + 9]
+    outs = refs[peers + 9 : 2 * peers + 9]
+    held, top_held, query, product, spread, spec, filt_spec, weighted, conv = refs[2 * peers + 9 :]
     rank = lax.axis_index("ctx")
     rows, width = outs[0].shape
     part, half = rows // 2, rows * peers // 2
-    base = blocks[0].shape[0] - EXTRA
+    top = top_held.shape[2] - 8
     chans = pl.ds(pl.multiple_of(rank * width, width), width)
-    taps = [[taps_ref[f, i : i + 1, chans].astype(jnp.float32) for i in range(TAPS)] for f in range(3)]
+    taps = read_taps(taps_ref, chans)
     skip = skip_ref[:, chans]
-    held[:, :8, :] = jnp.zeros((2, 8, width), jnp.float32)
-    for step in range(peers):
-        here = blocks[step][base:, :].astype(jnp.float32)
-        there = other_sums[step * EXTRA : (step + 1) * EXTRA, :].astype(jnp.float32)
-        square = jnp.sum(here, axis=0, keepdims=True) + jnp.sum(there, axis=0, keepdims=True)
-        scale = column_of(lax.rsqrt(square * (1.0 / CHAN) + 1e-06))
-        begin = pl.multiple_of(next_place(rank, -step, peers) * part, part) + 8
-        for tile in range(width // LANES):
-            lanes = slice(tile * LANES, (tile + 1) * LANES)
-            for odd in range(2):
-                acts = blocks[step][tile * rows + odd * part : tile * rows + (odd + 1) * part, :]
-                scaled = acts.astype(jnp.float32) * scale[odd * part : (odd + 1) * part]
-                held[odd, pl.ds(pl.multiple_of(begin, 8), part), lanes] = scaled
+    places = [next_place(rank, -step, peers) for step in range(peers)]
+    tokens = [pl.ds(pl.multiple_of(place * part, part), part) for place in places]
+    tops = [pl.ds(pl.multiple_of(place * part, part), top) for place in places]
+
+    for step in range(peers):
+        both = early_spread[early.index(step)] if step in early else spread_out(blocks[step], spread_ref)
+        for odd in range(2):
+            spread[odd, tokens[step], :] = both[odd * part : (odd + 1) * part]
+    for i, step in enumerate(late):
+        scale_block(blocks[step], scale_of(blocks[step][blocks[step].shape[0] - EXTRA :, :]), held.at[i])
+    for i, step in enumerate(early):
+        top_held[i, :, 8:, :] = early_held[i, :, 8 : 8 + top, :]
+    for step in range(peers):
+        mine = held.at[late.index(step)] if step in late else top_held.at[early.index(step)]
+        before = (step + 1) % peers
+        theirs = held.at[late.index(before)] if before in late else early_held.at[early.index(before)]
+        for odd in range(2):
+            row = theirs[odd, 7 + part : 8 + part, :]
+            mine[odd, 7:8, :] = jnp.where(places[step] > 0, row, 0.0)
+    for i, step in enumerate(early):
+        for odd in range(2):
+            query[odd, tokens[step], :] = early_query[i, odd]
+            product[odd, tokens[step], :] = early_product[i, odd]
     for first in range(0, width, LANES):
         lanes = slice(first, first + LANES)
-        near = [[jnp.broadcast_to(tap[:, lanes], (DEPTH, LANES)) for tap in feature] for feature in taps]
-        for top in range(0, half, DEPTH):
-            now = [held[odd, 8 + top : 8 + top + DEPTH, lanes] for odd in range(2)]
-            last = [held[odd, 7 + top : 7 + top + DEPTH, lanes] for odd in range(2)]
-            for odd, moved in ((0, (now[0], last[1], last[0])), (1, (now[1], now[0], last[1]))):
-                features = []
-                for feature in near:
-                    running = feature[0] * moved[0]
-                    for i in range(1, TAPS):
-                        running = running + feature[i] * moved[i]
-                    features.append(running)
-                query[odd, top : top + DEPTH, lanes] = features[0].astype(jnp.bfloat16)
-                product[odd, top : top + DEPTH, lanes] = (features[1] * features[2]).astype(jnp.bfloat16)
+        for step in range(peers):
+            if step in late:
+                source, depth, here = held.at[late.index(step)], part, tokens[step]
+            else:
+                source, depth, here = top_held.at[early.index(step)], top, tops[step]
+            for odd, results in enumerate(short_filters(source, depth, taps, lanes)):
+                query[odd, here, lanes], product[odd, here, lanes] = results
     for odd in range(2):
         table = ahead_ref[2 * odd * half : 2 * (odd + 1) * half, :]
+        filt_spec[odd] = jnp.dot(table, spread[odd], preferred_element_type=jnp.float32)
         spec[odd] = jnp.dot(table, product[odd], preferred_element_type=jnp.float32)
     for first in range(0, width, LANES):
         lanes = slice(first, first + LANES)
-        for top in range(0, half, DEPTH):
-            re, im = slice(top, top + DEPTH), slice(half + top, half + top + DEPTH)
-            far_re, far_im = (slice(2 * half + at.start, 2 * half + at.stop) for at in (re, im))
-            even_re, even_im = spec[0, re, lanes], spec[0, im, lanes]
-            odd_re, odd_im = spec[1, re, lanes], spec[1, im, lanes]
-            near_out = product_of(even_re + odd_re, even_im + odd_im, filt_spec[re, lanes], filt_spec[im, lanes])
-            far_out = product_of(
-                even_re - odd_re, odd_im - even_im, filt_spec[far_re, lanes], filt_spec[far_im, lanes]
-            )
-            weighted[0, re, lanes] = (near_out[0] + far_out[0]).astype(jnp.bfloat16)
-            weighted[0, im, lanes] = (near_out[1] - far_out[1]).astype(jnp.bfloat16)
-            weighted[1, re, lanes] = (near_out[0] - far_out[0]).astype(jnp.bfloat16)
-            weighted[1, im, lanes] = (near_out[1] + far_out[1]).astype(jnp.bfloat16)
+        for begin in range(0, half, DEPTH):
+            re, im = slice(begin, begin + DEPTH), slice(half + begin, half + begin + DEPTH)
+            near, far = [], []
+            for values in (spec, filt_spec):
+                even_re, even_im = values[0, re, lanes], values[0, im, lanes]
+                odd_re, odd_im = values[1, re, lanes], values[1, im, lanes]
+                near += [even_re + odd_re, even_im + odd_im]
+                far += [even_re - odd_re, odd_im - even_im]
+            near_re, near_im = product_of(*near)
+            far_re, far_im = product_of(*far)
+            weighted[0, re, lanes] = (near_re + far_re).astype(jnp.bfloat16)
+            weighted[0, im, lanes] = (near_im - far_im).astype(jnp.bfloat16)
+            weighted[1, re, lanes] = (near_re - far_re).astype(jnp.bfloat16)
+            weighted[1, im, lanes] = (near_im + far_im).astype(jnp.bfloat16)
     for odd in range(2):
         table = return_ref[odd * half : (odd + 1) * half, :]
         conv[odd] = jnp.dot(table, weighted[odd], preferred_element_type=jnp.float32)
     for step in range(peers):
-        tokens = pl.ds(pl.multiple_of(next_place(rank, step, peers) * part, part), part)
+        source = (peers - step) % peers
+        here = tokens[source]
         for tile in range(width // LANES):
             lanes = slice(tile * LANES, (tile + 1) * LANES)
             for odd in range(2):
                 own = tile * rows + odd * part
-                acts = blocks[(peers - step) % peers][own : own + part, :].astype(jnp.float32)
-                gated = conv[odd, tokens, lanes] + skip[:, lanes] * product[odd, tokens, lanes].astype(jnp.float32)
-                finished = acts + query[odd, tokens, lanes].astype(jnp.float32) * gated
+                acts = blocks[source][own : own + part, :].astype(jnp.float32)
+                gated = conv[odd, here, lanes] + skip[:, lanes] * product[odd, here, lanes].astype(jnp.float32)
+                finished = acts + query[odd, here, lanes].astype(jnp.float32) * gated
                 outs[step][odd * part : (odd + 1) * part, lanes] = finished.astype(jnp.bfloat16)
 
 
@@ -423,11 +475,12 @@
     half = length // 2
     bf16, f32 = jnp.bfloat16, jnp.float32
     pieces = 4
-    base = width // LANES * rows + filters
-    sent = on_device(
+    part, tail = rows // 2, width // LANES * rows + filters
+    message = jax.ShapeDtypeStruct((tail + EXTRA, rows), bf16)
+    *sent, own_sums = on_device(
         functools.partial(cut_kernel, peers),
         [acts, long_filter[0]],
-        [jax.ShapeDtypeStruct((base + EXTRA, rows), bf16)] * peers,
+        [message] * peers + [jax.ShapeDtypeStruct((EXTRA, rows), bf16)],
         [
             pltpu.VMEM((chans // LANES, rows, LANES), f32),
             pltpu.VMEM(long_filter.shape[1:], bf16),
@@ -437,65 +490,66 @@
         ],
         in_hbm=(0, 1),
     )
+    early, late = [0, 1], list(range(2, peers))
     got = [sent[0]] + [None] * (peers - 1)
-    far_first = sorted(range(1, peers), key=lambda k: abs(2 * k - peers))
-    for k in far_first:
-        got[k] = hop(sent[k], sections, peers, 0, k)
-    tables = [jnp.asarray(t) for t in odd_tables(length)]
-    ahead, back = on_device(
+    got[early[1]] = hop(sent[early[1]], sections, peers, 0, early[1])
+    other_sums = lax.ppermute(own_sums, "tp", [(0, 1), (1, 0)])
+    ready = on_device(
+        functools.partial(attach_kernel, len(late)),
+        [*(sent[k] for k in late), own_sums, other_sums],
+        [message] * len(late),
+        aliases={i: i for i in range(len(late))},
+    )
+    for k, x in zip(late, ready):
+        got[k] = hop(x, sections, peers, 0, k)
+    tables = [jnp.asarray(t) for t in (*odd_tables(length), spread_table(filters, width))]
+    tables += [short_filter[0], skip_gain]
+    ahead, back, spread, taps, skip = on_device(
         functools.partial(table_kernel, pieces),
-        [sent[0], *tables],
-        [jax.ShapeDtypeStruct(t.shape, bf16) for t in tables],
-        [pltpu.SemaphoreType.DMA((2 * pieces,))],
-        in_hbm=(1, 2),
-    )
-    own_sums = jnp.concatenate([g[base:] for g in got], axis=0)
-    other_sums = lax.ppermute(own_sums, "tp", [(0, 1), (1, 0)])
-    (filt_spec,) = on_device(
-        functools.partial(filter_kernel, peers),
-        [*got, ahead, jnp.asarray(spread_table(filters, width))],
-        [jax.ShapeDtypeStruct((2 * length, width), f32)],
-        [pltpu.VMEM((half, width), bf16)] * 2,
-        flops=2 * length * length * width,
+        [other_sums, *tables],
+        [jax.ShapeDtypeStruct(t.shape, t.dtype) for t in tables],
+        [pltpu.SemaphoreType.DMA((pieces * len(tables),))],
+        in_hbm=range(1, 1 + len(tables)),
+    )
+    far_sums = got[early[1]][tail:]
+    far_other = lax.ppermute(far_sums, "tp", [(0, 1), (1, 0)])
+    begun = on_device(
+        early_kernel,
+        [got[0], got[early[1]], own_sums, other_sums, far_sums, far_other, taps, spread],
+        [
+            jax.ShapeDtypeStruct((2, 2, part + 8, width), f32),
+            jax.ShapeDtypeStruct((2, 2, part, width), bf16),
+            jax.ShapeDtypeStruct((2, 2, part, width), bf16),
+            jax.ShapeDtypeStruct((2, rows, width), bf16),
+        ],
     )
     done = on_device(
-        functools.partial(layer_kernel, peers),
-        [*got, other_sums, short_filter[0], skip_gain, ahead, back, filt_spec],
+        functools.partial(layer_kernel, peers, early, late),
+        [*got, taps, skip, ahead, back, spread, *begun],
         [jax.ShapeDtypeStruct((rows, width), bf16)] * peers,
         [
-            pltpu.VMEM((2, half + 8, width), f32),
+            pltpu.VMEM((len(late), 2, part + 8, width), f32),
+            pltpu.VMEM((2, 2, EXTRA + 8, width), f32),
             pltpu.VMEM((2, half, width), bf16),
             pltpu.VMEM((2, half, width), bf16),
+            pltpu.VMEM((2, half, width), bf16),
+            pltpu.VMEM((2, length, width), f32),
             pltpu.VMEM((2, length, width), f32),
             pltpu.VMEM((2, length, width), bf16),
             pltpu.VMEM((2, half, width), f32),
         ],
-        flops=4 * length * length * width,
-    )
-    arrived = [None] * peers
-    for k in [*far_first, 0]:
-        arrived[k] = hop(done[k], sections, peers, 1, k)
+        flops=6 * length * length * width,
+    )
+    order = list(range(peers))
+    arrived = {k: hop(done[k], sections, peers, 1, k) for k in order}
     out = jax.ShapeDtypeStruct((rows, chans), f32)
     tiles = width // LANES
-
-    def staging(count):
-        return [pltpu.VMEM((count * tiles, rows, LANES), f32), pltpu.SemaphoreType.DMA((count * tiles,))]
-
     (received,) = on_device(
-        functools.partial(join_kernel, peers, far_first),
-        [arrived[k] for k in far_first],
+        functools.partial(join_kernel, peers, order),
+        [arrived[k] for k in order],
         [out],
-        staging(len(far_first)),
+        [pltpu.VMEM((peers * tiles, rows, LANES), f32), pltpu.SemaphoreType.DMA((peers * tiles,))],
         out_hbm=True,
-    )
-    (received,) = on_device(
-        functools.partial(join_kernel, peers, [0]),
-        [arrived[0], received],
-        [out],
-        staging(1),
-        in_hbm=(1,),
-        out_hbm=True,
-        aliases={1: 0},
     )
     return received[None]
 
@@ -506,7 +560,8 @@
     width = section_input.shape[2] // (peers * cores)
     filters = long_filter.shape[2] // (peers * cores)
     return (
-        tokens == peers * LANES
+        peers > 2
+        and tokens == peers * LANES
         and tokens <= 1024
         and width % LANES == 0
         and filters % EXTRA == 0

time: 40.8 us -> 37.9 us (0.929)
  waiting for transfers between devices: 15.8 us -> 14 us
  starting transfers between devices: 16.7 us -> 16.1 us
  Pallas kernels: 8.03 us -> 7.59 us
    ppermute x7, waiting for transfers between devices: 15.4 us -> 12.8 us  [hop(): return lax.ppermute(x, ('section', 'ctx'), route)]
    ppermute x1, waiting for transfers between devices: 0.4 us -> 1.16 us  [channel_local(): other_sums = lax.ppermute(own_sums, 'tp', [(0, 1), (1, 0)])]
    ppermute x7, starting transfers between devices: 16.6 us -> 16.1 us  [hop(): return lax.ppermute(x, ('section', 'ctx'), route)]
    pallas_call x6, Pallas kernels: 8.03 us -> 7.59 us  [on_device(): pl.pallas_call(kernel, out_shape=outs, in_specs=[far if i in in_hbm else...]
  transfers between devices with their start and end apart: 8 -> 9, of which waited for: 6 -> 7; matrix products, arithmetic and copies ran while one was open for 0% -> 0% of each run, Pallas kernels for 8% -> 6%
where the time goes in v4:
time: 37.9 us; the launch traced here: 37.7 us
  starting transfers between devices  16.1 us (42%)
  waiting for transfers between devices  14 us (37%)
  Pallas kernels  7.59 us (20%)
    ppermute x7, starting transfers between devices, hop(): return lax.ppermute(x, ('section', 'ctx'), route)  16.1 us
    ppermute x7, waiting for transfers between devices, hop(): return lax.ppermute(x, ('section', 'ctx'), route)  12.8 us
    pallas_call x6, Pallas kernels, on_device(): pl.pallas_call(kernel, out_shape=outs, in_specs=[far if i in in_hbm else...  7.59 us
    ppermute x1, waiting for transfers between devices, channel_local(): other_sums = lax.ppermute(own_sums, 'tp', [(0, 1), (1, 0)])  1.16 us
  transfers between devices with their start and end apart: 9, of which 7 were waited for; matrix products, arithmetic and copies ran while one was open for 0% of the time, Pallas kernels for 6%

profile of v4, /device:TPU:0, one launch (start us, length us, event | category | flops | bytes accessed | tf_op | source)
XLA Modules:
  0.0 37.7 jit_solution(15047531999984971514)
XLA Ops:
  0.0 1.6 %shard_map.73 = (bf16[560,128]{1,0:T(8,128)(2,1)S(1)}, bf16[560,128]{1,0:T(8,128)(2,1)S(1)}, bf16[560,128]{1,0:T(8,128)(2,1)S(1)}, bf16[560,128]{1,0:T(8,128)(2,1)S(1)}, bf16[16,128]{1,0:T(8,128)(2,1)S(1)}) custom-call(f32[128,2048]{1,0:T(8,128)} %bitcast.4, bf16[128,128]{1,0:T(8,128)(2,1)} %bitcast.6), custom_call_target="tpu_custom_call" | custom-call | bytes 1658880 | tf_op jit(solution)/shard_map/pallas_call | solution.py:448
  1.6 3.1 %collective-permute-start = (bf16[560,128]{1,0:T(8,128)(2,1)S(1)}, bf16[560,128]{1,0:T(8,128)(2,1)S(1)}, u32[]{:S(2)}, u32[]{:S(2)}) collective-permute-start(bf16[560,128]{1,0:T(8,128)(2,1)S(1)} %get-tuple-element.26), channel_id=1, source_target_pairs={{0,2},{2,4},{4,6},{6,0},{8,10},{10,12},{12,14},{14,8},{16,18},{18,... | collective-permute-start | bytes 430088 | tf_op jit(solution)/shard_map/ppermute | solution.py:466
  4.7 0.0 collective-permute-start.1
  4.7 1.2 %collective-permute-done.1.refs_3_.after = bf16[16,128]{1,0:T(8,128)(2,1)S(1)} collective-permute-done((bf16[16,128]{1,0:T(8,128)(2,1)S(1)}, bf16[16,128]{1,0:T(8,128)(2,1)S(1)}, u32[]{:S(2)}, u32[]{:S(2)}) %collective-permute-start.1) | collective-permute-done | bytes 4128 | tf_op jit(solution)/shard_map/ppermute | solution.py:496
  5.8 2.6 %collective-permute-start.2 = (bf16[560,128]{1,0:T(8,128)(2,1)S(1)}, bf16[560,128]{1,0:T(8,128)(2,1)S(1)}, u32[]{:S(2)}, u32[]{:S(2)}) collective-permute-start(bf16[560,128]{1,0:T(8,128)(2,1)S(1)} %get-tuple-element.30), channel_id=1, source_target_pairs={{0,4},{2,6},{4,0},{6,2},{8,12},{10,14},{12,8},{14,10},{16,20},{18,... | collective-permute-start | bytes 430088 | tf_op jit(solution)/shard_map/ppermute | solution.py:466
  8.4 1.3 %collective-permute-start.3 = (bf16[560,128]{1,0:T(8,128)(2,1)S(1)}, bf16[560,128]{1,0:T(8,128)(2,1)S(1)}, u32[]{:S(2)}, u32[]{:S(2)}) collective-permute-start(bf16[560,128]{1,0:T(8,128)(2,1)S(1)} %get-tuple-element.31), channel_id=1, source_target_pairs={{0,6},{2,0},{4,2},{6,4},{8,14},{10,8},{12,10},{14,12},{16,22},{18,... | collective-permute-start | bytes 430088 | tf_op jit(solution)/shard_map/ppermute | solution.py:466
  9.8 0.8 %collective-permute-done.refs_1_ = bf16[560,128]{1,0:T(8,128)(2,1)S(1)} collective-permute-done((bf16[560,128]{1,0:T(8,128)(2,1)S(1)}, bf16[560,128]{1,0:T(8,128)(2,1)S(1)}, u32[]{:S(2)}, u32[]{:S(2)}) %collective-permute-start) | collective-permute-done | bytes 143392 | tf_op jit(solution)/shard_map/ppermute | solution.py:466
  10.5 0.0 collective-permute-start.4
  10.5 1.5 %shard_map.75 = (bf16[1024,256]{1,0:T(8,128)(2,1)S(1)}, bf16[512,512]{1,0:T(8,128)(2,1)S(1)}, bf16[32,512]{1,0:T(8,128)(2,1)S(1)}, bf16[3,3,2048]{2,1,0:T(4,128)(2,1)S(1)}, f32[1,2048]{1,0:T(1,128)S(1)}) custom-call(bf16[16,128]{1,0:T(8,128)(2,1)S(1)} %collective-permute-done.1.refs_3_.after, bf16[1024,256]{1,0:T(8,128)(2,1)} %constant.6.clone.refs_0_, ...), custom_call_target="tpu_custom_call" | custom-call | bytes 2256896 | tf_op jit(solution)/shard_map/pallas_call | solution.py:448
  12.0 0.0 collective-permute-done.4.refs_5_
  12.0 0.8 %shard_map.76 = (f32[2,2,72,512]{3,2,1,0:T(8,128)S(1)}, bf16[2,2,64,512]{3,2,1,0:T(8,128)(2,1)S(1)}, bf16[2,2,64,512]{3,2,1,0:T(8,128)(2,1)S(1)}, bf16[2,128,512]{2,1,0:T(8,128)(2,1)S(1)}) custom-call(bf16[560,128]{1,0:T(8,128)(2,1)S(1)} %get-tuple-element.25.refs_0_, bf16[560,128]{1,0:T(8,128)(2,1)S(1)} %collective-permute-done.refs_1_, ...), custom_call_target="tpu_custom_call" | custom-call | bytes 1748992 | tf_op jit(solution)/shard_map/pallas_call | solution.py:448
  12.8 3.9 %collective-permute-done.2.refs_2_ = bf16[560,128]{1,0:T(8,128)(2,1)S(1)} collective-permute-done((bf16[560,128]{1,0:T(8,128)(2,1)S(1)}, bf16[560,128]{1,0:T(8,128)(2,1)S(1)}, u32[]{:S(2)}, u32[]{:S(2)}) %collective-permute-start.2) | collective-permute-done | bytes 143392 | tf_op jit(solution)/shard_map/ppermute | solution.py:466
  16.7 0.2 collective-permute-done.3.refs_3_
  16.9 2.7 %shard_map.77 = (bf16[128,512]{1,0:T(8,128)(2,1)S(1)}, bf16[128,512]{1,0:T(8,128)(2,1)S(1)}, bf16[128,512]{1,0:T(8,128)(2,1)S(1)}, bf16[128,512]{1,0:T(8,128)(2,1)S(1)}) custom-call(bf16[560,128]{1,0:T(8,128)(2,1)S(1)} %get-tuple-element.25.refs_0_, bf16[560,128]{1,0:T(8,128)(2,1)S(1)} %collective-permute-done.refs_1_, ...), custom_call_target="tpu_custom_call" | custom-call | flops 805306368 | bytes 3600384 | tf_op jit(solution)/shard_map/pallas_call | solution.py:448
  19.6 1.5 %collective-permute-start.5 = (bf16[128,512]{1,0:T(8,128)(2,1)S(1)}, bf16[128,512]{1,0:T(8,128)(2,1)S(1)}, u32[]{:S(2)}, u32[]{:S(2)}) collective-permute-start(bf16[128,512]{1,0:T(8,128)(2,1)S(1)} %get-tuple-element.41), channel_id=1, source_target_pairs={{0,8},{2,10},{4,12},{6,14},{8,16},{10,18},{12,20},{14,22},{16,24},... | collective-permute-start | bytes 393224 | tf_op jit(solution)/shard_map/ppermute | solution.py:466
  21.1 4.3 %collective-permute-start.6 = (bf16[128,512]{1,0:T(8,128)(2,1)S(1)}, bf16[128,512]{1,0:T(8,128)(2,1)S(1)}, u32[]{:S(2)}, u32[]{:S(2)}) collective-permute-start(bf16[128,512]{1,0:T(8,128)(2,1)S(1)} %get-tuple-element.42), channel_id=1, source_target_pairs={{0,10},{2,12},{4,14},{6,8},{8,18},{10,20},{12,22},{14,16},{16,26},... | collective-permute-start | bytes 393224 | tf_op jit(solution)/shard_map/ppermute | solution.py:466
  25.4 2.5 %collective-permute-start.7 = (bf16[128,512]{1,0:T(8,128)(2,1)S(1)}, bf16[128,512]{1,0:T(8,128)(2,1)S(1)}, u32[]{:S(2)}, u32[]{:S(2)}) collective-permute-start(bf16[128,512]{1,0:T(8,128)(2,1)S(1)} %get-tuple-element.43), channel_id=1, source_target_pairs={{0,12},{2,14},{4,8},{6,10},{8,20},{10,22},{12,16},{14,18},{16,28},... | collective-permute-start | bytes 393224 | tf_op jit(solution)/shard_map/ppermute | solution.py:466
  27.9 0.8 %collective-permute-start.8 = (bf16[128,512]{1,0:T(8,128)(2,1)S(1)}, bf16[128,512]{1,0:T(8,128)(2,1)S(1)}, u32[]{:S(2)}, u32[]{:S(2)}) collective-permute-start(bf16[128,512]{1,0:T(8,128)(2,1)S(1)} %get-tuple-element.44), channel_id=1, source_target_pairs={{0,14},{2,8},{4,10},{6,12},{8,22},{10,16},{12,18},{14,20},{16,30},... | collective-permute-start | bytes 393224 | tf_op jit(solution)/shard_map/ppermute | solution.py:466
  28.7 0.0 collective-permute-done.5.refs_0_
  28.7 1.6 %collective-permute-done.6.refs_1_ = bf16[128,512]{1,0:T(8,128)(2,1)S(1)} collective-permute-done((bf16[128,512]{1,0:T(8,128)(2,1)S(1)}, bf16[128,512]{1,0:T(8,128)(2,1)S(1)}, u32[]{:S(2)}, u32[]{:S(2)}) %collective-permute-start.6) | collective-permute-done | bytes 131104 | tf_op jit(solution)/shard_map/ppermute | solution.py:466
  30.3 5.5 %collective-permute-done.7.refs_2_ = bf16[128,512]{1,0:T(8,128)(2,1)S(1)} collective-permute-done((bf16[128,512]{1,0:T(8,128)(2,1)S(1)}, bf16[128,512]{1,0:T(8,128)(2,1)S(1)}, u32[]{:S(2)}, u32[]{:S(2)}) %collective-permute-start.7) | collective-permute-done | bytes 131104 | tf_op jit(solution)/shard_map/ppermute | solution.py:466
  35.8 0.9 %collective-permute-done.8.refs_3_ = bf16[128,512]{1,0:T(8,128)(2,1)S(1)} collective-permute-done((bf16[128,512]{1,0:T(8,128)(2,1)S(1)}, bf16[128,512]{1,0:T(8,128)(2,1)S(1)}, u32[]{:S(2)}, u32[]{:S(2)}) %collective-permute-start.8) | collective-permute-done | bytes 131104 | tf_op jit(solution)/shard_map/ppermute | solution.py:466
  36.6 1.1 %shard_map.78 = f32[128,2048]{1,0:T(8,128)} custom-call(bf16[128,512]{1,0:T(8,128)(2,1)S(1)} %collective-permute-done.5.refs_0_, bf16[128,512]{1,0:T(8,128)(2,1)S(1)} %collective-permute-done.6.refs_1_, bf16[128,512]{1,0:T(8,128)(2,1)S(1)} %collective-permute-done.7.refs_2_, bf16[128,512]{1,0:T(8,128)(2,1)S(1)} %collective-permute-done.8.refs_3_), custom_call_target="tpu_custom_call" | custom-call | bytes 1572864 | tf_op jit(solution)/shard_map/pallas_call | solution.py:448
  (2 shorter events, 0.0 us)
Async XLA Ops:
  1.6 9.0 %collective-permute-start = (bf16[560,128]{1,0:T(8,128)(2,1)S(1)}, bf16[560,128]{1,0:T(8,128)(2,1)S(1)}, u32[]{:S(2)}, u32[]{:S(2)}) collective-permute-start(bf16[560,128]{1,0:T(8,128)(2,1)S(1)} %get-tuple-element.26), channel_id=1, source_target_pairs={{0,2},{2,4},{4,6},{6,0},{8,10},{10,12},{12,14},{14,8},{16,18},{18,... | collective-permute-start | bytes 430088 | tf_op jit(solution)/shard_map/ppermute | solution.py:466
  4.7 1.2 %collective-permute-start.1 = (bf16[16,128]{1,0:T(8,128)(2,1)S(1)}, bf16[16,128]{1,0:T(8,128)(2,1)S(1)}, u32[]{:S(2)}, u32[]{:S(2)}) collective-permute-start(bf16[16,128]{1,0:T(8,128)(2,1)S(1)} %get-tuple-element.29.refs_2_), channel_id=1, source_target_pairs={{0,1},{1,0},{2,3},{3,2},{4,5},{5,4},{6,7},{7,6},{8,9},{9,8},{10,11... | collective-permute-start | bytes 12296 | tf_op jit(solution)/shard_map/ppermute | solution.py:496
  5.8 10.9 %collective-permute-start.2 = (bf16[560,128]{1,0:T(8,128)(2,1)S(1)}, bf16[560,128]{1,0:T(8,128)(2,1)S(1)}, u32[]{:S(2)}, u32[]{:S(2)}) collective-permute-start(bf16[560,128]{1,0:T(8,128)(2,1)S(1)} %get-tuple-element.30), channel_id=1, source_target_pairs={{0,4},{2,6},{4,0},{6,2},{8,12},{10,14},{12,8},{14,10},{16,20},{18,... | collective-permute-start | bytes 430088 | tf_op jit(solution)/shard_map/ppermute | solution.py:466
  8.4 8.5 %collective-permute-start.3 = (bf16[560,128]{1,0:T(8,128)(2,1)S(1)}, bf16[560,128]{1,0:T(8,128)(2,1)S(1)}, u32[]{:S(2)}, u32[]{:S(2)}) collective-permute-start(bf16[560,128]{1,0:T(8,128)(2,1)S(1)} %get-tuple-element.31), channel_id=1, source_target_pairs={{0,6},{2,0},{4,2},{6,4},{8,14},{10,8},{12,10},{14,12},{16,22},{18,... | collective-permute-start | bytes 430088 | tf_op jit(solution)/shard_map/ppermute | solution.py:466
  10.5 1.5 %collective-permute-start.4 = (bf16[16,128]{1,0:T(8,128)(2,1)S(1)}, bf16[16,128]{1,0:T(8,128)(2,1)S(1)}, u32[]{:S(2)}, u32[]{:S(2)}) collective-permute-start(bf16[16,128]{1,0:T(8,128)(2,1)S(1)} %slice.4.refs_4_), channel_id=1, source_target_pairs={{0,1},{1,0},{2,3},{3,2},{4,5},{5,4},{6,7},{7,6},{8,9},{9,8},{10,11... | collective-permute-start | bytes 12296 | tf_op jit(solution)/shard_map/ppermute | solution.py:515
  19.6 9.1 %collective-permute-start.5 = (bf16[128,512]{1,0:T(8,128)(2,1)S(1)}, bf16[128,512]{1,0:T(8,128)(2,1)S(1)}, u32[]{:S(2)}, u32[]{:S(2)}) collective-permute-start(bf16[128,512]{1,0:T(8,128)(2,1)S(1)} %get-tuple-element.41), channel_id=1, source_target_pairs={{0,8},{2,10},{4,12},{6,14},{8,16},{10,18},{12,20},{14,22},{16,24},... | collective-permute-start | bytes 393224 | tf_op jit(solution)/shard_map/ppermute | solution.py:466
  21.1 9.2 %collective-permute-start.6 = (bf16[128,512]{1,0:T(8,128)(2,1)S(1)}, bf16[128,512]{1,0:T(8,128)(2,1)S(1)}, u32[]{:S(2)}, u32[]{:S(2)}) collective-permute-start(bf16[128,512]{1,0:T(8,128)(2,1)S(1)} %get-tuple-element.42), channel_id=1, source_target_pairs={{0,10},{2,12},{4,14},{6,8},{8,18},{10,20},{12,22},{14,16},{16,26},... | collective-permute-start | bytes 393224 | tf_op jit(solution)/shard_map/ppermute | solution.py:466
  25.4 10.4 %collective-permute-start.7 = (bf16[128,512]{1,0:T(8,128)(2,1)S(1)}, bf16[128,512]{1,0:T(8,128)(2,1)S(1)}, u32[]{:S(2)}, u32[]{:S(2)}) collective-permute-start(bf16[128,512]{1,0:T(8,128)(2,1)S(1)} %get-tuple-element.43), channel_id=1, source_target_pairs={{0,12},{2,14},{4,8},{6,10},{8,20},{10,22},{12,16},{14,18},{16,28},... | collective-permute-start | bytes 393224 | tf_op jit(solution)/shard_map/ppermute | solution.py:466
  27.9 8.7 %collective-permute-start.8 = (bf16[128,512]{1,0:T(8,128)(2,1)S(1)}, bf16[128,512]{1,0:T(8,128)(2,1)S(1)}, u32[]{:S(2)}, u32[]{:S(2)}) collective-permute-start(bf16[128,512]{1,0:T(8,128)(2,1)S(1)} %get-tuple-element.44), channel_id=1, source_target_pairs={{0,14},{2,8},{4,10},{6,12},{8,22},{10,16},{12,18},{14,20},{16,30},... | collective-permute-start | bytes 393224 | tf_op jit(solution)/shard_map/ppermute | solution.py:466

commit v5 on v4

--- a/solution.py
+++ b/solution.py
@@ -257,6 +257,12 @@
         out[out.shape[0] - EXTRA :, :] = both.astype(jnp.bfloat16)
 
 
+def collect_kernel(count, *refs):
+    out = refs[-1]
+    for i in range(count):
+        out[i * EXTRA : (i + 1) * EXTRA, :] = refs[i][refs[i].shape[0] - EXTRA :, :]
+
+
 def table_kernel(pieces, after, *refs):
     count = (len(refs) - 1) // 2
     tables, outs, sems = refs[:count], refs[count : 2 * count], refs[2 * count]
@@ -318,29 +324,45 @@
     ).astype(jnp.bfloat16)
 
 
-def early_kernel(*refs):
-    blocks, sums = refs[:2], (refs[2:4], refs[4:6])
-    taps_ref, spread_ref, held, query, product, spread = refs[6:]
-    width = held.shape[3]
-    chans = pl.ds(pl.multiple_of(lax.axis_index("ctx") * width, width), width)
+def lead_in(held, before, inside):
+    for odd in range(2):
+        row = before[odd, before.shape[1] - 1 :, :]
+        held[odd, 7:8, :] = jnp.where(inside, row, 0.0)
+
+
+def early_kernel(peers, early, *refs):
+    count = len(early)
+    blocks, halves = refs[:count], refs[count : 3 * count]
+    taps_ref, spread_ref, held, query, product, spread = refs[3 * count :]
+    width, part = held.shape[3], held.shape[2] - 8
+    rank = lax.axis_index("ctx")
+    chans = pl.ds(pl.multiple_of(rank * width, width), width)
     taps = read_taps(taps_ref, chans)
-    part = product.shape[2]
-    for i in range(2):
+    for i in range(count):
         held[i, :, :8, :] = jnp.zeros((2, 8, width), jnp.float32)
-        scale_block(blocks[i], scale_of(sums[i][0][...], sums[i][1][...]), held.at[i])
-        for first in range(0, width, LANES):
-            lanes = slice(first, first + LANES)
+        scale_block(blocks[i], scale_of(halves[2 * i][...], halves[2 * i + 1][...]), held.at[i])
+    for i, step in enumerate(early):
+        before = (step + 1) % peers
+        if before in early:
+            lead_in(held.at[i], held.at[early.index(before)], next_place(rank, -step, peers) > 0)
+    tokens = [pl.ds(pl.multiple_of(next_place(rank, -step, peers) * part, part), part) for step in early]
+    for first in range(0, width, LANES):
+        lanes = slice(first, first + LANES)
+        for i in range(count):
             for odd, results in enumerate(short_filters(held.at[i], part, taps, lanes)):
-                query[i, odd, :, lanes], product[i, odd, :, lanes] = results
-        spread[i] = spread_out(blocks[i], spread_ref)
+                query[odd, tokens[i], lanes], product[odd, tokens[i], lanes] = results
+    for i in range(count):
+        both = spread_out(blocks[i], spread_ref)
+        for odd in range(2):
+            spread[odd, tokens[i], :] = both[odd * part : (odd + 1) * part]
 
 
 def layer_kernel(peers, early, late, *refs):
     blocks = refs[:peers]
     taps_ref, skip_ref, ahead_ref, return_ref, spread_ref = refs[peers : peers + 5]
-    early_held, early_query, early_product, early_spread = refs[peers + 5 : peers + 9]
+    early_held = refs[peers + 5]
     outs = refs[peers + 9 : 2 * peers + 9]
-    held, top_held, query, product, spread, spec, filt_spec, weighted, conv = refs[2 * peers + 9 :]
+    query, product, spread, held, top_held, spec, filt_spec, weighted, conv = refs[2 * peers + 9 :]
     rank = lax.axis_index("ctx")
     rows, width = outs[0].shape
     part, half = rows // 2, rows * peers // 2
@@ -352,32 +374,25 @@
     tokens = [pl.ds(pl.multiple_of(place * part, part), part) for place in places]
     tops = [pl.ds(pl.multiple_of(place * part, part), top) for place in places]
 
-    for step in range(peers):
-        both = early_spread[early.index(step)] if step in early else spread_out(blocks[step], spread_ref)
+    for step in late:
+        both = spread_out(blocks[step], spread_ref)
         for odd in range(2):
             spread[odd, tokens[step], :] = both[odd * part : (odd + 1) * part]
     for i, step in enumerate(late):
         scale_block(blocks[step], scale_of(blocks[step][blocks[step].shape[0] - EXTRA :, :]), held.at[i])
-    for i, step in enumerate(early):
-        top_held[i, :, 8:, :] = early_held[i, :, 8 : 8 + top, :]
-    for step in range(peers):
-        mine = held.at[late.index(step)] if step in late else top_held.at[early.index(step)]
+    sources = [(held.at[i], part, step) for i, step in enumerate(late)]
+    lacking = [step for step in early if (step + 1) % peers in late]
+    for i, step in enumerate(lacking):
+        top_held[i, :, 8:, :] = early_held[early.index(step), :, 8 : 8 + top, :]
+        sources.append((top_held.at[i], top, step))
+    for source, _, step in sources:
         before = (step + 1) % peers
         theirs = held.at[late.index(before)] if before in late else early_held.at[early.index(before)]
-        for odd in range(2):
-            row = theirs[odd, 7 + part : 8 + part, :]
-            mine[odd, 7:8, :] = jnp.where(places[step] > 0, row, 0.0)
-    for i, step in enumerate(early):
-        for odd in range(2):
-            query[odd, tokens[step], :] = early_query[i, odd]
-            product[odd, tokens[step], :] = early_product[i, odd]
+        lead_in(source, theirs, places[step] > 0)
     for first in range(0, width, LANES):
         lanes = slice(first, first + LANES)
-        for step in range(peers):
-            if step in late:
-                source, depth, here = held.at[late.index(step)], part, tokens[step]
-            else:
-                source, depth, here = top_held.at[early.index(step)], top, tops[step]
+        for source, depth, step in sources:
+            here = tokens[step] if depth == part else tops[step]
             for odd, results in enumerate(short_filters(source, depth, taps, lanes)):
                 query[odd, here, lanes], product[odd, here, lanes] = results
     for odd in range(2):
@@ -490,9 +505,10 @@
         ],
         in_hbm=(0, 1),
     )
-    early, late = [0, 1], list(range(2, peers))
-    got = [sent[0]] + [None] * (peers - 1)
-    got[early[1]] = hop(sent[early[1]], sections, peers, 0, early[1])
+    early, late = [0, 1], list(range(peers - 1, 1, -1))
+    got = {0: sent[0]}
+    for k in early[1:]:
+        got[k] = hop(sent[k], sections, peers, 0, k)
     other_sums = lax.ppermute(own_sums, "tp", [(0, 1), (1, 0)])
     ready = on_device(
         functools.partial(attach_kernel, len(late)),
@@ -511,36 +527,42 @@
         [pltpu.SemaphoreType.DMA((pieces * len(tables),))],
         in_hbm=range(1, 1 + len(tables)),
     )
-    far_sums = got[early[1]][tail:]
-    far_other = lax.ppermute(far_sums, "tp", [(0, 1), (1, 0)])
+    (halves,) = on_device(
+        functools.partial(collect_kernel, len(early) - 1),
+        [*(got[k] for k in early[1:]), ready[0]],
+        [jax.ShapeDtypeStruct(((len(early) - 1) * EXTRA, rows), bf16)],
+    )
+    others = lax.ppermute(halves, "tp", [(0, 1), (1, 0)])
+    pairs = [own_sums, other_sums]
+    for i in range(len(early) - 1):
+        pairs += [half_sums[i * EXTRA : (i + 1) * EXTRA] for half_sums in (halves, others)]
     begun = on_device(
-        early_kernel,
-        [got[0], got[early[1]], own_sums, other_sums, far_sums, far_other, taps, spread],
+        functools.partial(early_kernel, peers, early),
+        [*(got[k] for k in early), *pairs, taps, spread],
         [
-            jax.ShapeDtypeStruct((2, 2, part + 8, width), f32),
-            jax.ShapeDtypeStruct((2, 2, part, width), bf16),
-            jax.ShapeDtypeStruct((2, 2, part, width), bf16),
-            jax.ShapeDtypeStruct((2, rows, width), bf16),
+            jax.ShapeDtypeStruct((len(early), 2, part + 8, width), f32),
+            *[jax.ShapeDtypeStruct((2, half, width), bf16)] * 3,
         ],
     )
     done = on_device(
         functools.partial(layer_kernel, peers, early, late),
-        [*got, taps, skip, ahead, back, spread, *begun],
-        [jax.ShapeDtypeStruct((rows, width), bf16)] * peers,
+        [*(got[k] for k in range(peers)), taps, skip, ahead, back, spread, *begun],
+        [
+            *[jax.ShapeDtypeStruct((rows, width), bf16)] * peers,
+            *[jax.ShapeDtypeStruct((2, half, width), bf16)] * 3,
+        ],
         [
             pltpu.VMEM((len(late), 2, part + 8, width), f32),
             pltpu.VMEM((2, 2, EXTRA + 8, width), f32),
-            pltpu.VMEM((2, half, width), bf16),
-            pltpu.VMEM((2, half, width), bf16),
-            pltpu.VMEM((2, half, width), bf16),
             pltpu.VMEM((2, length, width), f32),
             pltpu.VMEM((2, length, width), f32),
             pltpu.VMEM((2, length, width), bf16),
             pltpu.VMEM((2, half, width), f32),
         ],
         flops=6 * length * length * width,
-    )
-    order = list(range(peers))
+        aliases={peers + 6 + i: peers + i for i in range(3)},
+    )
+    order = sorted(range(peers), key=lambda k: (k % 2, k))
     arrived = {k: hop(done[k], sections, peers, 1, k) for k in order}
     out = jax.ShapeDtypeStruct((rows, chans), f32)
     tiles = width // LANES

time: 37.9 us -> 37.7 us (level)
  waiting for transfers between devices: 14 us -> 13.5 us
  starting transfers between devices: 16.1 us -> 16.5 us
    ppermute x7, waiting for transfers between devices: 12.8 us -> 12.3 us  [hop(): return lax.ppermute(x, ('section', 'ctx'), route)]
    ppermute x7, starting transfers between devices: 16.1 us -> 16.5 us  [hop(): return lax.ppermute(x, ('section', 'ctx'), route)]
    pallas_call x6 -> x7, Pallas kernels: 7.59 us -> 7.43 us  [on_device(): pl.pallas_call(kernel, out_shape=outs, in_specs=[far if i in in_hbm else...]
  transfers between devices with their start and end apart: 9 -> 9, of which waited for: 7 -> 6; matrix products, arithmetic and copies ran while one was open for 0% -> 0% of each run, Pallas kernels for 6% -> 6%
where the time goes in v5:
time: 37.7 us; the launch traced here: 37.4 us
  starting transfers between devices  16.5 us (44%)
  waiting for transfers between devices  13.5 us (36%)
  Pallas kernels  7.43 us (20%)
    ppermute x7, starting transfers between devices, hop(): return lax.ppermute(x, ('section', 'ctx'), route)  16.5 us
    ppermute x7, waiting for transfers between devices, hop(): return lax.ppermute(x, ('section', 'ctx'), route)  12.3 us
    pallas_call x7, Pallas kernels, on_device(): pl.pallas_call(kernel, out_shape=outs, in_specs=[far if i in in_hbm else...  7.43 us
    ppermute x1, waiting for transfers between devices, channel_local(): other_sums = lax.ppermute(own_sums, 'tp', [(0, 1), (1, 0)])  1.16 us
  transfers between devices with their start and end apart: 9, of which 6 were waited for; matrix products, arithmetic and copies ran while one was open for 0% of the time, Pallas kernels for 6%

profile of v5, /device:TPU:0, one launch (start us, length us, event | category | flops | bytes accessed | tf_op | source)
XLA Modules:
  0.0 37.4 jit_solution(6787754747892393848)
XLA Ops:
  0.0 1.6 %shard_map.73 = (bf16[560,128]{1,0:T(8,128)(2,1)S(1)}, bf16[560,128]{1,0:T(8,128)(2,1)S(1)}, bf16[560,128]{1,0:T(8,128)(2,1)S(1)}, bf16[560,128]{1,0:T(8,128)(2,1)S(1)}, bf16[16,128]{1,0:T(8,128)(2,1)S(1)}) custom-call(f32[128,2048]{1,0:T(8,128)} %bitcast.4, bf16[128,128]{1,0:T(8,128)(2,1)} %bitcast.6), custom_call_target="tpu_custom_call" | custom-call | bytes 1658880 | tf_op jit(solution)/shard_map/pallas_call | solution.py:463
  1.6 3.1 %collective-permute-start = (bf16[560,128]{1,0:T(8,128)(2,1)S(1)}, bf16[560,128]{1,0:T(8,128)(2,1)S(1)}, u32[]{:S(2)}, u32[]{:S(2)}) collective-permute-start(bf16[560,128]{1,0:T(8,128)(2,1)S(1)} %get-tuple-element.26), channel_id=1, source_target_pairs={{0,2},{2,4},{4,6},{6,0},{8,10},{10,12},{12,14},{14,8},{16,18},{18,... | collective-permute-start | bytes 430088 | tf_op jit(solution)/shard_map/ppermute | solution.py:481
  4.7 0.0 collective-permute-start.1
  4.7 1.2 %collective-permute-done.1.refs_3_.after = bf16[16,128]{1,0:T(8,128)(2,1)S(1)} collective-permute-done((bf16[16,128]{1,0:T(8,128)(2,1)S(1)}, bf16[16,128]{1,0:T(8,128)(2,1)S(1)}, u32[]{:S(2)}, u32[]{:S(2)}) %collective-permute-start.1) | collective-permute-done | bytes 4128 | tf_op jit(solution)/shard_map/ppermute | solution.py:512
  5.8 2.6 %collective-permute-start.2 = (bf16[560,128]{1,0:T(8,128)(2,1)S(1)}, bf16[560,128]{1,0:T(8,128)(2,1)S(1)}, u32[]{:S(2)}, u32[]{:S(2)}) collective-permute-start(bf16[560,128]{1,0:T(8,128)(2,1)S(1)} %get-tuple-element.30), channel_id=1, source_target_pairs={{0,4},{2,6},{4,0},{6,2},{8,12},{10,14},{12,8},{14,10},{16,20},{18,... | collective-permute-start | bytes 430088 | tf_op jit(solution)/shard_map/ppermute | solution.py:481
  8.4 1.3 %collective-permute-start.3 = (bf16[560,128]{1,0:T(8,128)(2,1)S(1)}, bf16[560,128]{1,0:T(8,128)(2,1)S(1)}, u32[]{:S(2)}, u32[]{:S(2)}) collective-permute-start(bf16[560,128]{1,0:T(8,128)(2,1)S(1)} %get-tuple-element.31.refs_1_), channel_id=1, source_target_pairs={{0,6},{2,0},{4,2},{6,4},{8,14},{10,8},{12,10},{14,12},{16,22},{18,... | collective-permute-start | bytes 430088 | tf_op jit(solution)/shard_map/ppermute | solution.py:481
  9.8 0.8 %collective-permute-done.refs_0_.refs_1_ = bf16[560,128]{1,0:T(8,128)(2,1)S(1)} collective-permute-done((bf16[560,128]{1,0:T(8,128)(2,1)S(1)}, bf16[560,128]{1,0:T(8,128)(2,1)S(1)}, u32[]{:S(2)}, u32[]{:S(2)}) %collective-permute-start) | collective-permute-done | bytes 143392 | tf_op jit(solution)/shard_map/ppermute | solution.py:481
  10.5 0.0 collective-permute-start.4
  10.5 1.5 %shard_map.75 = (bf16[1024,256]{1,0:T(8,128)(2,1)S(1)}, bf16[512,512]{1,0:T(8,128)(2,1)S(1)}, bf16[32,512]{1,0:T(8,128)(2,1)S(1)}, bf16[3,3,2048]{2,1,0:T(4,128)(2,1)S(1)}, f32[1,2048]{1,0:T(1,128)S(1)}) custom-call(bf16[16,128]{1,0:T(8,128)(2,1)S(1)} %collective-permute-done.1.refs_3_.after, bf16[1024,256]{1,0:T(8,128)(2,1)} %constant.6.clone.refs_0_, ...), custom_call_target="tpu_custom_call" | custom-call | bytes 2256896 | tf_op jit(solution)/shard_map/pallas_call | solution.py:463
  12.0 0.0 collective-permute-done.4.refs_5_
  12.0 0.8 %shard_map.77 = (f32[2,2,72,512]{3,2,1,0:T(8,128)S(1)}, bf16[2,256,512]{2,1,0:T(8,128)(2,1)S(1)}, bf16[2,256,512]{2,1,0:T(8,128)(2,1)S(1)}, bf16[2,256,512]{2,1,0:T(8,128)(2,1)S(1)}) custom-call(bf16[560,128]{1,0:T(8,128)(2,1)S(1)} %get-tuple-element.25.refs_0_, bf16[560,128]{1,0:T(8,128)(2,1)S(1)} %collective-permute-done.refs_0_.refs_1_, ...), custom_call_target="tpu_custom_call" | custom-call | bytes 2535424 | tf_op jit(solution)/shard_map/pallas_call | solution.py:463
  12.8 3.9 %collective-permute-done.2.refs_2_ = bf16[560,128]{1,0:T(8,128)(2,1)S(1)} collective-permute-done((bf16[560,128]{1,0:T(8,128)(2,1)S(1)}, bf16[560,128]{1,0:T(8,128)(2,1)S(1)}, u32[]{:S(2)}, u32[]{:S(2)}) %collective-permute-start.2) | collective-permute-done | bytes 143392 | tf_op jit(solution)/shard_map/ppermute | solution.py:481
  16.7 0.2 collective-permute-done.3.refs_3_
  16.9 2.5 %shard_map.78 = (bf16[128,512]{1,0:T(8,128)(2,1)S(1)}, bf16[128,512]{1,0:T(8,128)(2,1)S(1)}, bf16[128,512]{1,0:T(8,128)(2,1)S(1)}, bf16[128,512]{1,0:T(8,128)(2,...) custom-call(bf16[560,128]{1,0:T(8,128)(2,1)S(1)} %get-tuple-element., ...), custom_call_target="tpu_custom_call", output_to_operand_aliasing={{4}: (10, {}), {5}: (11, {}), {6}: (12, {})} | custom-call | flops 805306368 | bytes 5959680 | tf_op jit(solution)/shard_map/pallas_call | solution.py:463
  19.5 1.5 %collective-permute-start.5 = (bf16[128,512]{1,0:T(8,128)(2,1)S(1)}, bf16[128,512]{1,0:T(8,128)(2,1)S(1)}, u32[]{:S(2)}, u32[]{:S(2)}) collective-permute-start(bf16[128,512]{1,0:T(8,128)(2,1)S(1)} %get-tuple-element.41), channel_id=1, source_target_pairs={{0,8},{2,10},{4,12},{6,14},{8,16},{10,18},{12,20},{14,22},{16,24},... | collective-permute-start | bytes 393224 | tf_op jit(solution)/shard_map/ppermute | solution.py:481
  21.0 3.3 %collective-permute-start.6 = (bf16[128,512]{1,0:T(8,128)(2,1)S(1)}, bf16[128,512]{1,0:T(8,128)(2,1)S(1)}, u32[]{:S(2)}, u32[]{:S(2)}) collective-permute-start(bf16[128,512]{1,0:T(8,128)(2,1)S(1)} %get-tuple-element.42), channel_id=1, source_target_pairs={{0,12},{2,14},{4,8},{6,10},{8,20},{10,22},{12,16},{14,18},{16,28},... | collective-permute-start | bytes 393224 | tf_op jit(solution)/shard_map/ppermute | solution.py:481
  24.3 3.5 %collective-permute-start.7 = (bf16[128,512]{1,0:T(8,128)(2,1)S(1)}, bf16[128,512]{1,0:T(8,128)(2,1)S(1)}, u32[]{:S(2)}, u32[]{:S(2)}) collective-permute-start(bf16[128,512]{1,0:T(8,128)(2,1)S(1)} %get-tuple-element.43), channel_id=1, source_target_pairs={{0,10},{2,12},{4,14},{6,8},{8,18},{10,20},{12,22},{14,16},{16,26},... | collective-permute-start | bytes 393224 | tf_op jit(solution)/shard_map/ppermute | solution.py:481
  27.8 1.2 %collective-permute-start.8 = (bf16[128,512]{1,0:T(8,128)(2,1)S(1)}, bf16[128,512]{1,0:T(8,128)(2,1)S(1)}, u32[]{:S(2)}, u32[]{:S(2)}) collective-permute-start(bf16[128,512]{1,0:T(8,128)(2,1)S(1)} %get-tuple-element.44), channel_id=1, source_target_pairs={{0,14},{2,8},{4,10},{6,12},{8,22},{10,16},{12,18},{14,20},{16,30},... | collective-permute-start | bytes 393224 | tf_op jit(solution)/shard_map/ppermute | solution.py:481
  28.9 0.0 collective-permute-done.5.refs_0_
  28.9 0.0 collective-permute-done.6.refs_1_
  28.9 6.8 %collective-permute-done.7.refs_2_ = bf16[128,512]{1,0:T(8,128)(2,1)S(1)} collective-permute-done((bf16[128,512]{1,0:T(8,128)(2,1)S(1)}, bf16[128,512]{1,0:T(8,128)(2,1)S(1)}, u32[]{:S(2)}, u32[]{:S(2)}) %collective-permute-start.7) | collective-permute-done | bytes 131104 | tf_op jit(solution)/shard_map/ppermute | solution.py:481
  35.7 0.6 %collective-permute-done.8.refs_3_ = bf16[128,512]{1,0:T(8,128)(2,1)S(1)} collective-permute-done((bf16[128,512]{1,0:T(8,128)(2,1)S(1)}, bf16[128,512]{1,0:T(8,128)(2,1)S(1)}, u32[]{:S(2)}, u32[]{:S(2)}) %collective-permute-start.8) | collective-permute-done | bytes 131104 | tf_op jit(solution)/shard_map/ppermute | solution.py:481
  36.3 1.1 %shard_map.79 = f32[128,2048]{1,0:T(8,128)} custom-call(bf16[128,512]{1,0:T(8,128)(2,1)S(1)} %collective-permute-done.5.refs_0_, bf16[128,512]{1,0:T(8,128)(2,1)S(1)} %collective-permute-done.6.refs_1_, bf16[128,512]{1,0:T(8,128)(2,1)S(1)} %collective-permute-done.7.refs_2_, bf16[128,512]{1,0:T(8,128)(2,1)S(1)} %collective-permute-done.8.refs_3_), custom_call_target="tpu_custom_call" | custom-call | bytes 1572864 | tf_op jit(solution)/shard_map/pallas_call | solution.py:463
  (2 shorter events, 0.0 us)
Async XLA Ops:
  1.6 9.0 %collective-permute-start = (bf16[560,128]{1,0:T(8,128)(2,1)S(1)}, bf16[560,128]{1,0:T(8,128)(2,1)S(1)}, u32[]{:S(2)}, u32[]{:S(2)}) collective-permute-start(bf16[560,128]{1,0:T(8,128)(2,1)S(1)} %get-tuple-element.26), channel_id=1, source_target_pairs={{0,2},{2,4},{4,6},{6,0},{8,10},{10,12},{12,14},{14,8},{16,18},{18,... | collective-permute-start | bytes 430088 | tf_op jit(solution)/shard_map/ppermute | solution.py:481
  4.7 1.2 %collective-permute-start.1 = (bf16[16,128]{1,0:T(8,128)(2,1)S(1)}, bf16[16,128]{1,0:T(8,128)(2,1)S(1)}, u32[]{:S(2)}, u32[]{:S(2)}) collective-permute-start(bf16[16,128]{1,0:T(8,128)(2,1)S(1)} %get-tuple-element.29.refs_2_), channel_id=1, source_target_pairs={{0,1},{1,0},{2,3},{3,2},{4,5},{5,4},{6,7},{7,6},{8,9},{9,8},{10,11... | collective-permute-start | bytes 12296 | tf_op jit(solution)/shard_map/ppermute | solution.py:512
  5.8 10.9 %collective-permute-start.2 = (bf16[560,128]{1,0:T(8,128)(2,1)S(1)}, bf16[560,128]{1,0:T(8,128)(2,1)S(1)}, u32[]{:S(2)}, u32[]{:S(2)}) collective-permute-start(bf16[560,128]{1,0:T(8,128)(2,1)S(1)} %get-tuple-element.30), channel_id=1, source_target_pairs={{0,4},{2,6},{4,0},{6,2},{8,12},{10,14},{12,8},{14,10},{16,20},{18,... | collective-permute-start | bytes 430088 | tf_op jit(solution)/shard_map/ppermute | solution.py:481
  8.4 8.5 %collective-permute-start.3 = (bf16[560,128]{1,0:T(8,128)(2,1)S(1)}, bf16[560,128]{1,0:T(8,128)(2,1)S(1)}, u32[]{:S(2)}, u32[]{:S(2)}) collective-permute-start(bf16[560,128]{1,0:T(8,128)(2,1)S(1)} %get-tuple-element.31.refs_1_), channel_id=1, source_target_pairs={{0,6},{2,0},{4,2},{6,4},{8,14},{10,8},{12,10},{14,12},{16,22},{18,... | collective-permute-start | bytes 430088 | tf_op jit(solution)/shard_map/ppermute | solution.py:481
  10.5 1.5 %collective-permute-start.4 = (bf16[16,128]{1,0:T(8,128)(2,1)S(1)}, bf16[16,128]{1,0:T(8,128)(2,1)S(1)}, u32[]{:S(2)}, u32[]{:S(2)}) collective-permute-start(bf16[16,128]{1,0:T(8,128)(2,1)S(1)} %shard_map.76.refs_4_), channel_id=1, source_target_pairs={{0,1},{1,0},{2,3},{3,2},{4,5},{5,4},{6,7},{7,6},{8,9},{9,8},{10,11... | collective-permute-start | bytes 12296 | tf_op jit(solution)/shard_map/ppermute | solution.py:535
  19.5 9.5 %collective-permute-start.5 = (bf16[128,512]{1,0:T(8,128)(2,1)S(1)}, bf16[128,512]{1,0:T(8,128)(2,1)S(1)}, u32[]{:S(2)}, u32[]{:S(2)}) collective-permute-start(bf16[128,512]{1,0:T(8,128)(2,1)S(1)} %get-tuple-element.41), channel_id=1, source_target_pairs={{0,8},{2,10},{4,12},{6,14},{8,16},{10,18},{12,20},{14,22},{16,24},... | collective-permute-start | bytes 393224 | tf_op jit(solution)/shard_map/ppermute | solution.py:481
  21.0 7.9 %collective-permute-start.6 = (bf16[128,512]{1,0:T(8,128)(2,1)S(1)}, bf16[128,512]{1,0:T(8,128)(2,1)S(1)}, u32[]{:S(2)}, u32[]{:S(2)}) collective-permute-start(bf16[128,512]{1,0:T(8,128)(2,1)S(1)} %get-tuple-element.42), channel_id=1, source_target_pairs={{0,12},{2,14},{4,8},{6,10},{8,20},{10,22},{12,16},{14,18},{16,28},... | collective-permute-start | bytes 393224 | tf_op jit(solution)/shard_map/ppermute | solution.py:481
  24.3 11.5 %collective-permute-start.7 = (bf16[128,512]{1,0:T(8,128)(2,1)S(1)}, bf16[128,512]{1,0:T(8,128)(2,1)S(1)}, u32[]{:S(2)}, u32[]{:S(2)}) collective-permute-start(bf16[128,512]{1,0:T(8,128)(2,1)S(1)} %get-tuple-element.43), channel_id=1, source_target_pairs={{0,10},{2,12},{4,14},{6,8},{8,18},{10,20},{12,22},{14,16},{16,26},... | collective-permute-start | bytes 393224 | tf_op jit(solution)/shard_map/ppermute | solution.py:481
  27.8 8.6 %collective-permute-start.8 = (bf16[128,512]{1,0:T(8,128)(2,1)S(1)}, bf16[128,512]{1,0:T(8,128)(2,1)S(1)}, u32[]{:S(2)}, u32[]{:S(2)}) collective-permute-start(bf16[128,512]{1,0:T(8,128)(2,1)S(1)} %get-tuple-element.44), channel_id=1, source_target_pairs={{0,14},{2,8},{4,10},{6,12},{8,22},{10,16},{12,18},{14,20},{16,30},... | collective-permute-start | bytes 393224 | tf_op jit(solution)/shard_map/ppermute | solution.py:481

commit v6 on v5

--- a/solution.py
+++ b/solution.py
@@ -566,13 +566,17 @@
     arrived = {k: hop(done[k], sections, peers, 1, k) for k in order}
     out = jax.ShapeDtypeStruct((rows, chans), f32)
     tiles = width // LANES
-    (received,) = on_device(
-        functools.partial(join_kernel, peers, order),
-        [arrived[k] for k in order],
-        [out],
-        [pltpu.VMEM((peers * tiles, rows, LANES), f32), pltpu.SemaphoreType.DMA((peers * tiles,))],
-        out_hbm=True,
-    )
+    received = None
+    for steps in (order[: peers // 2], order[peers // 2 :]):
+        (received,) = on_device(
+            functools.partial(join_kernel, peers, steps),
+            [arrived[k] for k in steps] + ([] if received is None else [received]),
+            [out],
+            [pltpu.VMEM((len(steps) * tiles, rows, LANES), f32), pltpu.SemaphoreType.DMA((len(steps) * tiles,))],
+            in_hbm=(len(steps),),
+            out_hbm=True,
+            aliases={} if received is None else {len(steps): 0},
+        )
     return received[None]
 
 

time: 37.7 us -> 37.4 us (level)
  waiting for transfers between devices: 13.5 us -> 12.6 us
  Pallas kernels: 7.43 us -> 8.05 us
    ppermute x7, waiting for transfers between devices: 12.3 us -> 11.4 us  [hop(): return lax.ppermute(x, ('section', 'ctx'), route)]
    pallas_call x7 -> x8, Pallas kernels: 7.43 us -> 8.05 us  [on_device(): pl.pallas_call(kernel, out_shape=outs, in_specs=[far if i in in_hbm else...]
  transfers between devices with their start and end apart: 9 -> 9, of which waited for: 6 -> 6; matrix products, arithmetic and copies ran while one was open for 0% -> 0% of each run, Pallas kernels for 6% -> 8%
where the time goes in v6:
time: 37.4 us; the launch traced here: 37.2 us
  starting transfers between devices  16.5 us (44%)
  waiting for transfers between devices  12.6 us (34%)
  Pallas kernels  8.05 us (22%)
    ppermute x7, starting transfers between devices, hop(): return lax.ppermute(x, ('section', 'ctx'), route)  16.5 us
    ppermute x7, waiting for transfers between devices, hop(): return lax.ppermute(x, ('section', 'ctx'), route)  11.4 us
    pallas_call x8, Pallas kernels, on_device(): pl.pallas_call(kernel, out_shape=outs, in_specs=[far if i in in_hbm else...  8.05 us
    ppermute x1, waiting for transfers between devices, channel_local(): other_sums = lax.ppermute(own_sums, 'tp', [(0, 1), (1, 0)])  1.16 us
  transfers between devices with their start and end apart: 9, of which 6 were waited for; matrix products, arithmetic and copies ran while one was open for 0% of the time, Pallas kernels for 8%

profile of v6, /device:TPU:0, one launch (start us, length us, event | category | flops | bytes accessed | tf_op | source)
XLA Modules:
  0.0 37.2 jit_solution(8380118635273097187)
XLA Ops:
  0.0 1.6 %shard_map.73 = (bf16[560,128]{1,0:T(8,128)(2,1)S(1)}, bf16[560,128]{1,0:T(8,128)(2,1)S(1)}, bf16[560,128]{1,0:T(8,128)(2,1)S(1)}, bf16[560,128]{1,0:T(8,128)(2,1)S(1)}, bf16[16,128]{1,0:T(8,128)(2,1)S(1)}) custom-call(f32[128,2048]{1,0:T(8,128)} %bitcast.4, bf16[128,128]{1,0:T(8,128)(2,1)} %bitcast.6), custom_call_target="tpu_custom_call" | custom-call | bytes 1658880 | tf_op jit(solution)/shard_map/pallas_call | solution.py:463
  1.6 3.1 %collective-permute-start = (bf16[560,128]{1,0:T(8,128)(2,1)S(1)}, bf16[560,128]{1,0:T(8,128)(2,1)S(1)}, u32[]{:S(2)}, u32[]{:S(2)}) collective-permute-start(bf16[560,128]{1,0:T(8,128)(2,1)S(1)} %get-tuple-element.26), channel_id=1, source_target_pairs={{0,2},{2,4},{4,6},{6,0},{8,10},{10,12},{12,14},{14,8},{16,18},{18,... | collective-permute-start | bytes 430088 | tf_op jit(solution)/shard_map/ppermute | solution.py:481
  4.7 0.0 collective-permute-start.1
  4.7 1.2 %collective-permute-done.1.refs_3_.after = bf16[16,128]{1,0:T(8,128)(2,1)S(1)} collective-permute-done((bf16[16,128]{1,0:T(8,128)(2,1)S(1)}, bf16[16,128]{1,0:T(8,128)(2,1)S(1)}, u32[]{:S(2)}, u32[]{:S(2)}) %collective-permute-start.1) | collective-permute-done | bytes 4128 | tf_op jit(solution)/shard_map/ppermute | solution.py:512
  5.8 2.6 %collective-permute-start.2 = (bf16[560,128]{1,0:T(8,128)(2,1)S(1)}, bf16[560,128]{1,0:T(8,128)(2,1)S(1)}, u32[]{:S(2)}, u32[]{:S(2)}) collective-permute-start(bf16[560,128]{1,0:T(8,128)(2,1)S(1)} %get-tuple-element.30), channel_id=1, source_target_pairs={{0,4},{2,6},{4,0},{6,2},{8,12},{10,14},{12,8},{14,10},{16,20},{18,... | collective-permute-start | bytes 430088 | tf_op jit(solution)/shard_map/ppermute | solution.py:481
  8.4 1.3 %collective-permute-start.3 = (bf16[560,128]{1,0:T(8,128)(2,1)S(1)}, bf16[560,128]{1,0:T(8,128)(2,1)S(1)}, u32[]{:S(2)}, u32[]{:S(2)}) collective-permute-start(bf16[560,128]{1,0:T(8,128)(2,1)S(1)} %get-tuple-element.31.refs_1_), channel_id=1, source_target_pairs={{0,6},{2,0},{4,2},{6,4},{8,14},{10,8},{12,10},{14,12},{16,22},{18,... | collective-permute-start | bytes 430088 | tf_op jit(solution)/shard_map/ppermute | solution.py:481
  9.8 0.8 %collective-permute-done.refs_0_.refs_1_ = bf16[560,128]{1,0:T(8,128)(2,1)S(1)} collective-permute-done((bf16[560,128]{1,0:T(8,128)(2,1)S(1)}, bf16[560,128]{1,0:T(8,128)(2,1)S(1)}, u32[]{:S(2)}, u32[]{:S(2)}) %collective-permute-start) | collective-permute-done | bytes 143392 | tf_op jit(solution)/shard_map/ppermute | solution.py:481
  10.5 0.0 collective-permute-start.4
  10.5 1.5 %shard_map.75 = (bf16[1024,256]{1,0:T(8,128)(2,1)S(1)}, bf16[512,512]{1,0:T(8,128)(2,1)S(1)}, bf16[32,512]{1,0:T(8,128)(2,1)S(1)}, bf16[3,3,2048]{2,1,0:T(4,128)(2,1)S(1)}, f32[1,2048]{1,0:T(1,128)S(1)}) custom-call(bf16[16,128]{1,0:T(8,128)(2,1)S(1)} %collective-permute-done.1.refs_3_.after, bf16[1024,256]{1,0:T(8,128)(2,1)} %constant.6.clone.refs_0_, ...), custom_call_target="tpu_custom_call" | custom-call | bytes 2256896 | tf_op jit(solution)/shard_map/pallas_call | solution.py:463
  12.0 0.0 collective-permute-done.4.refs_5_
  12.0 0.8 %shard_map.77 = (f32[2,2,72,512]{3,2,1,0:T(8,128)S(1)}, bf16[2,256,512]{2,1,0:T(8,128)(2,1)S(1)}, bf16[2,256,512]{2,1,0:T(8,128)(2,1)S(1)}, bf16[2,256,512]{2,1,0:T(8,128)(2,1)S(1)}) custom-call(bf16[560,128]{1,0:T(8,128)(2,1)S(1)} %get-tuple-element.25.refs_0_, bf16[560,128]{1,0:T(8,128)(2,1)S(1)} %collective-permute-done.refs_0_.refs_1_, ...), custom_call_target="tpu_custom_call" | custom-call | bytes 2535424 | tf_op jit(solution)/shard_map/pallas_call | solution.py:463
  12.8 3.9 %collective-permute-done.2.refs_2_ = bf16[560,128]{1,0:T(8,128)(2,1)S(1)} collective-permute-done((bf16[560,128]{1,0:T(8,128)(2,1)S(1)}, bf16[560,128]{1,0:T(8,128)(2,1)S(1)}, u32[]{:S(2)}, u32[]{:S(2)}) %collective-permute-start.2) | collective-permute-done | bytes 143392 | tf_op jit(solution)/shard_map/ppermute | solution.py:481
  16.7 0.2 collective-permute-done.3.refs_3_
  16.9 2.5 %shard_map.78 = (bf16[128,512]{1,0:T(8,128)(2,1)S(1)}, bf16[128,512]{1,0:T(8,128)(2,1)S(1)}, bf16[128,512]{1,0:T(8,128)(2,1)S(1)}, bf16[128,512]{1,0:T(8,128)(2,...) custom-call(bf16[560,128]{1,0:T(8,128)(2,1)S(1)} %get-tuple-element., ...), custom_call_target="tpu_custom_call", output_to_operand_aliasing={{4}: (10, {}), {5}: (11, {}), {6}: (12, {})} | custom-call | flops 805306368 | bytes 5959680 | tf_op jit(solution)/shard_map/pallas_call | solution.py:463
  19.5 1.5 %collective-permute-start.7 = (bf16[128,512]{1,0:T(8,128)(2,1)S(1)}, bf16[128,512]{1,0:T(8,128)(2,1)S(1)}, u32[]{:S(2)}, u32[]{:S(2)}) collective-permute-start(bf16[128,512]{1,0:T(8,128)(2,1)S(1)} %get-tuple-element.43), channel_id=1, source_target_pairs={{0,8},{2,10},{4,12},{6,14},{8,16},{10,18},{12,20},{14,22},{16,24},... | collective-permute-start | bytes 393224 | tf_op jit(solution)/shard_map/ppermute | solution.py:481
  21.0 3.3 %collective-permute-start.8 = (bf16[128,512]{1,0:T(8,128)(2,1)S(1)}, bf16[128,512]{1,0:T(8,128)(2,1)S(1)}, u32[]{:S(2)}, u32[]{:S(2)}) collective-permute-start(bf16[128,512]{1,0:T(8,128)(2,1)S(1)} %get-tuple-element.44), channel_id=1, source_target_pairs={{0,12},{2,14},{4,8},{6,10},{8,20},{10,22},{12,16},{14,18},{16,28},... | collective-permute-start | bytes 393224 | tf_op jit(solution)/shard_map/ppermute | solution.py:481
  24.3 3.5 %collective-permute-start.5 = (bf16[128,512]{1,0:T(8,128)(2,1)S(1)}, bf16[128,512]{1,0:T(8,128)(2,1)S(1)}, u32[]{:S(2)}, u32[]{:S(2)}) collective-permute-start(bf16[128,512]{1,0:T(8,128)(2,1)S(1)} %get-tuple-element.41), channel_id=1, source_target_pairs={{0,10},{2,12},{4,14},{6,8},{8,18},{10,20},{12,22},{14,16},{16,26},... | collective-permute-start | bytes 393224 | tf_op jit(solution)/shard_map/ppermute | solution.py:481
  27.8 1.2 %collective-permute-start.6 = (bf16[128,512]{1,0:T(8,128)(2,1)S(1)}, bf16[128,512]{1,0:T(8,128)(2,1)S(1)}, u32[]{:S(2)}, u32[]{:S(2)}) collective-permute-start(bf16[128,512]{1,0:T(8,128)(2,1)S(1)} %get-tuple-element.42), channel_id=1, source_target_pairs={{0,14},{2,8},{4,10},{6,12},{8,22},{10,16},{12,18},{14,20},{16,30},... | collective-permute-start | bytes 393224 | tf_op jit(solution)/shard_map/ppermute | solution.py:481
  28.9 0.0 collective-permute-done.7.refs_0_
  28.9 0.0 collective-permute-done.8.refs_1_
  28.9 0.9 %shard_map.79.refs_2_ = f32[128,2048]{1,0:T(8,128)} custom-call(bf16[128,512]{1,0:T(8,128)(2,1)S(1)} %collective-permute-done.7.refs_0_, bf16[128,512]{1,0:T(8,128)(2,1)S(1)} %collective-permute-done.8.refs_1_), custom_call_target="tpu_custom_call" | custom-call | bytes 1310720 | tf_op jit(solution)/shard_map/pallas_call | solution.py:463
  29.8 5.9 %collective-permute-done.5.refs_0_ = bf16[128,512]{1,0:T(8,128)(2,1)S(1)} collective-permute-done((bf16[128,512]{1,0:T(8,128)(2,1)S(1)}, bf16[128,512]{1,0:T(8,128)(2,1)S(1)}, u32[]{:S(2)}, u32[]{:S(2)}) %collective-permute-start.5) | collective-permute-done | bytes 131104 | tf_op jit(solution)/shard_map/ppermute | solution.py:481
  35.7 0.6 %collective-permute-done.6.refs_1_ = bf16[128,512]{1,0:T(8,128)(2,1)S(1)} collective-permute-done((bf16[128,512]{1,0:T(8,128)(2,1)S(1)}, bf16[128,512]{1,0:T(8,128)(2,1)S(1)}, u32[]{:S(2)}, u32[]{:S(2)}) %collective-permute-start.6) | collective-permute-done | bytes 131104 | tf_op jit(solution)/shard_map/ppermute | solution.py:481
  36.3 0.9 %shard_map.80 = f32[128,2048]{1,0:T(8,128)} custom-call(bf16[128,512]{1,0:T(8,128)(2,1)S(1)} %collective-permute-done.5.refs_0_, bf16[128,512]{1,0:T(8,128)(2,1)S(1)} %collective-permute-done.6.refs_1_, f32[128,2048]{1,0:T(8,128)} %shard_map.79.refs_2_), custom_call_target="tpu_custom_call", output_to_operand_aliasing={{}: (2, {})} | custom-call | bytes 2359296 | tf_op jit(solution)/shard_map/pallas_call | solution.py:463
  (2 shorter events, 0.0 us)
Async XLA Ops:
  1.6 9.0 %collective-permute-start = (bf16[560,128]{1,0:T(8,128)(2,1)S(1)}, bf16[560,128]{1,0:T(8,128)(2,1)S(1)}, u32[]{:S(2)}, u32[]{:S(2)}) collective-permute-start(bf16[560,128]{1,0:T(8,128)(2,1)S(1)} %get-tuple-element.26), channel_id=1, source_target_pairs={{0,2},{2,4},{4,6},{6,0},{8,10},{10,12},{12,14},{14,8},{16,18},{18,... | collective-permute-start | bytes 430088 | tf_op jit(solution)/shard_map/ppermute | solution.py:481
  4.7 1.2 %collective-permute-start.1 = (bf16[16,128]{1,0:T(8,128)(2,1)S(1)}, bf16[16,128]{1,0:T(8,128)(2,1)S(1)}, u32[]{:S(2)}, u32[]{:S(2)}) collective-permute-start(bf16[16,128]{1,0:T(8,128)(2,1)S(1)} %get-tuple-element.29.refs_2_), channel_id=1, source_target_pairs={{0,1},{1,0},{2,3},{3,2},{4,5},{5,4},{6,7},{7,6},{8,9},{9,8},{10,11... | collective-permute-start | bytes 12296 | tf_op jit(solution)/shard_map/ppermute | solution.py:512
  5.8 10.9 %collective-permute-start.2 = (bf16[560,128]{1,0:T(8,128)(2,1)S(1)}, bf16[560,128]{1,0:T(8,128)(2,1)S(1)}, u32[]{:S(2)}, u32[]{:S(2)}) collective-permute-start(bf16[560,128]{1,0:T(8,128)(2,1)S(1)} %get-tuple-element.30), channel_id=1, source_target_pairs={{0,4},{2,6},{4,0},{6,2},{8,12},{10,14},{12,8},{14,10},{16,20},{18,... | collective-permute-start | bytes 430088 | tf_op jit(solution)/shard_map/ppermute | solution.py:481
  8.4 8.5 %collective-permute-start.3 = (bf16[560,128]{1,0:T(8,128)(2,1)S(1)}, bf16[560,128]{1,0:T(8,128)(2,1)S(1)}, u32[]{:S(2)}, u32[]{:S(2)}) collective-permute-start(bf16[560,128]{1,0:T(8,128)(2,1)S(1)} %get-tuple-element.31.refs_1_), channel_id=1, source_target_pairs={{0,6},{2,0},{4,2},{6,4},{8,14},{10,8},{12,10},{14,12},{16,22},{18,... | collective-permute-start | bytes 430088 | tf_op jit(solution)/shard_map/ppermute | solution.py:481
  10.5 1.5 %collective-permute-start.4 = (bf16[16,128]{1,0:T(8,128)(2,1)S(1)}, bf16[16,128]{1,0:T(8,128)(2,1)S(1)}, u32[]{:S(2)}, u32[]{:S(2)}) collective-permute-start(bf16[16,128]{1,0:T(8,128)(2,1)S(1)} %shard_map.76.refs_4_), channel_id=1, source_target_pairs={{0,1},{1,0},{2,3},{3,2},{4,5},{5,4},{6,7},{7,6},{8,9},{9,8},{10,11... | collective-permute-start | bytes 12296 | tf_op jit(solution)/shard_map/ppermute | solution.py:535
  19.5 9.5 %collective-permute-start.7 = (bf16[128,512]{1,0:T(8,128)(2,1)S(1)}, bf16[128,512]{1,0:T(8,128)(2,1)S(1)}, u32[]{:S(2)}, u32[]{:S(2)}) collective-permute-start(bf16[128,512]{1,0:T(8,128)(2,1)S(1)} %get-tuple-element.43), channel_id=1, source_target_pairs={{0,8},{2,10},{4,12},{6,14},{8,16},{10,18},{12,20},{14,22},{16,24},... | collective-permute-start | bytes 393224 | tf_op jit(solution)/shard_map/ppermute | solution.py:481
  21.0 7.9 %collective-permute-start.8 = (bf16[128,512]{1,0:T(8,128)(2,1)S(1)}, bf16[128,512]{1,0:T(8,128)(2,1)S(1)}, u32[]{:S(2)}, u32[]{:S(2)}) collective-permute-start(bf16[128,512]{1,0:T(8,128)(2,1)S(1)} %get-tuple-element.44), channel_id=1, source_target_pairs={{0,12},{2,14},{4,8},{6,10},{8,20},{10,22},{12,16},{14,18},{16,28},... | collective-permute-start | bytes 393224 | tf_op jit(solution)/shard_map/ppermute | solution.py:481
  24.3 11.5 %collective-permute-start.5 = (bf16[128,512]{1,0:T(8,128)(2,1)S(1)}, bf16[128,512]{1,0:T(8,128)(2,1)S(1)}, u32[]{:S(2)}, u32[]{:S(2)}) collective-permute-start(bf16[128,512]{1,0:T(8,128)(2,1)S(1)} %get-tuple-element.41), channel_id=1, source_target_pairs={{0,10},{2,12},{4,14},{6,8},{8,18},{10,20},{12,22},{14,16},{16,26},... | collective-permute-start | bytes 393224 | tf_op jit(solution)/shard_map/ppermute | solution.py:481
  27.8 8.6 %collective-permute-start.6 = (bf16[128,512]{1,0:T(8,128)(2,1)S(1)}, bf16[128,512]{1,0:T(8,128)(2,1)S(1)}, u32[]{:S(2)}, u32[]{:S(2)}) collective-permute-start(bf16[128,512]{1,0:T(8,128)(2,1)S(1)} %get-tuple-element.42), channel_id=1, source_target_pairs={{0,14},{2,8},{4,10},{6,12},{8,22},{10,16},{12,18},{14,20},{16,30},... | collective-permute-start | bytes 393224 | tf_op jit(solution)/shard_map/ppermute | solution.py:481

commit v7 on v6

--- a/solution.py
+++ b/solution.py
@@ -239,8 +239,8 @@
                 top = tile * rows + odd * part
                 outs[step][top : top + part, :] = acts.astype(jnp.bfloat16)
                 totals[odd] = totals[odd] + acts * acts
-    column = jnp.sum(jnp.concatenate(totals, axis=0), axis=1, keepdims=True)
-    row = jnp.transpose(jnp.broadcast_to(column, (rows, LANES)))[:EXTRA, :]
+    row = jnp.sum(jnp.transpose(jnp.concatenate(totals, axis=0)), axis=0, keepdims=True)
+    row = jnp.broadcast_to(row, (EXTRA, rows))
     nth = lax.broadcasted_iota(jnp.int32, (EXTRA, rows), 0)
     terms = three_terms(row)
     sums = jnp.where(nth == 0, terms[0], jnp.where(nth == 1, terms[1], jnp.where(nth == 2, terms[2], 0.0)))
@@ -418,12 +418,11 @@
     for odd in range(2):
         table = return_ref[odd * half : (odd + 1) * half, :]
         conv[odd] = jnp.dot(table, weighted[odd], preferred_element_type=jnp.float32)
-    for step in range(peers):
-        source = (peers - step) % peers
-        here = tokens[source]
-        for tile in range(width // LANES):
-            lanes = slice(tile * LANES, (tile + 1) * LANES)
-            for odd in range(2):
+        for step in range(peers):
+            source = (peers - step) % peers
+            here = tokens[source]
+            for tile in range(width // LANES):
+                lanes = slice(tile * LANES, (tile + 1) * LANES)
                 own = tile * rows + odd * part
                 acts = blocks[source][own : own + part, :].astype(jnp.float32)
                 gated = conv[odd, here, lanes] + skip[:, lanes] * product[odd, here, lanes].astype(jnp.float32)

time: 37.4 us -> 37.4 us (level)
  no operation moved by 1% of the time
where the time goes in v7:
time: 37.4 us; the launch traced here: 37.2 us
  starting transfers between devices  16.5 us (44%)
  waiting for transfers between devices  12.6 us (34%)
  Pallas kernels  8.02 us (21%)
    ppermute x7, starting transfers between devices, hop(): return lax.ppermute(x, ('section', 'ctx'), route)  16.5 us
    ppermute x7, waiting for transfers between devices, hop(): return lax.ppermute(x, ('section', 'ctx'), route)  11.4 us
    pallas_call x8, Pallas kernels, on_device(): pl.pallas_call(kernel, out_shape=outs, in_specs=[far if i in in_hbm else...  8.02 us
    ppermute x1, waiting for transfers between devices, channel_local(): other_sums = lax.ppermute(own_sums, 'tp', [(0, 1), (1, 0)])  1.16 us
  transfers between devices with their start and end apart: 9, of which 6 were waited for; matrix products, arithmetic and copies ran while one was open for 0% of the time, Pallas kernels for 8%

profile of v7, /device:TPU:0, one launch (start us, length us, event | category | flops | bytes accessed | tf_op | source)
XLA Modules:
  0.0 37.2 jit_solution(8464384981967139028)
XLA Ops:
  0.0 1.5 %shard_map.73 = (bf16[560,128]{1,0:T(8,128)(2,1)S(1)}, bf16[560,128]{1,0:T(8,128)(2,1)S(1)}, bf16[560,128]{1,0:T(8,128)(2,1)S(1)}, bf16[560,128]{1,0:T(8,128)(2,1)S(1)}, bf16[16,128]{1,0:T(8,128)(2,1)S(1)}) custom-call(f32[128,2048]{1,0:T(8,128)} %bitcast.4, bf16[128,128]{1,0:T(8,128)(2,1)} %bitcast.6), custom_call_target="tpu_custom_call" | custom-call | bytes 1658880 | tf_op jit(solution)/shard_map/pallas_call | solution.py:462
  1.5 3.1 %collective-permute-start = (bf16[560,128]{1,0:T(8,128)(2,1)S(1)}, bf16[560,128]{1,0:T(8,128)(2,1)S(1)}, u32[]{:S(2)}, u32[]{:S(2)}) collective-permute-start(bf16[560,128]{1,0:T(8,128)(2,1)S(1)} %get-tuple-element.26), channel_id=1, source_target_pairs={{0,2},{2,4},{4,6},{6,0},{8,10},{10,12},{12,14},{14,8},{16,18},{18,... | collective-permute-start | bytes 430088 | tf_op jit(solution)/shard_map/ppermute | solution.py:480
  4.6 0.0 collective-permute-start.1
  4.6 1.2 %collective-permute-done.1.refs_3_.after = bf16[16,128]{1,0:T(8,128)(2,1)S(1)} collective-permute-done((bf16[16,128]{1,0:T(8,128)(2,1)S(1)}, bf16[16,128]{1,0:T(8,128)(2,1)S(1)}, u32[]{:S(2)}, u32[]{:S(2)}) %collective-permute-start.1) | collective-permute-done | bytes 4128 | tf_op jit(solution)/shard_map/ppermute | solution.py:511
  5.8 2.6 %collective-permute-start.2 = (bf16[560,128]{1,0:T(8,128)(2,1)S(1)}, bf16[560,128]{1,0:T(8,128)(2,1)S(1)}, u32[]{:S(2)}, u32[]{:S(2)}) collective-permute-start(bf16[560,128]{1,0:T(8,128)(2,1)S(1)} %get-tuple-element.30), channel_id=1, source_target_pairs={{0,4},{2,6},{4,0},{6,2},{8,12},{10,14},{12,8},{14,10},{16,20},{18,... | collective-permute-start | bytes 430088 | tf_op jit(solution)/shard_map/ppermute | solution.py:480
  8.4 1.3 %collective-permute-start.3 = (bf16[560,128]{1,0:T(8,128)(2,1)S(1)}, bf16[560,128]{1,0:T(8,128)(2,1)S(1)}, u32[]{:S(2)}, u32[]{:S(2)}) collective-permute-start(bf16[560,128]{1,0:T(8,128)(2,1)S(1)} %get-tuple-element.31.refs_1_), channel_id=1, source_target_pairs={{0,6},{2,0},{4,2},{6,4},{8,14},{10,8},{12,10},{14,12},{16,22},{18,... | collective-permute-start | bytes 430088 | tf_op jit(solution)/shard_map/ppermute | solution.py:480
  9.7 0.8 %collective-permute-done.refs_0_.refs_1_ = bf16[560,128]{1,0:T(8,128)(2,1)S(1)} collective-permute-done((bf16[560,128]{1,0:T(8,128)(2,1)S(1)}, bf16[560,128]{1,0:T(8,128)(2,1)S(1)}, u32[]{:S(2)}, u32[]{:S(2)}) %collective-permute-start) | collective-permute-done | bytes 143392 | tf_op jit(solution)/shard_map/ppermute | solution.py:480
  10.5 0.0 collective-permute-start.4
  10.5 1.5 %shard_map.75 = (bf16[1024,256]{1,0:T(8,128)(2,1)S(1)}, bf16[512,512]{1,0:T(8,128)(2,1)S(1)}, bf16[32,512]{1,0:T(8,128)(2,1)S(1)}, bf16[3,3,2048]{2,1,0:T(4,128)(2,1)S(1)}, f32[1,2048]{1,0:T(1,128)S(1)}) custom-call(bf16[16,128]{1,0:T(8,128)(2,1)S(1)} %collective-permute-done.1.refs_3_.after, bf16[1024,256]{1,0:T(8,128)(2,1)} %constant.6.clone.refs_0_, ...), custom_call_target="tpu_custom_call" | custom-call | bytes 2256896 | tf_op jit(solution)/shard_map/pallas_call | solution.py:462
  12.0 0.0 collective-permute-done.4.refs_5_
  12.0 0.8 %shard_map.77 = (f32[2,2,72,512]{3,2,1,0:T(8,128)S(1)}, bf16[2,256,512]{2,1,0:T(8,128)(2,1)S(1)}, bf16[2,256,512]{2,1,0:T(8,128)(2,1)S(1)}, bf16[2,256,512]{2,1,0:T(8,128)(2,1)S(1)}) custom-call(bf16[560,128]{1,0:T(8,128)(2,1)S(1)} %get-tuple-element.25.refs_0_, bf16[560,128]{1,0:T(8,128)(2,1)S(1)} %collective-permute-done.refs_0_.refs_1_, ...), custom_call_target="tpu_custom_call" | custom-call | bytes 2535424 | tf_op jit(solution)/shard_map/pallas_call | solution.py:462
  12.8 3.9 %collective-permute-done.2.refs_2_ = bf16[560,128]{1,0:T(8,128)(2,1)S(1)} collective-permute-done((bf16[560,128]{1,0:T(8,128)(2,1)S(1)}, bf16[560,128]{1,0:T(8,128)(2,1)S(1)}, u32[]{:S(2)}, u32[]{:S(2)}) %collective-permute-start.2) | collective-permute-done | bytes 143392 | tf_op jit(solution)/shard_map/ppermute | solution.py:480
  16.7 0.2 collective-permute-done.3.refs_3_
  16.9 2.5 %shard_map.78 = (bf16[128,512]{1,0:T(8,128)(2,1)S(1)}, bf16[128,512]{1,0:T(8,128)(2,1)S(1)}, bf16[128,512]{1,0:T(8,128)(2,1)S(1)}, bf16[128,512]{1,0:T(8,128)(2,...) custom-call(bf16[560,128]{1,0:T(8,128)(2,1)S(1)} %get-tuple-element., ...), custom_call_target="tpu_custom_call", output_to_operand_aliasing={{4}: (10, {}), {5}: (11, {}), {6}: (12, {})} | custom-call | flops 805306368 | bytes 5959680 | tf_op jit(solution)/shard_map/pallas_call | solution.py:462
  19.4 1.5 %collective-permute-start.7 = (bf16[128,512]{1,0:T(8,128)(2,1)S(1)}, bf16[128,512]{1,0:T(8,128)(2,1)S(1)}, u32[]{:S(2)}, u32[]{:S(2)}) collective-permute-start(bf16[128,512]{1,0:T(8,128)(2,1)S(1)} %get-tuple-element.43), channel_id=1, source_target_pairs={{0,8},{2,10},{4,12},{6,14},{8,16},{10,18},{12,20},{14,22},{16,24},... | collective-permute-start | bytes 393224 | tf_op jit(solution)/shard_map/ppermute | solution.py:480
  21.0 3.2 %collective-permute-start.8 = (bf16[128,512]{1,0:T(8,128)(2,1)S(1)}, bf16[128,512]{1,0:T(8,128)(2,1)S(1)}, u32[]{:S(2)}, u32[]{:S(2)}) collective-permute-start(bf16[128,512]{1,0:T(8,128)(2,1)S(1)} %get-tuple-element.44), channel_id=1, source_target_pairs={{0,12},{2,14},{4,8},{6,10},{8,20},{10,22},{12,16},{14,18},{16,28},... | collective-permute-start | bytes 393224 | tf_op jit(solution)/shard_map/ppermute | solution.py:480
  24.2 3.5 %collective-permute-start.5 = (bf16[128,512]{1,0:T(8,128)(2,1)S(1)}, bf16[128,512]{1,0:T(8,128)(2,1)S(1)}, u32[]{:S(2)}, u32[]{:S(2)}) collective-permute-start(bf16[128,512]{1,0:T(8,128)(2,1)S(1)} %get-tuple-element.41), channel_id=1, source_target_pairs={{0,10},{2,12},{4,14},{6,8},{8,18},{10,20},{12,22},{14,16},{16,26},... | collective-permute-start | bytes 393224 | tf_op jit(solution)/shard_map/ppermute | solution.py:480
  27.7 1.2 %collective-permute-start.6 = (bf16[128,512]{1,0:T(8,128)(2,1)S(1)}, bf16[128,512]{1,0:T(8,128)(2,1)S(1)}, u32[]{:S(2)}, u32[]{:S(2)}) collective-permute-start(bf16[128,512]{1,0:T(8,128)(2,1)S(1)} %get-tuple-element.42), channel_id=1, source_target_pairs={{0,14},{2,8},{4,10},{6,12},{8,22},{10,16},{12,18},{14,20},{16,30},... | collective-permute-start | bytes 393224 | tf_op jit(solution)/shard_map/ppermute | solution.py:480
  28.9 0.0 collective-permute-done.7.refs_0_
  28.9 0.0 collective-permute-done.8.refs_1_
  28.9 0.9 %shard_map.79.refs_2_ = f32[128,2048]{1,0:T(8,128)} custom-call(bf16[128,512]{1,0:T(8,128)(2,1)S(1)} %collective-permute-done.7.refs_0_, bf16[128,512]{1,0:T(8,128)(2,1)S(1)} %collective-permute-done.8.refs_1_), custom_call_target="tpu_custom_call" | custom-call | bytes 1310720 | tf_op jit(solution)/shard_map/pallas_call | solution.py:462
  29.8 5.9 %collective-permute-done.5.refs_0_ = bf16[128,512]{1,0:T(8,128)(2,1)S(1)} collective-permute-done((bf16[128,512]{1,0:T(8,128)(2,1)S(1)}, bf16[128,512]{1,0:T(8,128)(2,1)S(1)}, u32[]{:S(2)}, u32[]{:S(2)}) %collective-permute-start.5) | collective-permute-done | bytes 131104 | tf_op jit(solution)/shard_map/ppermute | solution.py:480
  35.7 0.6 %collective-permute-done.6.refs_1_ = bf16[128,512]{1,0:T(8,128)(2,1)S(1)} collective-permute-done((bf16[128,512]{1,0:T(8,128)(2,1)S(1)}, bf16[128,512]{1,0:T(8,128)(2,1)S(1)}, u32[]{:S(2)}, u32[]{:S(2)}) %collective-permute-start.6) | collective-permute-done | bytes 131104 | tf_op jit(solution)/shard_map/ppermute | solution.py:480
  36.3 0.9 %shard_map.80 = f32[128,2048]{1,0:T(8,128)} custom-call(bf16[128,512]{1,0:T(8,128)(2,1)S(1)} %collective-permute-done.5.refs_0_, bf16[128,512]{1,0:T(8,128)(2,1)S(1)} %collective-permute-done.6.refs_1_, f32[128,2048]{1,0:T(8,128)} %shard_map.79.refs_2_), custom_call_target="tpu_custom_call", output_to_operand_aliasing={{}: (2, {})} | custom-call | bytes 2359296 | tf_op jit(solution)/shard_map/pallas_call | solution.py:462
  (2 shorter events, 0.0 us)
Async XLA Ops:
  1.5 9.0 %collective-permute-start = (bf16[560,128]{1,0:T(8,128)(2,1)S(1)}, bf16[560,128]{1,0:T(8,128)(2,1)S(1)}, u32[]{:S(2)}, u32[]{:S(2)}) collective-permute-start(bf16[560,128]{1,0:T(8,128)(2,1)S(1)} %get-tuple-element.26), channel_id=1, source_target_pairs={{0,2},{2,4},{4,6},{6,0},{8,10},{10,12},{12,14},{14,8},{16,18},{18,... | collective-permute-start | bytes 430088 | tf_op jit(solution)/shard_map/ppermute | solution.py:480
  4.6 1.2 %collective-permute-start.1 = (bf16[16,128]{1,0:T(8,128)(2,1)S(1)}, bf16[16,128]{1,0:T(8,128)(2,1)S(1)}, u32[]{:S(2)}, u32[]{:S(2)}) collective-permute-start(bf16[16,128]{1,0:T(8,128)(2,1)S(1)} %get-tuple-element.29.refs_2_), channel_id=1, source_target_pairs={{0,1},{1,0},{2,3},{3,2},{4,5},{5,4},{6,7},{7,6},{8,9},{9,8},{10,11... | collective-permute-start | bytes 12296 | tf_op jit(solution)/shard_map/ppermute | solution.py:511
  5.8 10.9 %collective-permute-start.2 = (bf16[560,128]{1,0:T(8,128)(2,1)S(1)}, bf16[560,128]{1,0:T(8,128)(2,1)S(1)}, u32[]{:S(2)}, u32[]{:S(2)}) collective-permute-start(bf16[560,128]{1,0:T(8,128)(2,1)S(1)} %get-tuple-element.30), channel_id=1, source_target_pairs={{0,4},{2,6},{4,0},{6,2},{8,12},{10,14},{12,8},{14,10},{16,20},{18,... | collective-permute-start | bytes 430088 | tf_op jit(solution)/shard_map/ppermute | solution.py:480
  8.4 8.5 %collective-permute-start.3 = (bf16[560,128]{1,0:T(8,128)(2,1)S(1)}, bf16[560,128]{1,0:T(8,128)(2,1)S(1)}, u32[]{:S(2)}, u32[]{:S(2)}) collective-permute-start(bf16[560,128]{1,0:T(8,128)(2,1)S(1)} %get-tuple-element.31.refs_1_), channel_id=1, source_target_pairs={{0,6},{2,0},{4,2},{6,4},{8,14},{10,8},{12,10},{14,12},{16,22},{18,... | collective-permute-start | bytes 430088 | tf_op jit(solution)/shard_map/ppermute | solution.py:480
  10.5 1.5 %collective-permute-start.4 = (bf16[16,128]{1,0:T(8,128)(2,1)S(1)}, bf16[16,128]{1,0:T(8,128)(2,1)S(1)}, u32[]{:S(2)}, u32[]{:S(2)}) collective-permute-start(bf16[16,128]{1,0:T(8,128)(2,1)S(1)} %shard_map.76.refs_4_), channel_id=1, source_target_pairs={{0,1},{1,0},{2,3},{3,2},{4,5},{5,4},{6,7},{7,6},{8,9},{9,8},{10,11... | collective-permute-start | bytes 12296 | tf_op jit(solution)/shard_map/ppermute | solution.py:534
  19.4 9.5 %collective-permute-start.7 = (bf16[128,512]{1,0:T(8,128)(2,1)S(1)}, bf16[128,512]{1,0:T(8,128)(2,1)S(1)}, u32[]{:S(2)}, u32[]{:S(2)}) collective-permute-start(bf16[128,512]{1,0:T(8,128)(2,1)S(1)} %get-tuple-element.43), channel_id=1, source_target_pairs={{0,8},{2,10},{4,12},{6,14},{8,16},{10,18},{12,20},{14,22},{16,24},... | collective-permute-start | bytes 393224 | tf_op jit(solution)/shard_map/ppermute | solution.py:480
  21.0 7.9 %collective-permute-start.8 = (bf16[128,512]{1,0:T(8,128)(2,1)S(1)}, bf16[128,512]{1,0:T(8,128)(2,1)S(1)}, u32[]{:S(2)}, u32[]{:S(2)}) collective-permute-start(bf16[128,512]{1,0:T(8,128)(2,1)S(1)} %get-tuple-element.44), channel_id=1, source_target_pairs={{0,12},{2,14},{4,8},{6,10},{8,20},{10,22},{12,16},{14,18},{16,28},... | collective-permute-start | bytes 393224 | tf_op jit(solution)/shard_map/ppermute | solution.py:480
  24.2 11.5 %collective-permute-start.5 = (bf16[128,512]{1,0:T(8,128)(2,1)S(1)}, bf16[128,512]{1,0:T(8,128)(2,1)S(1)}, u32[]{:S(2)}, u32[]{:S(2)}) collective-permute-start(bf16[128,512]{1,0:T(8,128)(2,1)S(1)} %get-tuple-element.41), channel_id=1, source_target_pairs={{0,10},{2,12},{4,14},{6,8},{8,18},{10,20},{12,22},{14,16},{16,26},... | collective-permute-start | bytes 393224 | tf_op jit(solution)/shard_map/ppermute | solution.py:480
  27.7 8.6 %collective-permute-start.6 = (bf16[128,512]{1,0:T(8,128)(2,1)S(1)}, bf16[128,512]{1,0:T(8,128)(2,1)S(1)}, u32[]{:S(2)}, u32[]{:S(2)}) collective-permute-start(bf16[128,512]{1,0:T(8,128)(2,1)S(1)} %get-tuple-element.42), channel_id=1, source_target_pairs={{0,14},{2,8},{4,10},{6,12},{8,22},{10,16},{12,18},{14,20},{16,30},... | collective-permute-start | bytes 393224 | tf_op jit(solution)/shard_map/ppermute | solution.py:480

commit v8 on v6

--- a/solution.py
+++ b/solution.py
@@ -217,8 +217,8 @@
             lanes = pl.ds(pl.multiple_of(begin + tile * LANES, LANES), LANES)
             at = step * tiles + tile
             copies.append(pltpu.make_async_copy(x_hbm.at[:, lanes], x_ref.at[at], sems.at[at]))
-    for copy in copies:
-        copy.start()
+    for i, copy in enumerate(copies):
+        copy.start(priority=i % 2)
     copies[0].wait()
     for at in range(plain.shape[0]):
         lanes = slice(at * LANES, (at + 1) * LANES)
@@ -450,7 +450,7 @@
                 wide[at, pl.ds(odd, rows // 2, stride=2), :] = part.astype(jnp.float32)
             lanes = pl.ds(pl.multiple_of(begin + tile * LANES, LANES), LANES)
             copies.append(pltpu.make_async_copy(wide.at[at], out_hbm.at[:, lanes], sems.at[at]))
-            copies[-1].start()
+            copies[-1].start(priority=at % 2)
     for copy in copies:
         copy.wait()
 

time: 37.4 us -> 37.5 us (level)
  no operation moved by 1% of the time
where the time goes in v8:
time: 37.5 us; the launch traced here: 37.3 us
  starting transfers between devices  16.5 us (44%)
  waiting for transfers between devices  12.6 us (34%)
  Pallas kernels  8.14 us (22%)
    ppermute x7, starting transfers between devices, hop(): return lax.ppermute(x, ('section', 'ctx'), route)  16.5 us
    ppermute x7, waiting for transfers between devices, hop(): return lax.ppermute(x, ('section', 'ctx'), route)  11.4 us
    pallas_call x8, Pallas kernels, on_device(): pl.pallas_call(kernel, out_shape=outs, in_specs=[far if i in in_hbm else...  8.14 us
    ppermute x1, waiting for transfers between devices, channel_local(): other_sums = lax.ppermute(own_sums, 'tp', [(0, 1), (1, 0)])  1.16 us
  transfers between devices with their start and end apart: 9, of which 6 were waited for; matrix products, arithmetic and copies ran while one was open for 0% of the time, Pallas kernels for 8%

profile of v8, /device:TPU:0, one launch (start us, length us, event | category | flops | bytes accessed | tf_op | source)
XLA Modules:
  0.0 37.3 jit_solution(10039423353125958994)
XLA Ops:
  0.0 1.7 %shard_map.73 = (bf16[560,128]{1,0:T(8,128)(2,1)S(1)}, bf16[560,128]{1,0:T(8,128)(2,1)S(1)}, bf16[560,128]{1,0:T(8,128)(2,1)S(1)}, bf16[560,128]{1,0:T(8,128)(2,1)S(1)}, bf16[16,128]{1,0:T(8,128)(2,1)S(1)}) custom-call(f32[128,2048]{1,0:T(8,128)} %bitcast.4, bf16[128,128]{1,0:T(8,128)(2,1)} %bitcast.6), custom_call_target="tpu_custom_call" | custom-call | bytes 1658880 | tf_op jit(solution)/shard_map/pallas_call | solution.py:463
  1.7 3.1 %collective-permute-start = (bf16[560,128]{1,0:T(8,128)(2,1)S(1)}, bf16[560,128]{1,0:T(8,128)(2,1)S(1)}, u32[]{:S(2)}, u32[]{:S(2)}) collective-permute-start(bf16[560,128]{1,0:T(8,128)(2,1)S(1)} %get-tuple-element.26), channel_id=1, source_target_pairs={{0,2},{2,4},{4,6},{6,0},{8,10},{10,12},{12,14},{14,8},{16,18},{18,... | collective-permute-start | bytes 430088 | tf_op jit(solution)/shard_map/ppermute | solution.py:481
  4.7 0.0 collective-permute-start.1
  4.7 1.2 %collective-permute-done.1.refs_3_.after = bf16[16,128]{1,0:T(8,128)(2,1)S(1)} collective-permute-done((bf16[16,128]{1,0:T(8,128)(2,1)S(1)}, bf16[16,128]{1,0:T(8,128)(2,1)S(1)}, u32[]{:S(2)}, u32[]{:S(2)}) %collective-permute-start.1) | collective-permute-done | bytes 4128 | tf_op jit(solution)/shard_map/ppermute | solution.py:512
  5.9 2.6 %collective-permute-start.2 = (bf16[560,128]{1,0:T(8,128)(2,1)S(1)}, bf16[560,128]{1,0:T(8,128)(2,1)S(1)}, u32[]{:S(2)}, u32[]{:S(2)}) collective-permute-start(bf16[560,128]{1,0:T(8,128)(2,1)S(1)} %get-tuple-element.30), channel_id=1, source_target_pairs={{0,4},{2,6},{4,0},{6,2},{8,12},{10,14},{12,8},{14,10},{16,20},{18,... | collective-permute-start | bytes 430088 | tf_op jit(solution)/shard_map/ppermute | solution.py:481
  8.5 1.3 %collective-permute-start.3 = (bf16[560,128]{1,0:T(8,128)(2,1)S(1)}, bf16[560,128]{1,0:T(8,128)(2,1)S(1)}, u32[]{:S(2)}, u32[]{:S(2)}) collective-permute-start(bf16[560,128]{1,0:T(8,128)(2,1)S(1)} %get-tuple-element.31.refs_1_), channel_id=1, source_target_pairs={{0,6},{2,0},{4,2},{6,4},{8,14},{10,8},{12,10},{14,12},{16,22},{18,... | collective-permute-start | bytes 430088 | tf_op jit(solution)/shard_map/ppermute | solution.py:481
  9.9 0.8 %collective-permute-done.refs_0_.refs_1_ = bf16[560,128]{1,0:T(8,128)(2,1)S(1)} collective-permute-done((bf16[560,128]{1,0:T(8,128)(2,1)S(1)}, bf16[560,128]{1,0:T(8,128)(2,1)S(1)}, u32[]{:S(2)}, u32[]{:S(2)}) %collective-permute-start) | collective-permute-done | bytes 143392 | tf_op jit(solution)/shard_map/ppermute | solution.py:481
  10.6 0.0 collective-permute-start.4
  10.6 1.5 %shard_map.75 = (bf16[1024,256]{1,0:T(8,128)(2,1)S(1)}, bf16[512,512]{1,0:T(8,128)(2,1)S(1)}, bf16[32,512]{1,0:T(8,128)(2,1)S(1)}, bf16[3,3,2048]{2,1,0:T(4,128)(2,1)S(1)}, f32[1,2048]{1,0:T(1,128)S(1)}) custom-call(bf16[16,128]{1,0:T(8,128)(2,1)S(1)} %collective-permute-done.1.refs_3_.after, bf16[1024,256]{1,0:T(8,128)(2,1)} %constant.6.clone.refs_0_, ...), custom_call_target="tpu_custom_call" | custom-call | bytes 2256896 | tf_op jit(solution)/shard_map/pallas_call | solution.py:463
  12.1 0.0 collective-permute-done.4.refs_5_
  12.1 0.8 %shard_map.77 = (f32[2,2,72,512]{3,2,1,0:T(8,128)S(1)}, bf16[2,256,512]{2,1,0:T(8,128)(2,1)S(1)}, bf16[2,256,512]{2,1,0:T(8,128)(2,1)S(1)}, bf16[2,256,512]{2,1,0:T(8,128)(2,1)S(1)}) custom-call(bf16[560,128]{1,0:T(8,128)(2,1)S(1)} %get-tuple-element.25.refs_0_, bf16[560,128]{1,0:T(8,128)(2,1)S(1)} %collective-permute-done.refs_0_.refs_1_, ...), custom_call_target="tpu_custom_call" | custom-call | bytes 2535424 | tf_op jit(solution)/shard_map/pallas_call | solution.py:463
  12.9 3.9 %collective-permute-done.2.refs_2_ = bf16[560,128]{1,0:T(8,128)(2,1)S(1)} collective-permute-done((bf16[560,128]{1,0:T(8,128)(2,1)S(1)}, bf16[560,128]{1,0:T(8,128)(2,1)S(1)}, u32[]{:S(2)}, u32[]{:S(2)}) %collective-permute-start.2) | collective-permute-done | bytes 143392 | tf_op jit(solution)/shard_map/ppermute | solution.py:481
  16.8 0.2 collective-permute-done.3.refs_3_
  17.0 2.5 %shard_map.78 = (bf16[128,512]{1,0:T(8,128)(2,1)S(1)}, bf16[128,512]{1,0:T(8,128)(2,1)S(1)}, bf16[128,512]{1,0:T(8,128)(2,1)S(1)}, bf16[128,512]{1,0:T(8,128)(2,...) custom-call(bf16[560,128]{1,0:T(8,128)(2,1)S(1)} %get-tuple-element., ...), custom_call_target="tpu_custom_call", output_to_operand_aliasing={{4}: (10, {}), {5}: (11, {}), {6}: (12, {})} | custom-call | flops 805306368 | bytes 5959680 | tf_op jit(solution)/shard_map/pallas_call | solution.py:463
  19.5 1.5 %collective-permute-start.7 = (bf16[128,512]{1,0:T(8,128)(2,1)S(1)}, bf16[128,512]{1,0:T(8,128)(2,1)S(1)}, u32[]{:S(2)}, u32[]{:S(2)}) collective-permute-start(bf16[128,512]{1,0:T(8,128)(2,1)S(1)} %get-tuple-element.43), channel_id=1, source_target_pairs={{0,8},{2,10},{4,12},{6,14},{8,16},{10,18},{12,20},{14,22},{16,24},... | collective-permute-start | bytes 393224 | tf_op jit(solution)/shard_map/ppermute | solution.py:481
  21.1 3.3 %collective-permute-start.8 = (bf16[128,512]{1,0:T(8,128)(2,1)S(1)}, bf16[128,512]{1,0:T(8,128)(2,1)S(1)}, u32[]{:S(2)}, u32[]{:S(2)}) collective-permute-start(bf16[128,512]{1,0:T(8,128)(2,1)S(1)} %get-tuple-element.44), channel_id=1, source_target_pairs={{0,12},{2,14},{4,8},{6,10},{8,20},{10,22},{12,16},{14,18},{16,28},... | collective-permute-start | bytes 393224 | tf_op jit(solution)/shard_map/ppermute | solution.py:481
  24.3 3.5 %collective-permute-start.5 = (bf16[128,512]{1,0:T(8,128)(2,1)S(1)}, bf16[128,512]{1,0:T(8,128)(2,1)S(1)}, u32[]{:S(2)}, u32[]{:S(2)}) collective-permute-start(bf16[128,512]{1,0:T(8,128)(2,1)S(1)} %get-tuple-element.41), channel_id=1, source_target_pairs={{0,10},{2,12},{4,14},{6,8},{8,18},{10,20},{12,22},{14,16},{16,26},... | collective-permute-start | bytes 393224 | tf_op jit(solution)/shard_map/ppermute | solution.py:481
  27.8 1.2 %collective-permute-start.6 = (bf16[128,512]{1,0:T(8,128)(2,1)S(1)}, bf16[128,512]{1,0:T(8,128)(2,1)S(1)}, u32[]{:S(2)}, u32[]{:S(2)}) collective-permute-start(bf16[128,512]{1,0:T(8,128)(2,1)S(1)} %get-tuple-element.42), channel_id=1, source_target_pairs={{0,14},{2,8},{4,10},{6,12},{8,22},{10,16},{12,18},{14,20},{16,30},... | collective-permute-start | bytes 393224 | tf_op jit(solution)/shard_map/ppermute | solution.py:481
  29.0 0.0 collective-permute-done.7.refs_0_
  29.0 0.0 collective-permute-done.8.refs_1_
  29.0 0.9 %shard_map.79.refs_2_ = f32[128,2048]{1,0:T(8,128)} custom-call(bf16[128,512]{1,0:T(8,128)(2,1)S(1)} %collective-permute-done.7.refs_0_, bf16[128,512]{1,0:T(8,128)(2,1)S(1)} %collective-permute-done.8.refs_1_), custom_call_target="tpu_custom_call" | custom-call | bytes 1310720 | tf_op jit(solution)/shard_map/pallas_call | solution.py:463
  29.9 5.9 %collective-permute-done.5.refs_0_ = bf16[128,512]{1,0:T(8,128)(2,1)S(1)} collective-permute-done((bf16[128,512]{1,0:T(8,128)(2,1)S(1)}, bf16[128,512]{1,0:T(8,128)(2,1)S(1)}, u32[]{:S(2)}, u32[]{:S(2)}) %collective-permute-start.5) | collective-permute-done | bytes 131104 | tf_op jit(solution)/shard_map/ppermute | solution.py:481
  35.8 0.6 %collective-permute-done.6.refs_1_ = bf16[128,512]{1,0:T(8,128)(2,1)S(1)} collective-permute-done((bf16[128,512]{1,0:T(8,128)(2,1)S(1)}, bf16[128,512]{1,0:T(8,128)(2,1)S(1)}, u32[]{:S(2)}, u32[]{:S(2)}) %collective-permute-start.6) | collective-permute-done | bytes 131104 | tf_op jit(solution)/shard_map/ppermute | solution.py:481
  36.4 0.9 %shard_map.80 = f32[128,2048]{1,0:T(8,128)} custom-call(bf16[128,512]{1,0:T(8,128)(2,1)S(1)} %collective-permute-done.5.refs_0_, bf16[128,512]{1,0:T(8,128)(2,1)S(1)} %collective-permute-done.6.refs_1_, f32[128,2048]{1,0:T(8,128)} %shard_map.79.refs_2_), custom_call_target="tpu_custom_call", output_to_operand_aliasing={{}: (2, {})} | custom-call | bytes 2359296 | tf_op jit(solution)/shard_map/pallas_call | solution.py:463
  (2 shorter events, 0.0 us)
Async XLA Ops:
  1.7 9.0 %collective-permute-start = (bf16[560,128]{1,0:T(8,128)(2,1)S(1)}, bf16[560,128]{1,0:T(8,128)(2,1)S(1)}, u32[]{:S(2)}, u32[]{:S(2)}) collective-permute-start(bf16[560,128]{1,0:T(8,128)(2,1)S(1)} %get-tuple-element.26), channel_id=1, source_target_pairs={{0,2},{2,4},{4,6},{6,0},{8,10},{10,12},{12,14},{14,8},{16,18},{18,... | collective-permute-start | bytes 430088 | tf_op jit(solution)/shard_map/ppermute | solution.py:481
  4.7 1.2 %collective-permute-start.1 = (bf16[16,128]{1,0:T(8,128)(2,1)S(1)}, bf16[16,128]{1,0:T(8,128)(2,1)S(1)}, u32[]{:S(2)}, u32[]{:S(2)}) collective-permute-start(bf16[16,128]{1,0:T(8,128)(2,1)S(1)} %get-tuple-element.29.refs_2_), channel_id=1, source_target_pairs={{0,1},{1,0},{2,3},{3,2},{4,5},{5,4},{6,7},{7,6},{8,9},{9,8},{10,11... | collective-permute-start | bytes 12296 | tf_op jit(solution)/shard_map/ppermute | solution.py:512
  5.9 10.9 %collective-permute-start.2 = (bf16[560,128]{1,0:T(8,128)(2,1)S(1)}, bf16[560,128]{1,0:T(8,128)(2,1)S(1)}, u32[]{:S(2)}, u32[]{:S(2)}) collective-permute-start(bf16[560,128]{1,0:T(8,128)(2,1)S(1)} %get-tuple-element.30), channel_id=1, source_target_pairs={{0,4},{2,6},{4,0},{6,2},{8,12},{10,14},{12,8},{14,10},{16,20},{18,... | collective-permute-start | bytes 430088 | tf_op jit(solution)/shard_map/ppermute | solution.py:481
  8.5 8.5 %collective-permute-start.3 = (bf16[560,128]{1,0:T(8,128)(2,1)S(1)}, bf16[560,128]{1,0:T(8,128)(2,1)S(1)}, u32[]{:S(2)}, u32[]{:S(2)}) collective-permute-start(bf16[560,128]{1,0:T(8,128)(2,1)S(1)} %get-tuple-element.31.refs_1_), channel_id=1, source_target_pairs={{0,6},{2,0},{4,2},{6,4},{8,14},{10,8},{12,10},{14,12},{16,22},{18,... | collective-permute-start | bytes 430088 | tf_op jit(solution)/shard_map/ppermute | solution.py:481
  10.6 1.5 %collective-permute-start.4 = (bf16[16,128]{1,0:T(8,128)(2,1)S(1)}, bf16[16,128]{1,0:T(8,128)(2,1)S(1)}, u32[]{:S(2)}, u32[]{:S(2)}) collective-permute-start(bf16[16,128]{1,0:T(8,128)(2,1)S(1)} %shard_map.76.refs_4_), channel_id=1, source_target_pairs={{0,1},{1,0},{2,3},{3,2},{4,5},{5,4},{6,7},{7,6},{8,9},{9,8},{10,11... | collective-permute-start | bytes 12296 | tf_op jit(solution)/shard_map/ppermute | solution.py:535
  19.5 9.5 %collective-permute-start.7 = (bf16[128,512]{1,0:T(8,128)(2,1)S(1)}, bf16[128,512]{1,0:T(8,128)(2,1)S(1)}, u32[]{:S(2)}, u32[]{:S(2)}) collective-permute-start(bf16[128,512]{1,0:T(8,128)(2,1)S(1)} %get-tuple-element.43), channel_id=1, source_target_pairs={{0,8},{2,10},{4,12},{6,14},{8,16},{10,18},{12,20},{14,22},{16,24},... | collective-permute-start | bytes 393224 | tf_op jit(solution)/shard_map/ppermute | solution.py:481
  21.1 7.9 %collective-permute-start.8 = (bf16[128,512]{1,0:T(8,128)(2,1)S(1)}, bf16[128,512]{1,0:T(8,128)(2,1)S(1)}, u32[]{:S(2)}, u32[]{:S(2)}) collective-permute-start(bf16[128,512]{1,0:T(8,128)(2,1)S(1)} %get-tuple-element.44), channel_id=1, source_target_pairs={{0,12},{2,14},{4,8},{6,10},{8,20},{10,22},{12,16},{14,18},{16,28},... | collective-permute-start | bytes 393224 | tf_op jit(solution)/shard_map/ppermute | solution.py:481
  24.3 11.5 %collective-permute-start.5 = (bf16[128,512]{1,0:T(8,128)(2,1)S(1)}, bf16[128,512]{1,0:T(8,128)(2,1)S(1)}, u32[]{:S(2)}, u32[]{:S(2)}) collective-permute-start(bf16[128,512]{1,0:T(8,128)(2,1)S(1)} %get-tuple-element.41), channel_id=1, source_target_pairs={{0,10},{2,12},{4,14},{6,8},{8,18},{10,20},{12,22},{14,16},{16,26},... | collective-permute-start | bytes 393224 | tf_op jit(solution)/shard_map/ppermute | solution.py:481
  27.8 8.6 %collective-permute-start.6 = (bf16[128,512]{1,0:T(8,128)(2,1)S(1)}, bf16[128,512]{1,0:T(8,128)(2,1)S(1)}, u32[]{:S(2)}, u32[]{:S(2)}) collective-permute-start(bf16[128,512]{1,0:T(8,128)(2,1)S(1)} %get-tuple-element.42), channel_id=1, source_target_pairs={{0,14},{2,8},{4,10},{6,12},{8,22},{10,16},{12,18},{14,20},{16,30},... | collective-permute-start | bytes 393224 | tf_op jit(solution)/shard_map/ppermute | solution.py:481
